TPU v7x, 32 devices: a whole 2x2x4 slice. The times are simulated.
32 devices in a mesh: expert: 8 (over z, y), tensor: 4 (over x, core).
Axes of the slice: x: 2, y: 2, z: 4, core: 2. Of those that a mesh axis runs over, the one named last changes fastest.
Arguments:
- tokens: bfloat16 [4096, 2048], P('expert'), may hold values from -15 to 15
- gain_attn: float32 [2048], replicated, may hold values from 0.5 to 1.5
- w_query: bfloat16 [2048, 2048], P(None, 'tensor'), may hold values from -0.125 to 0.125
- w_key: bfloat16 [2048, 2048], P(None, 'tensor'), may hold values from -0.125 to 0.125
- w_value: bfloat16 [2048, 2048], P(None, 'tensor'), may hold values from -0.125 to 0.125
- w_out: bfloat16 [2048, 2048], P('tensor'), may hold values from -2 to 2
- gain_moe: float32 [2048], replicated, may hold values from 0.5 to 1.5
- w_router: bfloat16 [2048, 64], replicated, may hold values from -0.0625 to 0.0625
- w_gate: bfloat16 [64, 2048, 1024], P('expert', None, 'tensor'), may hold values from -0.125 to 0.125
- w_up: bfloat16 [64, 2048, 1024], P('expert', None, 'tensor'), may hold values from -0.125 to 0.125
- w_down: bfloat16 [64, 1024, 2048], P('expert', 'tensor'), may hold values from -0.75 to 0.75
- expert_ids: int32 [4096, 8], P(('expert', 'tensor')), may hold values from 0 to 63, all different within a row; in each aligned block of 128 rows (0 to 127, 128 to 255, ...) at most 24 rows name the same one
- cotangent: bfloat16 [4096, 2048], P(('expert', 'tensor')), may hold values from -6 to 6
Outputs:
- mixed: bfloat16 [4096, 2048], P(('expert', 'tensor'))
- grad_tokens: float32 [4096, 2048], P(('expert', 'tensor'))
- grad_gain_attn: float32 [2048], replicated
- grad_w_query: float32 [2048, 2048], P(None, 'tensor')
- grad_w_key: float32 [2048, 2048], P(None, 'tensor')
- grad_w_value: float32 [2048, 2048], P(None, 'tensor')
- grad_w_out: float32 [2048, 2048], P('tensor')
- grad_gain_moe: float32 [2048], replicated
- grad_w_router: float32 [2048, 64], replicated
- grad_w_gate: float32 [64, 2048, 1024], P('expert', None, 'tensor')
- grad_w_up: float32 [64, 2048, 1024], P('expert', None, 'tensor')
- grad_w_down: float32 [64, 1024, 2048], P('expert', 'tensor')
Inputs may be any that keep to these rules, and one draw needn't show every extreme that they name: `expert_ids`: each row names 8 different experts; among the rows of one device (aligned blocks of 128 rows) no expert is named more than 24 times, and in some blocks one is named exactly 24 times.
All inputs are finite; a program needn't handle non-finite values.
Results may differ from a plain program's by a relative error of at most 0.018.
Values may be sent and summed in bfloat16 or wider, within the bound.
No kernel may reach another device: no remote copies, remote signals or barrier semaphores. Data moves between devices by JAX's collectives and lax.ppermute only.
A program may use at most 448 MiB of HBM per device.

v0:
```python
import functools

import jax
import jax.numpy as jnp
from jax import lax
from jax.experimental import pallas as pl
from jax.experimental.pallas import tpu as pltpu
from jax.sharding import PartitionSpec as P

HD = 128


eps = 1e-06
theta_base = 10000.0
masked = -1e30

BOTH = ("expert", "tensor")
CORE, ACROSS, ASIDE, PLANE_NEXT, PLANE_FAR = 1, 2, 4, 8, 16
PLANES = (0, PLANE_NEXT, PLANE_FAR, PLANE_NEXT | PLANE_FAR)
BLOCKS = 8
WEIGHT_SLOTS = 3
LANES = 128

(
    G,
    H,
    M,
    R,
    QUERIES,
    KEYS,
    VALUES,
    TOTALS,
    HEADS,
    KEPT,
    SENT,
    RAW,
    HOME,
    SUMS,
    NEAR,
    AWAY,
    OTHER,
    FAR,
    OWN,
    SIDE,
    FULL,
    GOT,
    IN,
    OUT,
    TOKENS,
    NAMED,
    ROUTER,
    GATES,
    ATTN,
    RELAY,
    MIXED,
    EXPERTS,
    SMALL,
    GAIN,
    PAIR,
) = range(35)


def rope_tables(seq_length, head_size):
    half_dim = head_size // 2
    frequency = jnp.exp(
        -jnp.log(theta_base) * jnp.arange(half_dim, dtype=jnp.float32) * (2.0 / head_size)
    )
    angles = jnp.arange(seq_length, dtype=jnp.float32)[:, None] * frequency[None, :]
    return (jnp.cos(angles)[:, None, :], jnp.sin(angles)[:, None, :])


def rotate(source, cosine_table, sine_table):
    half_dim = source.shape[-1] // 2
    first_half = source[..., :half_dim]
    second = source[..., half_dim:]
    return jnp.concatenate(
        [
            first_half * cosine_table - second * sine_table,
            second * cosine_table + first_half * sine_table,
        ],
        axis=-1,
    )


def norm_forward(source, gain_vec):
    inverse = lax.rsqrt(jnp.mean(source * source, axis=-1, keepdims=True) + eps)
    return (inverse, source * inverse * gain_vec)


def norm_backward(source, inverse, gain_vec, grad_in):
    scaled = gain_vec * grad_in
    grad_source = inverse * scaled - source * inverse**3 * jnp.mean(
        scaled * source, axis=-1, keepdims=True
    )
    grad_gain = jnp.sum(grad_in * source * inverse, axis=0)
    return (grad_source, grad_gain)


def block_scores(q_block, key_rows, first_row, score_scale):
    scores = (
        jnp.einsum("qgrd,kgd->grqk", q_block, key_rows, preferred_element_type=jnp.float32)
        * score_scale
    )
    row_ids = first_row + jnp.arange(q_block.shape[0], dtype=jnp.int32)
    allowed = row_ids[:, None] >= jnp.arange(key_rows.shape[0], dtype=jnp.int32)[None, :]
    return jnp.where(allowed, scores, masked)


def routed_layer(
    tokens,
    gain_attn,
    w_query,
    w_key,
    w_value,
    w_out,
    gain_moe,
    w_router,
    w_gate,
    w_up,
    w_down,
    expert_ids,
    cotangent,
):
    seq_length, model_width = tokens.shape
    block_len, top_count = expert_ids.shape
    expert_count = w_router.shape[1]
    local_experts = w_gate.shape[0]
    local_heads = w_query.shape[1] // HD
    local_groups = w_key.shape[1] // HD
    group_size = local_heads // local_groups
    owners = lax.axis_size("expert")
    quarter = lax.axis_index("tensor")
    capacity = 3 * block_len * top_count // (2 * expert_count)
    block_rows = min(512, seq_length)
    block_count = seq_length // block_rows
    score_scale = HD ** (-0.5)
    first_own = quarter * block_len
    inputs = tokens.astype(jnp.float32)
    inverse_one, normed_one = norm_forward(inputs, gain_attn)
    hidden_one = normed_one.astype(jnp.bfloat16)
    cosine_table, sine_table = rope_tables(seq_length, HD)

    def rope_heads(source):
        return rotate(source, cosine_table, sine_table)

    query_raw = jnp.dot(hidden_one, w_query, preferred_element_type=jnp.float32).reshape(
        seq_length, local_heads, HD
    )
    key_raw = jnp.dot(hidden_one, w_key, preferred_element_type=jnp.float32).reshape(
        seq_length, local_groups, HD
    )
    queries = rope_heads(query_raw).astype(jnp.bfloat16)
    key_rows = rope_heads(key_raw).astype(jnp.bfloat16)
    value_rows = (
        jnp.dot(hidden_one, w_value, preferred_element_type=jnp.float32)
        .astype(jnp.bfloat16)
        .reshape(seq_length, local_groups, HD)
    )
    query_blocks = queries.reshape(block_count, block_rows, local_groups, group_size, HD)
    starts = jnp.arange(block_count, dtype=jnp.int32) * block_rows

    def attend_block(packed):
        first_row, q_block = packed
        scores = block_scores(q_block, key_rows, first_row, score_scale)
        row_max = jnp.max(scores, axis=-1, keepdims=True)
        exponent = jnp.exp(scores - row_max)
        row_total = jnp.sum(exponent, axis=-1, keepdims=True)
        weights = (exponent / row_total).astype(jnp.bfloat16)
        head_out = jnp.einsum(
            "grqk,kgd->qgrd", weights, value_rows, preferred_element_type=jnp.float32
        )
        return (head_out.astype(jnp.bfloat16), (row_max + jnp.log(row_total))[..., 0])

    head_blocks, log_totals = lax.map(attend_block, (starts, query_blocks))
    head_rows = head_blocks.reshape(seq_length, local_heads * HD)
    attention = lax.psum_scatter(
        jnp.dot(head_rows, w_out, preferred_element_type=jnp.float32),
        "tensor",
        scatter_dimension=0,
        tiled=True,
    )
    own_inputs = lax.dynamic_slice_in_dim(inputs, first_own, block_len, 0)
    own_inverse = lax.dynamic_slice_in_dim(inverse_one, first_own, block_len, 0)
    middle = own_inputs + attention
    inverse_two, normed_two = norm_forward(middle, gain_moe)
    hidden_two = normed_two.astype(jnp.bfloat16)
    logits = jnp.dot(hidden_two, w_router, preferred_element_type=jnp.float32)
    expert_range = jnp.arange(expert_count, dtype=jnp.int32)
    matches = expert_ids[:, :, None] == expert_range[None, None, :]
    chosen = jnp.sum(jnp.where(matches, logits[:, None, :], 0.0), axis=2)
    gate_weights = jax.nn.softmax(chosen, axis=-1)
    expert_hits = jnp.sum(matches.astype(jnp.int32), axis=1)
    earlier = jnp.cumsum(expert_hits, axis=0) - expert_hits
    slot_of = jnp.sum(jnp.where(matches, earlier[:, None, :], 0), axis=2)
    place = (slot_of * expert_count + expert_ids).reshape(-1)
    token_rows = jnp.broadcast_to(
        hidden_two[:, None, :], (block_len, top_count, model_width)
    ).reshape(block_len * top_count, model_width)
    grad_out = cotangent.astype(jnp.float32)
    gated_grads = (
        (gate_weights[:, :, None] * grad_out[:, None, :])
        .astype(jnp.bfloat16)
        .reshape(block_len * top_count, model_width)
    )
    empty = jnp.zeros((capacity * expert_count, model_width), jnp.bfloat16)
    send_rows = empty.at[place].set(token_rows).reshape(capacity, expert_count, model_width)
    send_grads = empty.at[place].set(gated_grads).reshape(capacity, expert_count, model_width)
    arrived_rows, arrived_grads = (
        lax.all_to_all(send_rows, "expert", split_axis=1, concat_axis=1, tiled=True),
        lax.all_to_all(send_grads, "expert", split_axis=1, concat_axis=1, tiled=True),
    )
    routed = arrived_rows.reshape(capacity, owners, local_experts, model_width)
    grads_in = arrived_grads.reshape(capacity, owners, local_experts, model_width)
    all_rows, all_grads = (
        lax.all_gather(routed, "tensor", axis=0, tiled=True),
        lax.all_gather(grads_in, "tensor", axis=0, tiled=True),
    )
    gate_pre = jnp.einsum("csld,ldf->cslf", all_rows, w_gate, preferred_element_type=jnp.float32)
    up_pre = jnp.einsum("csld,ldf->cslf", all_rows, w_up, preferred_element_type=jnp.float32)
    sigmoid_gate = jax.nn.sigmoid(gate_pre)
    silu_gate = gate_pre * sigmoid_gate
    activation = (silu_gate * up_pre).astype(jnp.bfloat16)
    grad_w_down = jnp.einsum(
        "cslf,csld->lfd", activation, all_grads, preferred_element_type=jnp.float32
    )
    grad_act = jnp.einsum("csld,lfd->cslf", all_grads, w_down, preferred_element_type=jnp.float32)
    grad_gate = (grad_act * up_pre * sigmoid_gate * (1.0 + gate_pre * (1.0 - sigmoid_gate))).astype(
        jnp.bfloat16
    )
    grad_up = (grad_act * silu_gate).astype(jnp.bfloat16)
    grad_w_gate = jnp.einsum(
        "csld,cslf->ldf", all_rows, grad_gate, preferred_element_type=jnp.float32
    )
    grad_w_up = jnp.einsum("csld,cslf->ldf", all_rows, grad_up, preferred_element_type=jnp.float32)
    forward_term = jnp.einsum(
        "cslf,lfd->csld", activation, w_down, preferred_element_type=jnp.float32
    )
    back_term = jnp.einsum("cslf,ldf->csld", grad_gate, w_gate, preferred_element_type=jnp.float32)
    back_term = back_term + jnp.einsum(
        "cslf,ldf->csld", grad_up, w_up, preferred_element_type=jnp.float32
    )
    both_terms = lax.psum_scatter(
        jnp.concatenate([forward_term, back_term], axis=3).astype(jnp.bfloat16),
        "tensor",
        scatter_dimension=0,
        tiled=True,
    )
    returned = both_terms[..., :model_width]
    row_grads = both_terms[..., model_width:]
    returned_home, row_grads_home = (
        lax.all_to_all(
            returned.reshape(capacity, expert_count, model_width),
            "expert",
            split_axis=1,
            concat_axis=1,
            tiled=True,
        ),
        lax.all_to_all(
            row_grads.reshape(capacity, expert_count, model_width),
            "expert",
            split_axis=1,
            concat_axis=1,
            tiled=True,
        ),
    )
    picked = returned_home.reshape(capacity * expert_count, model_width)[place].reshape(
        block_len, top_count, model_width
    )
    mixture = jnp.sum(gate_weights[:, :, None] * picked, axis=1)
    mixed_out = (middle + mixture).astype(jnp.bfloat16)
    grad_gates = jnp.sum(picked * grad_out[:, None, :], axis=2)
    grad_picked = row_grads_home.reshape(capacity * expert_count, model_width)[place].reshape(
        block_len, top_count, model_width
    )
    grad_hidden_disp = jnp.einsum(
        "lk,lkd->ld",
        jnp.ones((block_len, top_count), jnp.bfloat16),
        grad_picked,
        preferred_element_type=jnp.float32,
    )
    grad_chosen = gate_weights * (
        grad_gates - jnp.sum(gate_weights * grad_gates, axis=-1, keepdims=True)
    )
    grad_logits = jnp.sum(jnp.where(matches, grad_chosen[:, :, None], 0.0), axis=1).astype(
        jnp.bfloat16
    )
    grad_router = jnp.einsum(
        "ld,le->de", hidden_two, grad_logits, preferred_element_type=jnp.float32
    )
    grad_hidden_two = grad_hidden_disp + jnp.einsum(
        "le,de->ld", grad_logits, w_router, preferred_element_type=jnp.float32
    )
    grad_normed_two, grad_gain_moe = norm_backward(middle, inverse_two, gain_moe, grad_hidden_two)
    grad_middle = grad_out + grad_normed_two
    grad_attn = grad_middle.astype(jnp.bfloat16)
    grad_attn_all = lax.all_gather(grad_attn, "tensor", axis=0, tiled=True)
    grad_w_out = jnp.einsum(
        "lh,ld->hd", head_rows, grad_attn_all, preferred_element_type=jnp.float32
    )
    grad_heads = jnp.einsum(
        "ld,hd->lh", grad_attn_all, w_out, preferred_element_type=jnp.float32
    ).astype(jnp.bfloat16)
    grad_blocks = grad_heads.reshape(block_count, block_rows, local_groups, group_size, HD)

    def back_block(carried, packed):
        grad_keys, grad_values = carried
        first_row, q_block, g_block, lse_block = packed
        scores = block_scores(q_block, key_rows, first_row, score_scale)
        probability = jnp.exp(scores - lse_block[..., None])
        grad_values = grad_values + jnp.einsum(
            "grqk,qgrd->kgd",
            probability.astype(jnp.bfloat16),
            g_block,
            preferred_element_type=jnp.float32,
        )
        grad_prob = jnp.einsum(
            "qgrd,kgd->grqk", g_block, value_rows, preferred_element_type=jnp.float32
        )
        row_delta = jnp.sum(probability * grad_prob, axis=-1, keepdims=True)
        grad_scores = (probability * (grad_prob - row_delta)).astype(jnp.bfloat16)
        grad_query = (
            jnp.einsum("grqk,kgd->qgrd", grad_scores, key_rows, preferred_element_type=jnp.float32)
            * score_scale
        )
        grad_keys = (
            grad_keys
            + jnp.einsum("grqk,qgrd->kgd", grad_scores, q_block, preferred_element_type=jnp.float32)
            * score_scale
        )
        return ((grad_keys, grad_values), grad_query)

    zero_keys = jnp.zeros((seq_length, local_groups, HD), jnp.float32)
    (grad_keys, grad_values), grad_query_blocks = lax.scan(
        back_block, (zero_keys, zero_keys), (starts, query_blocks, grad_blocks, log_totals)
    )
    grad_query = grad_query_blocks.reshape(seq_length, local_heads, HD)
    grad_query_raw = (
        jax.vjp(rope_heads, query_raw)[1](grad_query)[0]
        .reshape(seq_length, local_heads * HD)
        .astype(jnp.bfloat16)
    )
    grad_key_raw = (
        jax.vjp(rope_heads, key_raw)[1](grad_keys)[0]
        .reshape(seq_length, local_groups * HD)
        .astype(jnp.bfloat16)
    )
    grad_value_raw = grad_values.reshape(seq_length, local_groups * HD).astype(jnp.bfloat16)
    grad_w_query = jnp.einsum(
        "ld,lh->dh", hidden_one, grad_query_raw, preferred_element_type=jnp.float32
    )
    grad_w_key = jnp.einsum(
        "ld,lh->dh", hidden_one, grad_key_raw, preferred_element_type=jnp.float32
    )
    grad_w_value = jnp.einsum(
        "ld,lh->dh", hidden_one, grad_value_raw, preferred_element_type=jnp.float32
    )
    term = jnp.einsum("lh,dh->ld", grad_query_raw, w_query, preferred_element_type=jnp.float32)
    term = term + jnp.einsum("lh,dh->ld", grad_key_raw, w_key, preferred_element_type=jnp.float32)
    grad_hidden_one = lax.psum_scatter(
        (
            term
            + jnp.einsum("lh,dh->ld", grad_value_raw, w_value, preferred_element_type=jnp.float32)
        ).astype(jnp.bfloat16),
        "tensor",
        scatter_dimension=0,
        tiled=True,
    ).astype(jnp.float32)
    grad_normed_one, grad_gain_attn = norm_backward(
        own_inputs, own_inverse, gain_attn, grad_hidden_one
    )
    grad_tokens = grad_middle + grad_normed_one
    attn_sums = lax.psum((grad_w_query, grad_w_key, grad_w_value, grad_w_out), "expert")
    small_sums = lax.psum((grad_gain_attn, grad_gain_moe, grad_router), ("expert", "tensor"))
    return (
        mixed_out,
        grad_tokens,
        small_sums[0],
        attn_sums[0],
        attn_sums[1],
        attn_sums[2],
        attn_sums[3],
        small_sums[1],
        small_sums[2],
        grad_w_gate,
        grad_w_up,
        grad_w_down,
    )


ROWS_ROWS = (((1,), (1,)), ((), ()))
def dot_nt(left, right):
    return lax.dot_general(left, right, ROWS_ROWS, preferred_element_type=jnp.float32)


def dot_nn(left, right):
    return jnp.dot(left, right, preferred_element_type=jnp.float32)


def expert_kernel(places, top_count, *refs):
    row_places, grad_places = places
    given = 1 + max(place[0] for place in row_places + grad_places)
    numbers_ref, router_ref, gate_ref, up_ref, down_ref = refs[given : given + 5]
    outs = refs[given + 5 : given + 14]
    mixed_refs, back_refs, sums_ref = outs[:2], outs[2:4], outs[4]
    rows_s, grads_s, ids_s, x_s, y_s, back_s, out_s = refs[given + 14 : given + 21]
    pick_s, place_s, gates_s, sums_s, gated_s, side_s = refs[given + 21 : given + 27]
    both_s, down_s, sems, weight_sems, out_sems, kept_sems = refs[given + 27 :]
    pairs, wide, _ = pick_s.shape
    experts = x_s.shape[0]
    hidden = down_s.shape[1]
    cap = wide // experts
    tokens_in, width = rows_s.shape[1:]
    block_len = tokens_in // 2
    narrow = jnp.bfloat16

    def copies(pair):
        out = []
        for half in range(2):
            target = pl.ds(half * block_len, block_len)
            at = 2 * pair + half
            array, row, column = row_places[at]
            rows = refs[array].at[pl.ds(row, block_len), pl.ds(column, width)]
            array, row, column = grad_places[at]
            block = refs[array].at[pl.ds(row, block_len)]
            grads = block.at[:, pl.ds(column, width)]
            ids = block.at[:, pl.ds(column + width, LANES)]
            for k, (source, scratch) in enumerate(
                ((rows, rows_s), (grads, grads_s), (ids, ids_s))
            ):
                out.append(
                    pltpu.make_async_copy(source, scratch.at[pair, target], sems.at[k, at])
                )
        return out

    def weight_copies(expert, slot):
        sides = [both_s.at[slot, :, pl.ds(k * hidden, hidden)] for k in range(2)]
        return [
            pltpu.make_async_copy(gate_ref.at[expert], sides[0], weight_sems.at[0, slot]),
            pltpu.make_async_copy(up_ref.at[expert], sides[1], weight_sems.at[1, slot]),
            pltpu.make_async_copy(down_ref.at[expert], down_s.at[slot], weight_sems.at[2, slot]),
        ]

    def result_copies(pair):
        half = pairs // 2
        place = pl.ds((pair % half) * tokens_in, tokens_in)
        sides = (rows_s, mixed_refs), (grads_s, back_refs)
        return [
            pltpu.make_async_copy(
                source.at[pair], targets[pair // half].at[place], out_sems.at[k, pair]
            )
            for k, (source, targets) in enumerate(sides)
        ]

    kept_copies = [
        pltpu.make_async_copy(source, target, kept_sems.at[k])
        for k, (source, target) in enumerate(zip((x_s, y_s, gated_s, side_s), outs[5:9]))
    ]

    for pair in range(pairs):
        for copy in copies(pair):
            copy.start()
    for slot in range(WEIGHT_SLOTS):
        for copy in weight_copies(slot, slot):
            copy.start()

    earlier = lax.broadcasted_iota(jnp.int32, (tokens_in, tokens_in), 0)
    later = lax.broadcasted_iota(jnp.int32, (tokens_in, tokens_in), 1)
    before = jnp.where(earlier < later, 1.0, 0.0).astype(narrow)

    for pair in range(pairs):
        for copy in copies(pair):
            copy.wait()
        rows_in = rows_s[pair]
        logits = dot_nt(router_ref[...], rows_in)
        ids = ids_s[pair].astype(jnp.float32).T
        named = jnp.zeros(logits.shape, jnp.float32)
        for k in range(top_count):
            named = jnp.where(ids[k : k + 1, :] == numbers_ref[:, :1], 1.0, named)
        hits = named[:experts]
        slots = jnp.where(hits > 0.0, dot_nn(hits.astype(narrow), before), -1.0)
        slots = slots.astype(jnp.int32)
        logits = jnp.where(named > 0.0, logits, masked)
        weights = jnp.exp(logits - jnp.max(logits, axis=0, keepdims=True)) * named
        gates = weights / jnp.sum(weights, axis=0, keepdims=True)
        ranks = lax.broadcasted_iota(jnp.int32, (cap, tokens_in), 0)
        place = pl.ds(pair * cap, cap)
        picks = []
        for expert in range(experts):
            pick = ranks == slots[expert : expert + 1, :]
            row_gates = jnp.sum(
                jnp.where(pick, gates[expert : expert + 1, :], 0.0), axis=1, keepdims=True
            )
            gates_s[expert, place, :] = jnp.broadcast_to(row_gates, (cap, LANES))
            picks.append(jnp.where(pick, 1.0, 0.0))
        pick_all = jnp.concatenate(picks, axis=0)
        pick_low = pick_all.astype(narrow)
        pick_s[pair] = pick_low
        place_s[pair] = pick_all.T.astype(narrow)
        for source, target in ((rows_in, x_s), (grads_s[pair], y_s)):
            spread = dot_nn(pick_low, source).astype(narrow)
            for expert in range(experts):
                target[expert, place, :] = spread[expert * cap : (expert + 1) * cap]

    kept_copies[0].start()
    kept_copies[1].start()

    def expert_step(expert, carried):
        slot = lax.rem(expert, WEIGHT_SLOTS)
        for copy in weight_copies(expert, slot):
            copy.wait()
        both = dot_nn(x_s[expert], both_s[slot])
        gate_pre, up_pre = both[:, :hidden], both[:, hidden:]
        plain = dot_nt(y_s[expert], down_s[slot])
        sigmoid_gate = jax.nn.sigmoid(gate_pre)
        silu_gate = gate_pre * sigmoid_gate
        activation = silu_gate * up_pre
        row_gates = gates_s[expert][:, :1]
        sums = jnp.sum(activation * plain, axis=1, keepdims=True)
        sums_s[expert] = jnp.broadcast_to(sums, sums_s.shape[1:])
        grad_act = row_gates * plain
        gated = (row_gates * activation).astype(narrow)
        slope = sigmoid_gate * (1.0 + gate_pre * (1.0 - sigmoid_gate))
        grad_gate = (grad_act * up_pre * slope).astype(narrow)
        grad_up = (grad_act * silu_gate).astype(narrow)
        grad_both = jnp.concatenate([grad_gate, grad_up], axis=1)
        gated_s[expert] = gated
        side_s[expert] = grad_both
        out_s[expert] = dot_nn(gated, down_s[slot]).astype(narrow)
        back_s[expert] = dot_nt(grad_both, both_s[slot]).astype(narrow)

        @pl.when(expert + WEIGHT_SLOTS < experts)
        def _():
            for copy in weight_copies(expert + WEIGHT_SLOTS, slot):
                copy.start()

        return carried

    lax.fori_loop(0, experts, expert_step, 0)
    kept_copies[2].start()
    kept_copies[3].start()

    for pair in range(pairs):
        sides = pl.ds(pair * cap, cap)
        for source, target in ((out_s, rows_s), (back_s, grads_s)):
            stacked = jnp.concatenate(
                [source[expert, sides, :] for expert in range(experts)], axis=0
            )
            target[pair] = dot_nn(place_s[pair], stacked).astype(narrow)
        for copy in result_copies(pair):
            copy.start()
        pick = pick_s[pair].astype(jnp.float32)
        sums = []
        for expert in range(experts):
            column = sums_s[expert, sides, :][:, :1]
            part = pick[expert * cap : (expert + 1) * cap] * column
            sums.append(jnp.sum(part, axis=0, keepdims=True))
        sums_ref[pair] = jnp.concatenate(sums, axis=0)

    for copy in kept_copies:
        copy.wait()
    for pair in range(pairs):
        for copy in result_copies(pair):
            copy.wait()


def expert_chunk(arrays, places, numbers, router, w_gate, w_up, w_down, tokens_in, top_count, cap):
    experts, width, hidden = w_gate.shape
    pairs = BLOCKS // 2
    rows = pairs * cap
    narrow, wide = jnp.bfloat16, jnp.float32
    shape = jax.ShapeDtypeStruct
    anywhere = pl.BlockSpec(memory_space=pl.ANY)
    inside = pl.BlockSpec(memory_space=pltpu.VMEM)
    half_shape = shape((pairs // 2 * tokens_in, width), narrow)
    whole_rows = (experts, rows, width)
    return pl.pallas_call(
        functools.partial(expert_kernel, places, top_count),
        in_specs=[anywhere] * len(arrays) + [inside] * 2 + [anywhere] * 3,
        out_specs=[anywhere] * 4 + [inside] + [anywhere] * 4,
        out_shape=[half_shape] * 4
        + [
            shape((pairs, experts, tokens_in), wide),
            shape(whole_rows, narrow),
            shape(whole_rows, narrow),
            shape((experts, rows, hidden), narrow),
            shape((experts, rows, 2 * hidden), narrow),
        ],
        scratch_shapes=[pltpu.VMEM((pairs, tokens_in, width), narrow)] * 2
        + [pltpu.VMEM((pairs, tokens_in, LANES), narrow)]
        + [pltpu.VMEM(whole_rows, narrow)] * 4
        + [
            pltpu.VMEM((pairs, experts * cap, tokens_in), narrow),
            pltpu.VMEM((pairs, tokens_in, experts * cap), narrow),
            pltpu.VMEM((experts, rows, LANES), wide),
            pltpu.VMEM((experts, rows, LANES), wide),
            pltpu.VMEM((experts, rows, hidden), narrow),
            pltpu.VMEM((experts, rows, 2 * hidden), narrow),
            pltpu.VMEM((WEIGHT_SLOTS, width, 2 * hidden), narrow),
            pltpu.VMEM((WEIGHT_SLOTS, hidden, width), narrow),
            pltpu.SemaphoreType.DMA((3, BLOCKS)),
            pltpu.SemaphoreType.DMA((3, WEIGHT_SLOTS)),
            pltpu.SemaphoreType.DMA((2, pairs)),
            pltpu.SemaphoreType.DMA((4,)),
        ],
        compiler_params=pltpu.CompilerParams(vmem_limit_bytes=60 << 20),
        cost_estimate=pl.CostEstimate(
            flops=24 * experts * rows * width * hidden,
            bytes_accessed=6 * experts * width * hidden + 4 * experts * rows * width,
            transcendentals=experts * rows * hidden,
        ),
    )(*arrays, numbers, router, w_gate, w_up, w_down)


def weight_kernel(parts, given, *refs):
    ins, (gate_ref, up_ref, down_ref) = refs[: 4 * parts], refs[4 * parts + given :]
    rows, grads, gated, both = [
        jnp.concatenate([ref[0] for ref in ins[k * parts : (k + 1) * parts]], axis=0)
        for k in range(4)
    ]
    turn = (((0,), (0,)), ((), ()))
    hidden = gated.shape[1]
    down_ref[0] = lax.dot_general(gated, grads, turn, preferred_element_type=jnp.float32)
    sides = lax.dot_general(rows, both, turn, preferred_element_type=jnp.float32)
    gate_ref[0] = sides[:, :hidden]
    up_ref[0] = sides[:, hidden:]


def weight_grads(kept, begin, count, partial):
    parts = len(kept)
    experts, rows, width = kept[0][0].shape
    hidden = kept[0][2].shape[2]
    operands = [part[k] for k in range(4) for part in kept]
    shape = jax.ShapeDtypeStruct

    def spec(rows, columns):
        return pl.BlockSpec((1, rows, columns), lambda i: (i + begin, 0, 0))

    return pl.pallas_call(
        functools.partial(weight_kernel, parts, len(partial)),
        grid=(count,),
        in_specs=[spec(rows, operand.shape[2]) for operand in operands]
        + [pl.BlockSpec(memory_space=pl.ANY)] * len(partial),
        out_specs=[spec(width, hidden), spec(width, hidden), spec(hidden, width)],
        out_shape=[
            shape((experts, width, hidden), jnp.float32),
            shape((experts, width, hidden), jnp.float32),
            shape((experts, hidden, width), jnp.float32),
        ],
        input_output_aliases={len(operands) + k: k for k in range(len(partial))},
        compiler_params=pltpu.CompilerParams(vmem_limit_bytes=56 << 20),
        cost_estimate=pl.CostEstimate(
            flops=6 * parts * count * rows * width * hidden,
            bytes_accessed=count * (parts * rows * (4 * width + 6 * hidden) + 12 * width * hidden),
            transcendentals=0,
        ),
    )(*operands, *partial)


def gathered_layer(
    tokens,
    gain_attn,
    w_query,
    w_key,
    w_value,
    w_out,
    gain_moe,
    w_router,
    w_gate,
    w_up,
    w_down,
    expert_ids,
    cotangent,
):
    seq_length, model_width = tokens.shape
    block_len, top_count = expert_ids.shape
    expert_count = w_router.shape[1]
    local_experts = w_gate.shape[0]
    local_heads = w_query.shape[1] // HD
    quarters = lax.axis_size("tensor")
    device_count = quarters * lax.axis_size("expert")
    quarter = lax.axis_index("tensor").astype(jnp.uint32)
    device = lax.axis_index(BOTH).astype(jnp.uint32)
    first_expert = lax.axis_index("expert") * local_experts
    pair_cap = 2 * (3 * block_len * top_count // (2 * expert_count))
    score_scale = HD ** (-0.5)
    narrow, wide = jnp.bfloat16, jnp.float32

    def swap(value, even, odd=None):
        odd = even if odd is None else odd
        perm = [(i, i ^ (odd if i & 1 else even)) for i in range(device_count)]
        return lax.ppermute(value, BOTH, perm)

    def near(value):
        return swap(value, ACROSS, ASIDE)

    def far(value):
        return swap(value, ASIDE, ACROSS)

    def core(value):
        return swap(value, CORE)

    def add(left, right):
        return (left.astype(wide) + right.astype(wide)).astype(narrow)

    live = {}

    def sync():
        keys = list(live)
        values = lax.optimization_barrier([live[key] for key in keys])
        live.update(zip(keys, values))

    def gather_near(name, plane):
        live[name, plane, 1] = near(live[name, plane, 0])
        live[name, plane, 2] = far(live[name, plane, 0])

    def gather_far(name, plane):
        live[name, plane, 3] = far(live[name, plane, 1])

    def gather_across(name, plane):
        live[name, plane, 3] = swap(live[name, plane, 0], ACROSS | ASIDE)

    def gather_core(name, plane, *slots):
        blocks = [live[name, plane, slot] for slot in slots]
        live[name, plane, (OTHER,) + slots] = core(jnp.concatenate(blocks, axis=0))

    def blocks_of(name, plane):
        found = {}
        for key in list(live):
            if isinstance(key, tuple) and key[:2] == (name, plane):
                slots = key[2]
                array = live.pop(key)
                if isinstance(slots, tuple):
                    for i, slot in enumerate(slots[1:]):
                        found[4 + slot] = (array, i * block_len)
                else:
                    found[slots] = (array, 0)
        return [found[slot] for slot in range(BLOCKS)]

    def reduce_core(name, plane):
        live[name, plane, OTHER] = core(live.pop((name, plane, AWAY)))

    def reduce_far(name, plane):
        kept = live.pop((name, plane, NEAR)).reshape(4, block_len, model_width)
        got = live.pop((name, plane, OTHER)).reshape(4, block_len, model_width)
        live[name, plane, SUMS] = add(kept[:2], got[:2])
        live[name, plane, FAR] = far(add(kept[2:], got[2:]))

    def reduce_near(name, plane):
        sums, got = live.pop((name, plane, SUMS)), live.pop((name, plane, FAR))
        live[name, plane, OWN] = add(sums[0], got[0])
        live[name, plane, SIDE] = near(add(sums[1], got[1]))

    def reduced(name, plane):
        return add(live.pop((name, plane, OWN)), live.pop((name, plane, SIDE)))

    def bit(mask):
        return (device // mask) % 2

    odd_core = bit(CORE)
    weight_hops = ((ASIDE, PLANE_NEXT), (PLANE_NEXT, ASIDE), (PLANE_FAR, PLANE_FAR))
    small_hops = tuple((mask, mask) for mask in (CORE, ACROSS, ASIDE, PLANE_NEXT, PLANE_FAR))

    def joined(own, got, side):
        count = own.shape[0]
        both = jnp.zeros((2 * count,) + own.shape[1:], own.dtype)
        both = lax.dynamic_update_slice_in_dim(both, own, side * count, 0)
        return lax.dynamic_update_slice_in_dim(both, got, (1 - side) * count, 0)

    def sum_step(name, step, hops=weight_hops, sent_as=narrow):
        count = len(hops)
        sides = [jnp.where(odd_core == 0, bit(even), bit(odd)) for even, odd in hops]
        if step == 0:
            kept = live.pop((name, FULL))
        elif step <= count:
            kept = live.pop((name, KEPT)) + live.pop((name, GOT)).astype(wide)
        else:
            kept = joined(live.pop((name, KEPT)), live.pop((name, GOT)), sides[2 * count - step])
        if step < count:
            half = kept.shape[0] // 2
            side = sides[step]
            live[name, KEPT] = lax.dynamic_slice_in_dim(kept, side * half, half, 0)
            sent = lax.dynamic_slice_in_dim(kept, (1 - side) * half, half, 0)
            live[name, GOT] = swap(sent.astype(sent_as), *hops[step])
        else:
            kept = kept.astype(sent_as)
            live[name, KEPT] = kept
            live[name, GOT] = swap(kept, *hops[2 * count - 1 - step])

    def summed(name, hops=weight_hops):
        even, odd = hops[0]
        side = jnp.where(odd_core == 0, bit(even), bit(odd))
        return joined(live.pop((name, KEPT)), live.pop((name, GOT)), side).astype(wide)

    own, nxt, far_plane, last = PLANES

    named_ids = jnp.pad(expert_ids.astype(narrow), ((0, 0), (0, LANES - top_count)))
    live[G, own, 0] = jnp.concatenate([cotangent, named_ids], axis=1)
    live[G, nxt, 0] = swap(live[G, own, 0], nxt)
    live[G, last, 0] = swap(live[G, own, 0], last)
    gather_near(G, own)

    by_block = tokens.reshape(quarters, block_len, model_width)
    inputs = jnp.concatenate(
        [lax.dynamic_slice_in_dim(by_block, quarter ^ r, 1, 0)[0] for r in range(quarters)], axis=0
    )
    inputs = lax.optimization_barrier(inputs).astype(wide)
    order = quarter.astype(jnp.int32) ^ jnp.arange(quarters, dtype=jnp.int32)
    positions = (order[:, None] * block_len + jnp.arange(block_len, dtype=jnp.int32)).reshape(-1)
    inverse_one, normed_one = norm_forward(inputs, gain_attn)
    hidden_one = normed_one.astype(narrow)
    frequency = jnp.exp(
        -jnp.log(theta_base) * jnp.arange(HD // 2, dtype=jnp.float32) * (2.0 / HD)
    )
    angles = positions.astype(wide)[:, None] * frequency[None, :]
    cosine_table, sine_table = (jnp.cos(angles)[:, None, :], jnp.sin(angles)[:, None, :])

    def project(weights):
        return jnp.dot(hidden_one, weights, preferred_element_type=wide).reshape(
            seq_length, local_heads, HD
        )

    live[QUERIES] = rotate(project(w_query), cosine_table, sine_table).astype(narrow)
    live[KEYS] = rotate(project(w_key), cosine_table, sine_table).astype(narrow)
    live[VALUES] = project(w_value).astype(narrow)
    sync()

    gather_far(G, own)
    gather_near(G, nxt)
    live[G, far_plane, 0] = swap(live[G, own, 0], far_plane)
    allowed = positions[:, None] >= positions[None, :]

    def masked_scores():
        scores = jnp.einsum(
            "qhd,khd->hqk", live[QUERIES], live[KEYS], preferred_element_type=wide
        )
        return jnp.where(allowed, scores * score_scale, masked)

    scores = masked_scores()
    row_max = jnp.max(scores, axis=-1, keepdims=True)
    exponent = jnp.exp(scores - row_max)
    row_total = jnp.sum(exponent, axis=-1, keepdims=True)
    weights = (exponent / row_total).astype(narrow)
    head_out = jnp.einsum("hqk,khd->qhd", weights, live[VALUES], preferred_element_type=wide)
    live[TOTALS] = row_max + jnp.log(row_total)
    live[HEADS] = head_out.astype(narrow).reshape(seq_length, local_heads * HD)

    def split_quarters(full):
        parts = full.reshape(quarters, block_len, model_width)
        live[KEPT] = [parts[0], parts[2]]
        live[SENT] = jnp.stack([parts[1], parts[3]]).astype(narrow)

    split_quarters(jnp.dot(live[HEADS], w_out, preferred_element_type=wide))
    sync()

    live[SENT] = core(live[SENT])
    gather_far(G, nxt)
    gather_core(G, own, 0, 1, 2, 3)
    sync()

    def cross_quarters():
        kept, sent = live.pop(KEPT), live.pop(SENT).astype(wide)
        live[KEPT] = kept[0] + sent[0]
        live[SENT] = swap((kept[1] + sent[1]).astype(narrow), ACROSS)

    def quarter_sum():
        return live.pop(KEPT) + live.pop(SENT).astype(wide)

    cross_quarters()
    gather_core(G, nxt, 0, 1, 2, 3)
    sync()

    own_inputs = inputs[:block_len]
    own_inverse = inverse_one[:block_len]
    middle = own_inputs + quarter_sum()
    inverse_two, normed_two = norm_forward(middle, gain_moe)
    hidden_two = normed_two.astype(narrow)
    live[H, own, 0] = hidden_two

    gather_near(H, own)
    live[H, nxt, 0] = swap(hidden_two, nxt)
    logits = jnp.dot(hidden_two, w_router, preferred_element_type=wide)
    expert_range = jnp.arange(expert_count, dtype=jnp.int32)
    matches = expert_ids[:, :, None] == expert_range[None, None, :]
    chosen = jnp.sum(jnp.where(matches, logits[:, None, :], 0.0), axis=2)
    gate_weights = jax.nn.softmax(chosen, axis=-1)
    rolled = (first_expert + expert_range) % expert_count
    live[ROUTER] = jnp.take(w_router.T, rolled, axis=0)
    live[NAMED] = jnp.broadcast_to(rolled.astype(wide)[:, None], (expert_count, LANES))
    sync()

    gather_far(H, own)
    gather_near(H, nxt)
    live[H, last, 0] = swap(live[H, own, 0], last)
    sync()

    gather_far(H, nxt)
    gather_core(H, own, 0, 1, 2, 3)
    live[PAIR, last, 0] = jnp.concatenate([live.pop((H, last, 0)), live.pop((G, last, 0))], axis=1)
    sync()

    def experts(plane):
        if (PAIR, plane, 0) in live:
            rows = blocks_of(PAIR, plane)
            grads, column = rows, model_width
        else:
            rows, grads, column = blocks_of(H, plane), blocks_of(G, plane), 0
        arrays = []
        for array, _ in rows + grads:
            if not any(array is other for other in arrays):
                arrays.append(array)

        def placed(blocks, column):
            indices = [[array is other for other in arrays].index(True) for array, _ in blocks]
            return [(index, row, column) for index, (_, row) in zip(indices, blocks)]

        done = expert_chunk(
            arrays,
            (placed(rows, 0), placed(grads, column)),
            live[NAMED],
            live[ROUTER],
            w_gate,
            w_up,
            w_down,
            2 * block_len,
            top_count,
            pair_cap,
        )
        live[M, plane, NEAR], live[M, plane, AWAY] = done[:2]
        live[R, plane, NEAR], live[R, plane, AWAY] = done[2:4]
        live[SUMS, plane] = done[4]
        live[KEPT, plane] = done[5:]

    hidden_two_sent = live[H, own, 0]
    gather_core(H, nxt, 0, 1, 2, 3)
    gather_near(PAIR, last)
    live[H, far_plane, 0] = swap(hidden_two_sent, far_plane)
    experts(own)
    sync()

    gather_far(PAIR, last)
    gather_core(PAIR, last, 0, 1, 2)
    live[PAIR, far_plane, 0] = jnp.concatenate(
        [live.pop((H, far_plane, 0)), live.pop((G, far_plane, 0))], axis=1
    )
    gather_near(PAIR, far_plane)
    reduce_core(R, own)
    experts(nxt)
    sync()
    gather_core(PAIR, last, 3)
    sync()

    gather_far(PAIR, far_plane)
    gather_core(PAIR, far_plane, 0, 1, 2)
    reduce_far(R, own)
    reduce_core(R, nxt)
    reduce_core(M, own)
    experts(last)
    sync()
    gather_core(PAIR, far_plane, 3)
    reduce_core(R, last)
    sync()

    reduce_near(R, own)
    reduce_far(R, nxt)
    reduce_far(R, last)
    reduce_core(M, nxt)
    experts(far_plane)
    sync()

    part_experts = local_experts // 4

    def some_weight_grads(part):
        kept = [live[KEPT, plane] for plane in PLANES]
        live[EXPERTS] = weight_grads(kept, part * part_experts, part_experts, live.get(EXPERTS, []))

    reduce_core(R, far_plane)
    sums = jnp.stack([live.pop((SUMS, plane)) for plane in PLANES])
    sums = sums.reshape(len(PLANES), -1, local_experts, 2, block_len).transpose(0, 1, 3, 2, 4)
    sums = sums.reshape(len(PLANES), BLOCKS, local_experts, block_len)
    live[GATES] = [sums[:, :4], core(sums[:, 4:])]
    reduce_core(M, last)
    sync()

    reduce_near(R, last)
    reduce_near(R, nxt)
    reduce_far(R, far_plane)
    sums = live[GATES][0] + live[GATES][1]
    crossed = jnp.stack([sums[:, 0], sums[:, 2], sums[:, 1], sums[:, 3]], axis=1)
    sums = jnp.where(odd_core == 0, sums, crossed)
    live[GATES] = [sums[:, ::2], swap(sums[:, 1::2], ACROSS)]
    live[HOME] = reduced(R, own)
    some_weight_grads(0)
    some_weight_grads(1)
    sync()

    live[RELAY] = swap(reduced(R, last), nxt)
    reduce_near(R, far_plane)
    sums = live[GATES][0] + live[GATES][1]
    live[GATES] = [sums[:, 0], swap(sums[:, 1], ASIDE)]
    reduce_core(M, far_plane)
    reduce_far(M, last)
    some_weight_grads(2)
    sync()

    live[RELAY] = swap(add(reduced(R, far_plane), live[RELAY]), far_plane)
    live[SIDE] = swap(reduced(R, nxt), nxt)
    sums = jnp.stack(live[GATES], axis=1)
    live[GATES] = [sums[0]] + [swap(sums[i], PLANES[i]) for i in range(1, len(PLANES))]
    reduce_near(M, last)
    reduce_far(M, far_plane)
    some_weight_grads(3)
    sync()
    for plane in PLANES:
        live.pop((KEPT, plane))

    grad_hidden_disp = live.pop(HOME).astype(wide) + live.pop(RELAY).astype(wide)
    grad_hidden_disp = grad_hidden_disp + live.pop(SIDE).astype(wide)
    sums = jnp.concatenate(live.pop(GATES), axis=0)
    owner = lax.axis_index("expert").astype(jnp.uint32)
    sums = [lax.dynamic_slice_in_dim(sums, owner ^ r, 1, 0)[0] for r in range(sums.shape[0])]
    own_sums = jnp.concatenate(sums, axis=0).T
    grad_out = cotangent.astype(wide)
    grad_gates = jnp.sum(jnp.where(matches, own_sums[:, None, :], 0.0), axis=2)
    grad_chosen = gate_weights * (
        grad_gates - jnp.sum(gate_weights * grad_gates, axis=-1, keepdims=True)
    )
    grad_logits = jnp.sum(jnp.where(matches, grad_chosen[:, :, None], 0.0), axis=1).astype(narrow)
    grad_router = jnp.einsum("ld,le->de", hidden_two, grad_logits, preferred_element_type=wide)
    grad_hidden_two = grad_hidden_disp + jnp.einsum(
        "le,de->ld", grad_logits, w_router, preferred_element_type=wide
    )
    grad_normed_two, grad_gain_moe = norm_backward(middle, inverse_two, gain_moe, grad_hidden_two)
    grad_middle = grad_out + grad_normed_two
    grad_attn = grad_middle.astype(narrow)

    small = jnp.concatenate([grad_router, grad_gain_moe[:, None]], axis=1)
    live[SMALL, FULL] = small.reshape(device_count, -1, small.shape[1])
    small_step = functools.partial(sum_step, SMALL, hops=small_hops, sent_as=wide)

    live[ATTN] = [grad_attn, core(grad_attn), swap(grad_attn, ACROSS)]
    sync()
    live[ATTN] = live[ATTN] + [core(live[ATTN][2])]
    small_step(0)
    sync()

    grad_attn_all = jnp.concatenate(live.pop(ATTN), axis=0)
    live[MIXED] = swap(reduced(M, last), nxt)
    reduce_near(M, far_plane)
    reduce_far(M, nxt)
    reduce_far(M, own)
    small_step(1)
    live[OUT, FULL] = jnp.einsum(
        "lh,ld->hd", live[HEADS], grad_attn_all, preferred_element_type=wide
    )
    grad_heads = (
        jnp.einsum("ld,hd->lh", grad_attn_all, w_out, preferred_element_type=wide)
        .astype(narrow)
        .reshape(seq_length, local_heads, HD)
    )
    probability = jnp.exp(masked_scores() - live[TOTALS])
    grad_values = jnp.einsum(
        "hqk,qhd->khd", probability.astype(narrow), grad_heads, preferred_element_type=wide
    )
    grad_prob = jnp.einsum("qhd,khd->hqk", grad_heads, live[VALUES], preferred_element_type=wide)
    row_delta = jnp.sum(probability * grad_prob, axis=-1, keepdims=True)
    grad_scores = (probability * (grad_prob - row_delta)).astype(narrow)
    grad_query = score_scale * jnp.einsum(
        "hqk,khd->qhd", grad_scores, live[KEYS], preferred_element_type=wide
    )
    grad_keys = score_scale * jnp.einsum(
        "hqk,qhd->khd", grad_scores, live[QUERIES], preferred_element_type=wide
    )

    def flat(source):
        return source.astype(narrow).reshape(seq_length, local_heads * HD)

    live[RAW] = [
        flat(rotate(grad_query, cosine_table, -sine_table)),
        flat(rotate(grad_keys, cosine_table, -sine_table)),
        flat(grad_values),
    ]
    sync()

    def back(grad_raw, weights):
        return jnp.einsum("lh,dh->ld", grad_raw, weights, preferred_element_type=wide)

    raw = live.pop(RAW)
    split_quarters(back(raw[0], w_query) + back(raw[1], w_key) + back(raw[2], w_value))
    live[IN, FULL] = jnp.einsum(
        "ld,lh->dh", hidden_one, jnp.concatenate(raw, axis=1), preferred_element_type=wide
    )
    sum_step(OUT, 0)
    live[MIXED] = swap(add(reduced(M, far_plane), live[MIXED]), far_plane)
    reduce_near(M, nxt)
    reduce_near(M, own)
    small_step(2)
    sync()

    live[SENT] = core(live[SENT])
    sum_step(IN, 0)
    sum_step(OUT, 1)
    small_step(3)
    live[SIDE] = reduced(M, nxt)
    live[HOME] = reduced(M, own)
    sync()

    cross_quarters()
    sum_step(IN, 1)
    sum_step(OUT, 2)
    small_step(4)
    sync()

    grad_normed_one, grad_gain_attn = norm_backward(
        own_inputs, own_inverse, gain_attn, quarter_sum()
    )
    live[TOKENS] = grad_middle + grad_normed_one
    live[GAIN] = [grad_gain_attn[None], jnp.zeros_like(grad_gain_attn)[None]]

    def gain_step(step):
        live[GAIN] = [live[GAIN][0] + live[GAIN][1]]
        live[GAIN] = live[GAIN] + [swap(live[GAIN][0], *small_hops[step])]

    sum_step(IN, 2)
    sum_step(OUT, 3)
    live[SIDE] = swap(live[SIDE], nxt)
    small_step(5)
    gain_step(0)
    sync()

    sum_step(IN, 3)
    sum_step(OUT, 4)
    small_step(6)
    small_step(7)
    gain_step(1)
    sync()

    sum_step(IN, 4)
    sum_step(OUT, 5)
    small_step(8)
    gain_step(2)
    gain_step(3)
    sync()

    grad_w_out = summed(OUT)
    sum_step(IN, 5)
    mixed_out = live[HOME].astype(wide) + live[MIXED].astype(wide) + live[SIDE].astype(wide)
    mixed_out = (middle + mixed_out).astype(narrow)
    small_step(9)
    gain_step(4)
    sync()
    grad_gain_attn = (live[GAIN][0] + live[GAIN][1])[0]
    small = summed(SMALL, small_hops).reshape(model_width, -1)
    grad_w_in = summed(IN)
    columns = local_heads * HD

    return (
        mixed_out,
        live[TOKENS],
        grad_gain_attn,
        grad_w_in[:, :columns],
        grad_w_in[:, columns : 2 * columns],
        grad_w_in[:, 2 * columns :],
        grad_w_out,
        small[:, expert_count],
        small[:, :expert_count],
        *live[EXPERTS],
    )


def on_device(*operands):
    tokens, w_router, w_gate, expert_ids = operands[0], operands[7], operands[8], operands[11]
    owners, quarters = lax.axis_size("expert"), lax.axis_size("tensor")
    block_len, top_count = expert_ids.shape
    capacity = 3 * block_len * top_count // (2 * w_router.shape[1])
    buffer_rows = capacity * quarters * owners * w_gate.shape[0]
    gathers = owners * tokens.shape[0] <= buffer_rows and (owners, quarters) == (8, 4)
    return (gathered_layer if gathers else routed_layer)(*operands)


def solution(mesh):
    return jax.shard_map(
        on_device,
        mesh=mesh,
        in_specs=(
            P("expert", None),
            P(),
            P(None, "tensor"),
            P(None, "tensor"),
            P(None, "tensor"),
            P("tensor", None),
            P(),
            P(),
            P("expert", None, "tensor"),
            P("expert", None, "tensor"),
            P("expert", "tensor", None),
            P(("expert", "tensor"), None),
            P(("expert", "tensor"), None),
        ),
        out_specs=(
            P(("expert", "tensor"), None),
            P(("expert", "tensor"), None),
            P(),
            P(None, "tensor"),
            P(None, "tensor"),
            P(None, "tensor"),
            P("tensor", None),
            P(),
            P(),
            P("expert", None, "tensor"),
            P("expert", None, "tensor"),
            P("expert", "tensor", None),
        ),
        check_vma=False,
    )
```

profile of v0, /device:TPU:0, one launch (start us, length us, event | category | flops | bytes accessed | tf_op | source)
XLA Modules:
  0.0 769.9 jit_solution(5621905273623569713)
XLA Ops:
  23.1 9.7 %collective-permute-done.1 = bf16[128,2176]{1,0:T(8,128)(2,1)} collective-permute-done((bf16[128,2176]{1,0:T(8,128)(2,1)S(1)}, bf16[128,2176]{1,0:T(8,128)(2,1)}, u32[]{:S(2)}, u32[]{:S(2)}) %collective-permute-start.1) | collective-permute-done | bytes 557088 | tf_op jit(solution)/shard_map/ppermute | solution.py:691
  43.8 8.4 %collective-permute-done.4.refs_8_ = bf16[128,2176]{1,0:T(8,128)(2,1)S(1)} collective-permute-done((bf16[128,2176]{1,0:T(8,128)(2,1)}, bf16[128,2176]{1,0:T(8,128)(2,1)S(1)}, u32[]{:S(2)}, u32[]{:S(2)}) %collective-permute-start.4) | collective-permute-done | bytes 557088 | tf_op jit(solution)/shard_map/ppermute | solution.py:691
  52.2 8.3 %collective-permute-done.7 = bf16[128,2176]{1,0:T(8,128)(2,1)S(1)} collective-permute-done((bf16[128,2176]{1,0:T(8,128)(2,1)S(1)}, bf16[128,2176]{1,0:T(8,128)(2,1)S(1)}, u32[]{:S(2)}, u32[]{:S(2)}) %collective-permute-start.7) | collective-permute-done | bytes 557088 | tf_op jit(solution)/shard_map/ppermute | solution.py:691
  63.8 9.0 %collective-permute-done.9.refs_8_ = bf16[128,2176]{1,0:T(8,128)(2,1)S(1)} collective-permute-done((bf16[128,2176]{1,0:T(8,128)(2,1)S(1)}, bf16[128,2176]{1,0:T(8,128)(2,1)S(1)}, u32[]{:S(2)}, u32[]{:S(2)}) %collective-permute-start.9) | collective-permute-done | bytes 557088 | tf_op jit(solution)/shard_map/ppermute | solution.py:691
  82.0 9.1 %collective-permute-done.11 = bf16[128,2048]{1,0:T(8,128)(2,1)} collective-permute-done((bf16[128,2048]{1,0:T(8,128)(2,1)}, bf16[128,2048]{1,0:T(8,128)(2,1)}, u32[]{:S(2)}, u32[]{:S(2)}) %collective-permute-start.11) | collective-permute-done | bytes 524320 | tf_op jit(solution)/shard_map/ppermute | solution.py:691
  96.8 11.0 %collective-permute-done.13.refs_1_ = bf16[128,2048]{1,0:T(8,128)(2,1)S(1)} collective-permute-done((bf16[128,2048]{1,0:T(8,128)(2,1)S(1)}, bf16[128,2048]{1,0:T(8,128)(2,1)S(1)}, u32[]{:S(2)}, u32[]{:S(2)}) %collective-permute-start.13) | collective-permute-done | bytes 524320 | tf_op jit(solution)/shard_map/ppermute | solution.py:691
  114.9 8.6 %collective-permute-done.16.refs_3_ = bf16[128,2048]{1,0:T(8,128)(2,1)S(1)} collective-permute-done((bf16[128,2048]{1,0:T(8,128)(2,1)S(1)}, bf16[128,2048]{1,0:T(8,128)(2,1)S(1)}, u32[]{:S(2)}, u32[]{:S(2)}) %collective-permute-start.16) | collective-permute-done | bytes 524320 | tf_op jit(solution)/shard_map/ppermute | solution.py:691
  149.6 30.3 %shard_map.220 = (bf16[512,2048]{1,0:T(8,128)(2,1)}, bf16[512,2048]{1,0:T(8,128)(2,1)}, bf16[512,2048]{1,0:T(8,128)(2,1)}, bf16[512,2048]{1,0:T(8,128)(2,1)}, f3...) custom-call(bf16[128,2048]{1,0:T(8,128)(2,1)} %copy-done.14, ...), custom_call_target="tpu_custom_call" | custom-call | flops 19327352832 | bytes 37748736 | tf_op jit(solution)/shard_map/pallas_call | solution.py:576
  188.5 30.0 %shard_map.221 = (bf16[512,2048]{1,0:T(8,128)(2,1)}, bf16[512,2048]{1,0:T(8,128)(2,1)}, bf16[512,2048]{1,0:T(8,128)(2,1)}, bf16[512,2048]{1,0:T(8,128)(2,1)}, f3...) custom-call(bf16[128,2048]{1,0:T(8,128)(2,1)} %copy-done.78, ...), custom_call_target="tpu_custom_call" | custom-call | flops 19327352832 | bytes 37748736 | tf_op jit(solution)/shard_map/pallas_call | solution.py:576
  235.6 30.0 %shard_map.222 = (bf16[512,2048]{1,0:T(8,128)(2,1)}, bf16[512,2048]{1,0:T(8,128)(2,1)}, bf16[512,2048]{1,0:T(8,128)(2,1)}, bf16[512,2048]{1,0:T(8,128)(2,1)}, f3...) custom-call(bf16[128,4224]{1,0:T(8,128)(2,1)} %copy-done.19, ...), custom_call_target="tpu_custom_call" | custom-call | flops 19327352832 | bytes 37748736 | tf_op jit(solution)/shard_map/pallas_call | solution.py:576
  283.1 30.2 %shard_map.223 = (bf16[512,2048]{1,0:T(8,128)(2,1)}, bf16[512,2048]{1,0:T(8,128)(2,1)}, bf16[512,2048]{1,0:T(8,128)(2,1)}, bf16[512,2048]{1,0:T(8,128)(2,1)}, f3...) custom-call(bf16[128,4224]{1,0:T(8,128)(2,1)} %copy-done.26, ...), custom_call_target="tpu_custom_call" | custom-call | flops 19327352832 | bytes 37748736 | tf_op jit(solution)/shard_map/pallas_call | solution.py:576
  335.8 11.2 %shard_map.224 = (f32[8,2048,256]{2,1,0:T(8,128)}, f32[8,2048,256]{2,1,0:T(8,128)}, f32[8,256,2048]{2,1,0:T(8,128)}) custom-call(bf16[8,192,2048]{2,1,0:T(8,128)(2,1)} %get-tuple-element.1210.refs_0_, bf16[8,192,2048]{2,1,0:T(8,128)(2,1)} %get-tuple-element.1215.refs_1_, bf16[8,192,2048]{2,1,0:T(8,128)(2,1)} %get-tuple-element.1225.refs_2_, ...), custom_call_target="tpu_custom_call" | custom-call | flops 4831838208 | bytes 27525120 | tf_op jit(solution)/shard_map/pallas_call | solution.py:638
  347.0 11.5 %shard_map.225 = (f32[8,2048,256]{2,1,0:T(8,128)}, f32[8,2048,256]{2,1,0:T(8,128)}, f32[8,256,2048]{2,1,0:T(8,128)}) custom-call(bf16[8,192,2048]{2,1,0:T(8,128)(2,1)} %get-tuple-element.1210.refs_0_, bf16[8,192,2048]{2,1,0:T(8,128)(2,1)} %get-tuple-element.1215.refs_1_, ...), custom_call_target="tpu_custom_call", output_to_operand_aliasing={{0}: (16, {}), {1}: (17, {}), {2}: (18, {})} | custom-call | flops 4831838208 | bytes 27525120 | tf_op jit(solution)/shard_map/pallas_call | solution.py:638
  369.5 11.2 %shard_map.226 = (f32[8,2048,256]{2,1,0:T(8,128)}, f32[8,2048,256]{2,1,0:T(8,128)}, f32[8,256,2048]{2,1,0:T(8,128)}) custom-call(bf16[8,192,2048]{2,1,0:T(8,128)(2,1)} %get-tuple-element.1210.refs_0_, bf16[8,192,2048]{2,1,0:T(8,128)(2,1)} %get-tuple-element.1215.refs_1_, ...), custom_call_target="tpu_custom_call", output_to_operand_aliasing={{0}: (16, {}), {1}: (17, {}), {2}: (18, {})} | custom-call | flops 4831838208 | bytes 27525120 | tf_op jit(solution)/shard_map/pallas_call | solution.py:638
  400.8 11.3 %shard_map.227 = (f32[8,2048,256]{2,1,0:T(8,128)}, f32[8,2048,256]{2,1,0:T(8,128)}, f32[8,256,2048]{2,1,0:T(8,128)}) custom-call(bf16[8,192,2048]{2,1,0:T(8,128)(2,1)} %get-tuple-element.1210.refs_0_, bf16[8,192,2048]{2,1,0:T(8,128)(2,1)} %get-tuple-element.1215.refs_1_, ...), custom_call_target="tpu_custom_call", output_to_operand_aliasing={{0}: (16, {}), {1}: (17, {}), {2}: (18, {})} | custom-call | flops 4831838208 | bytes 27525120 | tf_op jit(solution)/shard_map/pallas_call | solution.py:638
  425.8 9.3 %collective-permute-done.63 = bf16[128,2048]{1,0:T(8,128)(2,1)} collective-permute-done((bf16[128,2048]{1,0:T(8,128)(2,1)}, bf16[128,2048]{1,0:T(8,128)(2,1)}, u32[]{:S(2)}, u32[]{:S(2)}) %collective-permute-start.63) | collective-permute-done | bytes 524320 | tf_op jit(solution)/shard_map/ppermute | solution.py:691
  502.4 11.2 %collective-permute-done.75 = f32[4,64,65]{2,1,0:T(8,128)S(1)} collective-permute-done((f32[4,64,65]{2,1,0:T(8,128)S(1)}, f32[4,64,65]{2,1,0:T(8,128)S(1)}, u32[]{:S(2)}, u32[]{:S(2)}) %collective-permute-start.75) | collective-permute-done | bytes 66592 | tf_op jit(solution)/shard_map/ppermute | solution.py:691
  533.6 10.5 %collective-permute-done.79 = f32[2,64,65]{2,1,0:T(8,128)S(1)} collective-permute-done((f32[2,64,65]{2,1,0:T(8,128)S(1)}, f32[2,64,65]{2,1,0:T(8,128)S(1)}, u32[]{:S(2)}, u32[]{:S(2)}) %collective-permute-start.79) | collective-permute-done | bytes 33312 | tf_op jit(solution)/shard_map/ppermute | solution.py:691
  544.1 15.9 %collective-permute-done.77 = bf16[1024,1536]{1,0:T(8,128)(2,1)} collective-permute-done((bf16[1024,1536]{1,0:T(8,128)(2,1)}, bf16[1024,1536]{1,0:T(8,128)(2,1)}, u32[]{:S(2)}, u32[]{:S(2)}) %collective-permute-start.77) | collective-permute-done | bytes 3145760 | tf_op jit(solution)/shard_map/ppermute | solution.py:691
  569.9 19.9 %collective-permute-done.83 = f32[1,64,65]{2,1,0:T(8,128)S(1)} collective-permute-done((f32[1,64,65]{2,1,0:T(8,128)S(1)}, f32[1,64,65]{2,1,0:T(8,128)S(1)}, u32[]{:S(2)}, u32[]{:S(2)}) %collective-permute-start.83) | collective-permute-done | bytes 16672 | tf_op jit(solution)/shard_map/ppermute | solution.py:691
  599.6 44.7 %collective-permute-done.88 = f32[1,64,65]{2,1,0:T(8,128)S(1)} collective-permute-done((f32[1,64,65]{2,1,0:T(8,128)S(1)}, f32[1,64,65]{2,1,0:T(8,128)S(1)}, u32[]{:S(2)}, u32[]{:S(2)}) %collective-permute-start.88) | collective-permute-done | bytes 16672 | tf_op jit(solution)/shard_map/ppermute | solution.py:691
  647.4 20.7 %collective-permute-done.92 = f32[2,64,65]{2,1,0:T(8,128)S(1)} collective-permute-done((f32[2,64,65]{2,1,0:T(8,128)S(1)}, f32[2,64,65]{2,1,0:T(8,128)S(1)}, u32[]{:S(2)}, u32[]{:S(2)}) %collective-permute-start.92) | collective-permute-done | bytes 33312 | tf_op jit(solution)/shard_map/ppermute | solution.py:691
  685.0 22.1 %collective-permute-done.94 = f32[1,2048]{1,0:T(1,128)S(1)} collective-permute-done((f32[1,2048]{1,0:T(1,128)S(1)}, f32[1,2048]{1,0:T(1,128)S(1)}, u32[]{:S(2)}, u32[]{:S(2)}) %collective-permute-start.94) | collective-permute-done | bytes 8224 | tf_op jit(solution)/shard_map/ppermute | solution.py:691
  723.0 27.3 %collective-permute-done.100 = bf16[1024,1536]{1,0:T(8,128)(2,1)} collective-permute-done((bf16[1024,1536]{1,0:T(8,128)(2,1)S(1)}, bf16[1024,1536]{1,0:T(8,128)(2,1)}, u32[]{:S(2)}, u32[]{:S(2)}) %collective-permute-start.100) | collective-permute-done | bytes 3145760 | tf_op jit(solution)/shard_map/ppermute | solution.py:691
  (615 shorter events, 355.1 us)
Async XLA Ops:
  140.4 39.6 %collective-permute-start.22 = (bf16[512,2048]{1,0:T(8,128)(2,1)}, bf16[512,2048]{1,0:T(8,128)(2,1)}, u32[]{:S(2)}, u32[]{:S(2)}) collective-permute-start(bf16[512,2048]{1,0:T(8,128)(2,1)} %pad_maximum_fusion.6), channel_id=1, source_target_pairs={{0,1},{1,0},{2,3},{3,2},{4,5},{5,4},{6,7},{7,6},{8,9},{9,8},{10,11... | collective-permute-start | bytes 6291464 | tf_op jit(solution)/shard_map/ppermute | solution.py:691
  140.4 39.6 %collective-permute-start.23 = (bf16[128,4224]{1,0:T(8,128)(2,1)S(1)}, bf16[128,4224]{1,0:T(8,128)(2,1)}, u32[]{:S(2)}, u32[]{:S(2)}) collective-permute-start(bf16[128,4224]{1,0:T(8,128)(2,1)S(1)} %pad_maximum_fusion.7.refs_0_), channel_id=1, source_target_pairs={{0,2},{1,5},{2,0},{3,7},{4,6},{5,1},{6,4},{7,3},{8,10},{9,13},{10,... | collective-permute-start | bytes 3244040 | tf_op jit(solution)/shard_map/ppermute | solution.py:691
  140.9 39.0 %collective-permute-start.24 = (bf16[128,4224]{1,0:T(8,128)(2,1)S(1)}, bf16[128,4224]{1,0:T(8,128)(2,1)}, u32[]{:S(2)}, u32[]{:S(2)}) collective-permute-start(bf16[128,4224]{1,0:T(8,128)(2,1)S(1)} %pad_maximum_fusion.7.refs_0_), channel_id=1, source_target_pairs={{0,4},{1,3},{2,6},{3,1},{4,0},{5,7},{6,2},{7,5},{8,12},{9,11},{10,... | collective-permute-start | bytes 3244040 | tf_op jit(solution)/shard_map/ppermute | solution.py:691
  142.6 37.3 %collective-permute-start.25 = (bf16[128,2048]{1,0:T(8,128)(2,1)S(1)}, bf16[128,2048]{1,0:T(8,128)(2,1)}, u32[]{:S(2)}, u32[]{:S(2)}) collective-permute-start(bf16[128,2048]{1,0:T(8,128)(2,1)S(1)} %multiply_convert_fusion.2.refs_0_), channel_id=1, source_target_pairs={{0,16},{1,17},{2,18},{3,19},{4,20},{5,21},{6,22},{7,23},{8,24},{9,... | collective-permute-start | bytes 1572872 | tf_op jit(solution)/shard_map/ppermute | solution.py:691
  183.5 38.6 %collective-permute-start.27 = (bf16[384,4224]{1,0:T(8,128)(2,1)}, bf16[384,4224]{1,0:T(8,128)(2,1)}, u32[]{:S(2)}, u32[]{:S(2)}) collective-permute-start(bf16[384,4224]{1,0:T(8,128)(2,1)} %pad_maximum_fusion), channel_id=1, source_target_pairs={{0,1},{1,0},{2,3},{3,2},{4,5},{5,4},{6,7},{7,6},{8,9},{9,8},{10,11... | collective-permute-start | bytes 9732104 | tf_op jit(solution)/shard_map/ppermute | solution.py:691
  183.5 35.0 %collective-permute-start.26 = (bf16[128,4224]{1,0:T(8,128)(2,1)}, bf16[128,4224]{1,0:T(8,128)(2,1)}, u32[]{:S(2)}, u32[]{:S(2)}) collective-permute-start(bf16[128,4224]{1,0:T(8,128)(2,1)} %collective-permute-done.23.refs_1_), channel_id=1, source_target_pairs={{0,4},{1,3},{2,6},{3,1},{4,0},{5,7},{6,2},{7,5},{8,12},{9,11},{10,... | collective-permute-start | bytes 3244040 | tf_op jit(solution)/shard_map/ppermute | solution.py:691
  185.0 37.1 %collective-permute-start.30 = (bf16[512,2048]{1,0:T(8,128)(2,1)}, bf16[512,2048]{1,0:T(8,128)(2,1)}, u32[]{:S(2)}, u32[]{:S(2)}) collective-permute-start(bf16[512,2048]{1,0:T(8,128)(2,1)} %get-tuple-element.890), channel_id=1, source_target_pairs={{0,1},{1,0},{2,3},{3,2},{4,5},{5,4},{6,7},{7,6},{8,9},{9,8},{10,11... | collective-permute-start | bytes 6291464 | tf_op jit(solution)/shard_map/ppermute | solution.py:691
  187.7 34.4 %collective-permute-start.29 = (bf16[128,4224]{1,0:T(8,128)(2,1)S(1)}, bf16[128,4224]{1,0:T(8,128)(2,1)}, u32[]{:S(2)}, u32[]{:S(2)}) collective-permute-start(bf16[128,4224]{1,0:T(8,128)(2,1)S(1)} %constant_dynamic-update-slice_fusion.refs_0_), channel_id=1, source_target_pairs={{0,4},{1,3},{2,6},{3,1},{4,0},{5,7},{6,2},{7,5},{8,12},{9,11},{10,... | collective-permute-start | bytes 3244040 | tf_op jit(solution)/shard_map/ppermute | solution.py:691
  229.0 36.7 %collective-permute-start.33 = (bf16[384,4224]{1,0:T(8,128)(2,1)}, bf16[384,4224]{1,0:T(8,128)(2,1)}, u32[]{:S(2)}, u32[]{:S(2)}) collective-permute-start(bf16[384,4224]{1,0:T(8,128)(2,1)} %pad_maximum_fusion.1), channel_id=1, source_target_pairs={{0,1},{1,0},{2,3},{3,2},{4,5},{5,4},{6,7},{7,6},{8,9},{9,8},{10,11... | collective-permute-start | bytes 9732104 | tf_op jit(solution)/shard_map/ppermute | solution.py:691
  229.2 36.5 %collective-permute-start.32 = (bf16[128,4224]{1,0:T(8,128)(2,1)}, bf16[128,4224]{1,0:T(8,128)(2,1)}, u32[]{:S(2)}, u32[]{:S(2)}) collective-permute-start(bf16[128,4224]{1,0:T(8,128)(2,1)} %collective-permute-done.28.refs_1_), channel_id=1, source_target_pairs={{0,4},{1,3},{2,6},{3,1},{4,0},{5,7},{6,2},{7,5},{8,12},{9,11},{10,... | collective-permute-start | bytes 3244040 | tf_op jit(solution)/shard_map/ppermute | solution.py:691
  230.7 35.0 %collective-permute-start.35 = (bf16[512,2048]{1,0:T(8,128)(2,1)}, bf16[512,2048]{1,0:T(8,128)(2,1)}, u32[]{:S(2)}, u32[]{:S(2)}) collective-permute-start(bf16[512,2048]{1,0:T(8,128)(2,1)} %get-tuple-element.969), channel_id=1, source_target_pairs={{0,1},{1,0},{2,3},{3,2},{4,5},{5,4},{6,7},{7,6},{8,9},{9,8},{10,11... | collective-permute-start | bytes 6291464 | tf_op jit(solution)/shard_map/ppermute | solution.py:691
  230.7 34.9 %collective-permute-start.36 = (bf16[512,2048]{1,0:T(8,128)(2,1)}, bf16[512,2048]{1,0:T(8,128)(2,1)}, u32[]{:S(2)}, u32[]{:S(2)}) collective-permute-start(bf16[512,2048]{1,0:T(8,128)(2,1)} %get-tuple-element.970), channel_id=1, source_target_pairs={{0,1},{1,0},{2,3},{3,2},{4,5},{5,4},{6,7},{7,6},{8,9},{9,8},{10,11... | collective-permute-start | bytes 6291464 | tf_op jit(solution)/shard_map/ppermute | solution.py:691
  274.6 38.7 %collective-permute-start.39 = (bf16[128,2048]{1,0:T(8,128)(2,1)}, bf16[128,2048]{1,0:T(8,128)(2,1)}, u32[]{:S(2)}, u32[]{:S(2)}) collective-permute-start(bf16[128,2048]{1,0:T(8,128)(2,1)} %get-tuple-element.1482), channel_id=1, source_target_pairs={{0,2},{1,5},{2,0},{3,7},{4,6},{5,1},{6,4},{7,3},{8,10},{9,13},{10,... | collective-permute-start | bytes 1572872 | tf_op jit(solution)/shard_map/ppermute | solution.py:691
  278.9 34.4 %collective-permute-start.40 = (bf16[2,128,2048]{2,1,0:T(8,128)(2,1)}, bf16[2,128,2048]{2,1,0:T(8,128)(2,1)}, u32[]{:S(2)}, u32[]{:S(2)}) collective-permute-start(bf16[2,128,2048]{2,1,0:T(8,128)(2,1)} %bitcast.24), channel_id=1, source_target_pairs={{0,4},{1,3},{2,6},{3,1},{4,0},{5,7},{6,2},{7,5},{8,12},{9,11},{10,... | collective-permute-start | bytes 3145736 | tf_op jit(solution)/shard_map/ppermute | solution.py:691
  321.1 37.4 %collective-permute-start.46 = (f32[4,2,8,128]{3,2,0,1:T(8,128)S(1)}, f32[4,2,8,128]{3,2,0,1:T(8,128)S(1)}, u32[]{:S(2)}, u32[]{:S(2)}) collective-permute-start(f32[4,2,8,128]{3,2,0,1:T(8,128)S(1)} %get-tuple-element.1518), channel_id=1, source_target_pairs={{0,2},{1,3},{2,0},{3,1},{4,6},{5,7},{6,4},{7,5},{8,10},{9,11},{10,... | collective-permute-start | bytes 98312 | tf_op jit(solution)/shard_map/ppermute | solution.py:691
  325.2 33.2 %collective-permute-start.47 = (bf16[128,2048]{1,0:T(8,128)(2,1)}, bf16[128,2048]{1,0:T(8,128)(2,1)}, u32[]{:S(2)}, u32[]{:S(2)}) collective-permute-start(bf16[128,2048]{1,0:T(8,128)(2,1)} %get-tuple-element.1480), channel_id=1, source_target_pairs={{0,2},{1,5},{2,0},{3,7},{4,6},{5,1},{6,4},{7,3},{8,10},{9,13},{10,... | collective-permute-start | bytes 1572872 | tf_op jit(solution)/shard_map/ppermute | solution.py:691
  475.5 38.2 %collective-permute-start.71 = (bf16[128,2048]{1,0:T(8,128)(2,1)}, bf16[128,2048]{1,0:T(8,128)(2,1)}, u32[]{:S(2)}, u32[]{:S(2)}) collective-permute-start(bf16[128,2048]{1,0:T(8,128)(2,1)} %add_convert_fusion.24), channel_id=1, source_target_pairs={{0,16},{1,17},{2,18},{3,19},{4,20},{5,21},{6,22},{7,23},{8,24},{9,... | collective-permute-start | bytes 1572872 | tf_op jit(solution)/shard_map/ppermute | solution.py:691
  516.0 44.0 %collective-permute-start.77 = (bf16[1024,1536]{1,0:T(8,128)(2,1)}, bf16[1024,1536]{1,0:T(8,128)(2,1)}, u32[]{:S(2)}, u32[]{:S(2)}) collective-permute-start(bf16[1024,1536]{1,0:T(8,128)(2,1)} %dynamic-slice_convert_fusion), channel_id=1, source_target_pairs={{0,4},{1,9},{2,6},{3,11},{4,0},{5,13},{6,2},{7,15},{8,12},{9,1},{1... | collective-permute-start | bytes 9437192 | tf_op jit(solution)/shard_map/ppermute | solution.py:691
  590.6 53.8 %collective-permute-start.84 = (bf16[128,2048]{1,0:T(8,128)(2,1)S(1)}, bf16[128,2048]{1,0:T(8,128)(2,1)S(1)}, u32[]{:S(2)}, u32[]{:S(2)}) collective-permute-start(bf16[128,2048]{1,0:T(8,128)(2,1)S(1)} %add_convert_fusion.19), channel_id=1, source_target_pairs={{0,8},{1,9},{2,10},{3,11},{4,12},{5,13},{6,14},{7,15},{8,0},{9,1},... | collective-permute-start | bytes 1572872 | tf_op jit(solution)/shard_map/ppermute | solution.py:691
  594.4 50.0 %collective-permute-start.86 = (bf16[256,1536]{1,0:T(8,128)(2,1)S(1)}, bf16[256,1536]{1,0:T(8,128)(2,1)S(1)}, u32[]{:S(2)}, u32[]{:S(2)}) collective-permute-start(bf16[256,1536]{1,0:T(8,128)(2,1)S(1)} %dynamic-slice_convert_fusion.3), channel_id=1, source_target_pairs={{0,16},{1,17},{2,18},{3,19},{4,20},{5,21},{6,22},{7,23},{8,24},{9,... | collective-permute-start | bytes 2359304 | tf_op jit(solution)/shard_map/ppermute | solution.py:691
  595.1 49.2 %collective-permute-start.87 = (bf16[64,2048]{1,0:T(8,128)(2,1)S(1)}, bf16[64,2048]{1,0:T(8,128)(2,1)S(1)}, u32[]{:S(2)}, u32[]{:S(2)}) collective-permute-start(bf16[64,2048]{1,0:T(8,128)(2,1)S(1)} %add_convert_fusion.44), channel_id=1, source_target_pairs={{0,16},{1,17},{2,18},{3,19},{4,20},{5,21},{6,22},{7,23},{8,24},{9,... | collective-permute-start | bytes 786440 | tf_op jit(solution)/shard_map/ppermute | solution.py:691
  597.5 46.9 %collective-permute-start.88 = (f32[1,64,65]{2,1,0:T(8,128)S(1)}, f32[1,64,65]{2,1,0:T(8,128)S(1)}, u32[]{:S(2)}, u32[]{:S(2)}) collective-permute-start(f32[1,64,65]{2,1,0:T(8,128)S(1)} %add.547), channel_id=1, source_target_pairs={{0,16},{1,17},{2,18},{3,19},{4,20},{5,21},{6,22},{7,23},{8,24},{9,... | collective-permute-start | bytes 49928 | tf_op jit(solution)/shard_map/ppermute | solution.py:691
  644.6 35.6 %collective-permute-start.90 = (bf16[256,1536]{1,0:T(8,128)(2,1)S(1)}, bf16[256,1536]{1,0:T(8,128)(2,1)S(1)}, u32[]{:S(2)}, u32[]{:S(2)}) collective-permute-start(bf16[256,1536]{1,0:T(8,128)(2,1)S(1)} %add_convert_fusion.16), channel_id=1, source_target_pairs={{0,16},{1,17},{2,18},{3,19},{4,20},{5,21},{6,22},{7,23},{8,24},{9,... | collective-permute-start | bytes 2359304 | tf_op jit(solution)/shard_map/ppermute | solution.py:691
  712.9 37.4 %collective-permute-start.100 = (bf16[1024,1536]{1,0:T(8,128)(2,1)S(1)}, bf16[1024,1536]{1,0:T(8,128)(2,1)}, u32[]{:S(2)}, u32[]{:S(2)}) collective-permute-start(bf16[1024,1536]{1,0:T(8,128)(2,1)S(1)} %constant_dynamic-update-slice_fusion.26), channel_id=1, source_target_pairs={{0,4},{1,9},{2,6},{3,11},{4,0},{5,13},{6,2},{7,15},{8,12},{9,1},{1... | collective-permute-start | bytes 9437192 | tf_op jit(solution)/shard_map/ppermute | solution.py:691
  (185 other events, 2527.5 us)
where the time goes:
time: 781 us; the launch traced here: 770 us
  waiting for transfers between devices  305 us (39%)
  Pallas kernels  166 us (21%)
  starting transfers between devices  113 us (14%)
  other arithmetic  97.8 us (13%)
  local copies, waits for them, and re-layouts  54 us (7%)
  matrix products  31.1 us (4%)
    ppermute x102, waiting for transfers between devices, swap(): return lax.ppermute(value, BOTH, perm)  305 us
    pallas_call x4, Pallas kernels, expert_chunk(): pl.pallas_call(functools.partial(expert_kernel, places, top_count), in_sp...  121 us
    ppermute x102, starting transfers between devices, swap(): return lax.ppermute(value, BOTH, perm)  113 us
    convert_element_type x24, other arithmetic, add(): return (left.astype(wide) + right.astype(wide)).astype(narrow)  47.9 us
    pallas_call x4, Pallas kernels, weight_grads(): pl.pallas_call(functools.partial(weight_kernel, parts, len(partial)), gri...  45.2 us
  transfers between devices with their start and end apart: 102, of which 34 were waited for; matrix products, arithmetic and copies ran while one was open for 16% of the time, Pallas kernels for 22%

commit v1 on v0

--- a/solution.py
+++ b/solution.py
@@ -740,15 +740,19 @@
         live[name, plane, OTHER] = core(live.pop((name, plane, AWAY)))
 
     def reduce_far(name, plane):
+        kept = live[name, plane, NEAR].reshape(4, block_len, model_width)
+        got = live[name, plane, OTHER].reshape(4, block_len, model_width)
+        live[name, plane, FAR] = far(add(kept[2:], got[2:]))
+
+    def reduce_near(name, plane):
         kept = live.pop((name, plane, NEAR)).reshape(4, block_len, model_width)
         got = live.pop((name, plane, OTHER)).reshape(4, block_len, model_width)
-        live[name, plane, SUMS] = add(kept[:2], got[:2])
-        live[name, plane, FAR] = far(add(kept[2:], got[2:]))
-
-    def reduce_near(name, plane):
-        sums, got = live.pop((name, plane, SUMS)), live.pop((name, plane, FAR))
-        live[name, plane, OWN] = add(sums[0], got[0])
-        live[name, plane, SIDE] = near(add(sums[1], got[1]))
+        back = live.pop((name, plane, FAR))
+        sums = [
+            kept[i].astype(wide) + got[i].astype(wide) + back[i].astype(wide) for i in range(2)
+        ]
+        live[name, plane, OWN] = sums[0].astype(narrow)
+        live[name, plane, SIDE] = near(sums[1].astype(narrow))
 
     def reduced(name, plane):
         return add(live.pop((name, plane, OWN)), live.pop((name, plane, SIDE)))
@@ -795,18 +799,19 @@
 
     named_ids = jnp.pad(expert_ids.astype(narrow), ((0, 0), (0, LANES - top_count)))
     live[G, own, 0] = jnp.concatenate([cotangent, named_ids], axis=1)
+    half_block = block_len // 2
     live[G, nxt, 0] = swap(live[G, own, 0], nxt)
-    live[G, last, 0] = swap(live[G, own, 0], last)
+    live[G, far_plane, 0] = [swap(live[G, own, 0][:half_block], far_plane)]
     gather_near(G, own)
 
     by_block = tokens.reshape(quarters, block_len, model_width)
     inputs = jnp.concatenate(
         [lax.dynamic_slice_in_dim(by_block, quarter ^ r, 1, 0)[0] for r in range(quarters)], axis=0
     )
-    inputs = lax.optimization_barrier(inputs).astype(wide)
+    inputs = lax.optimization_barrier(inputs)
     order = quarter.astype(jnp.int32) ^ jnp.arange(quarters, dtype=jnp.int32)
     positions = (order[:, None] * block_len + jnp.arange(block_len, dtype=jnp.int32)).reshape(-1)
-    inverse_one, normed_one = norm_forward(inputs, gain_attn)
+    inverse_one, normed_one = norm_forward(inputs.astype(wide), gain_attn)
     hidden_one = normed_one.astype(narrow)
     frequency = jnp.exp(
         -jnp.log(theta_base) * jnp.arange(HD // 2, dtype=jnp.float32) * (2.0 / HD)
@@ -826,7 +831,9 @@
 
     gather_far(G, own)
     gather_near(G, nxt)
-    live[G, far_plane, 0] = swap(live[G, own, 0], far_plane)
+    live[G, far_plane, 0] = live[G, far_plane, 0] + [
+        swap(live[G, own, 0][half_block:], far_plane)
+    ]
     allowed = positions[:, None] >= positions[None, :]
 
     def masked_scores():
@@ -854,7 +861,7 @@
 
     live[SENT] = core(live[SENT])
     gather_far(G, nxt)
-    gather_core(G, own, 0, 1, 2, 3)
+    live[G, far_plane, 0] = jnp.concatenate(live[G, far_plane, 0], axis=0)
     sync()
 
     def cross_quarters():
@@ -866,10 +873,10 @@
         return live.pop(KEPT) + live.pop(SENT).astype(wide)
 
     cross_quarters()
-    gather_core(G, nxt, 0, 1, 2, 3)
-    sync()
-
-    own_inputs = inputs[:block_len]
+    live[G, last, 0] = swap(live[G, far_plane, 0], nxt)
+    sync()
+
+    own_inputs = inputs[:block_len].astype(wide)
     own_inverse = inverse_one[:block_len]
     middle = own_inputs + quarter_sum()
     inverse_two, normed_two = norm_forward(middle, gain_moe)
@@ -878,6 +885,7 @@
 
     gather_near(H, own)
     live[H, nxt, 0] = swap(hidden_two, nxt)
+    gather_core(G, own, 0, 1, 2, 3)
     logits = jnp.dot(hidden_two, w_router, preferred_element_type=wide)
     expert_range = jnp.arange(expert_count, dtype=jnp.int32)
     matches = expert_ids[:, :, None] == expert_range[None, None, :]
@@ -890,13 +898,22 @@
 
     gather_far(H, own)
     gather_near(H, nxt)
-    live[H, last, 0] = swap(live[H, own, 0], last)
+    hidden_two = live[H, own, 0]
+    gather_core(G, nxt, 0, 1, 2, 3)
+    live[H, last, 0] = [swap(hidden_two[:half_block], last)]
     sync()
 
     gather_far(H, nxt)
     gather_core(H, own, 0, 1, 2, 3)
-    live[PAIR, last, 0] = jnp.concatenate([live.pop((H, last, 0)), live.pop((G, last, 0))], axis=1)
-    sync()
+    hidden_two = live[H, own, 0]
+    live[H, last, 0] = live[H, last, 0] + [swap(hidden_two[half_block:], last)]
+    sync()
+
+    def join_pair(plane):
+        rows, grads = [live.pop((name, plane, 0)) for name in (H, G)]
+        if isinstance(rows, list):
+            rows = jnp.concatenate(rows, axis=0)
+        live[PAIR, plane, 0] = jnp.concatenate([rows, grads], axis=1)
 
     def experts(plane):
         if (PAIR, plane, 0) in live:
@@ -930,18 +947,16 @@
         live[SUMS, plane] = done[4]
         live[KEPT, plane] = done[5:]
 
-    hidden_two_sent = live[H, own, 0]
     gather_core(H, nxt, 0, 1, 2, 3)
+    join_pair(last)
     gather_near(PAIR, last)
-    live[H, far_plane, 0] = swap(hidden_two_sent, far_plane)
+    live[H, far_plane, 0] = swap(live[H, own, 0], far_plane)
     experts(own)
     sync()
 
     gather_far(PAIR, last)
     gather_core(PAIR, last, 0, 1, 2)
-    live[PAIR, far_plane, 0] = jnp.concatenate(
-        [live.pop((H, far_plane, 0)), live.pop((G, far_plane, 0))], axis=1
-    )
+    join_pair(far_plane)
     gather_near(PAIR, far_plane)
     reduce_core(R, own)
     experts(nxt)
@@ -981,41 +996,36 @@
     reduce_core(M, last)
     sync()
 
+    reduce_far(R, far_plane)
     reduce_near(R, last)
     reduce_near(R, nxt)
-    reduce_far(R, far_plane)
     sums = live[GATES][0] + live[GATES][1]
     crossed = jnp.stack([sums[:, 0], sums[:, 2], sums[:, 1], sums[:, 3]], axis=1)
     sums = jnp.where(odd_core == 0, sums, crossed)
     live[GATES] = [sums[:, ::2], swap(sums[:, 1::2], ACROSS)]
-    live[HOME] = reduced(R, own)
-    some_weight_grads(0)
-    some_weight_grads(1)
     sync()
 
     live[RELAY] = swap(reduced(R, last), nxt)
     reduce_near(R, far_plane)
     sums = live[GATES][0] + live[GATES][1]
-    live[GATES] = [sums[:, 0], swap(sums[:, 1], ASIDE)]
+    sums = jnp.stack([sums[:, 0], swap(sums[:, 1], ASIDE)], axis=1)
+    live[GATES] = [sums[::2], swap(sums[1::2], nxt)]
     reduce_core(M, far_plane)
+    live[HOME] = reduced(R, own)
+    live[SIDE] = reduced(R, nxt)
+    sync()
+
+    live[RELAY] = swap(add(reduced(R, far_plane), live[RELAY]), far_plane)
+    live[SIDE] = swap(live[SIDE], nxt)
+    sums = jnp.stack(live[GATES], axis=1)
+    live[GATES] = [sums[0], swap(sums[1], far_plane)]
     reduce_far(M, last)
-    some_weight_grads(2)
-    sync()
-
-    live[RELAY] = swap(add(reduced(R, far_plane), live[RELAY]), far_plane)
-    live[SIDE] = swap(reduced(R, nxt), nxt)
-    sums = jnp.stack(live[GATES], axis=1)
-    live[GATES] = [sums[0]] + [swap(sums[i], PLANES[i]) for i in range(1, len(PLANES))]
-    reduce_near(M, last)
     reduce_far(M, far_plane)
-    some_weight_grads(3)
-    sync()
-    for plane in PLANES:
-        live.pop((KEPT, plane))
+    sync()
 
     grad_hidden_disp = live.pop(HOME).astype(wide) + live.pop(RELAY).astype(wide)
     grad_hidden_disp = grad_hidden_disp + live.pop(SIDE).astype(wide)
-    sums = jnp.concatenate(live.pop(GATES), axis=0)
+    sums = jnp.concatenate(live.pop(GATES), axis=0).reshape(-1, local_experts, block_len)
     owner = lax.axis_index("expert").astype(jnp.uint32)
     sums = [lax.dynamic_slice_in_dim(sums, owner ^ r, 1, 0)[0] for r in range(sums.shape[0])]
     own_sums = jnp.concatenate(sums, axis=0).T
@@ -1038,17 +1048,16 @@
     small_step = functools.partial(sum_step, SMALL, hops=small_hops, sent_as=wide)
 
     live[ATTN] = [grad_attn, core(grad_attn), swap(grad_attn, ACROSS)]
+    small_step(0)
     sync()
     live[ATTN] = live[ATTN] + [core(live[ATTN][2])]
-    small_step(0)
+    small_step(1)
     sync()
 
     grad_attn_all = jnp.concatenate(live.pop(ATTN), axis=0)
-    live[MIXED] = swap(reduced(M, last), nxt)
+    reduce_near(M, last)
     reduce_near(M, far_plane)
-    reduce_far(M, nxt)
-    reduce_far(M, own)
-    small_step(1)
+    small_step(2)
     live[OUT, FULL] = jnp.einsum(
         "lh,ld->hd", live[HEADS], grad_attn_all, preferred_element_type=wide
     )
@@ -1057,6 +1066,12 @@
         .astype(narrow)
         .reshape(seq_length, local_heads, HD)
     )
+    live[RAW] = grad_heads
+    sync()
+
+    grad_heads = live.pop(RAW)
+    live[MIXED] = swap(reduced(M, last), nxt)
+    reduce_far(M, nxt)
     probability = jnp.exp(masked_scores() - live[TOTALS])
     grad_values = jnp.einsum(
         "hqk,qhd->khd", probability.astype(narrow), grad_heads, preferred_element_type=wide
@@ -1090,24 +1105,24 @@
         "ld,lh->dh", hidden_one, jnp.concatenate(raw, axis=1), preferred_element_type=wide
     )
     sum_step(OUT, 0)
+    sum_step(OUT, 1)
     live[MIXED] = swap(add(reduced(M, far_plane), live[MIXED]), far_plane)
     reduce_near(M, nxt)
-    reduce_near(M, own)
-    small_step(2)
+    small_step(3)
     sync()
 
     live[SENT] = core(live[SENT])
     sum_step(IN, 0)
-    sum_step(OUT, 1)
-    small_step(3)
-    live[SIDE] = reduced(M, nxt)
-    live[HOME] = reduced(M, own)
+    sum_step(OUT, 2)
+    small_step(4)
+    some_weight_grads(0)
     sync()
 
     cross_quarters()
     sum_step(IN, 1)
-    sum_step(OUT, 2)
-    small_step(4)
+    sum_step(OUT, 3)
+    small_step(5)
+    some_weight_grads(1)
     sync()
 
     grad_normed_one, grad_gain_attn = norm_backward(
@@ -1121,46 +1136,58 @@
         live[GAIN] = live[GAIN] + [swap(live[GAIN][0], *small_hops[step])]
 
     sum_step(IN, 2)
-    sum_step(OUT, 3)
-    live[SIDE] = swap(live[SIDE], nxt)
-    small_step(5)
+    sum_step(OUT, 4)
+    reduce_far(M, own)
+    live[SIDE] = swap(reduced(M, nxt), nxt)
+    small_step(6)
     gain_step(0)
+    some_weight_grads(2)
     sync()
 
     sum_step(IN, 3)
-    sum_step(OUT, 4)
-    small_step(6)
+    sum_step(OUT, 5)
+    reduce_near(M, own)
     small_step(7)
     gain_step(1)
-    sync()
-
+    some_weight_grads(3)
+    sync()
+    for plane in PLANES:
+        live.pop((KEPT, plane))
+
+    mixed_out = middle + reduced(M, own).astype(wide) + live.pop(MIXED).astype(wide)
+    live[MIXED] = (mixed_out + live.pop(SIDE).astype(wide)).astype(narrow)
+    live[OUT] = summed(OUT)
     sum_step(IN, 4)
-    sum_step(OUT, 5)
     small_step(8)
     gain_step(2)
     gain_step(3)
     sync()
 
-    grad_w_out = summed(OUT)
-    sum_step(IN, 5)
-    mixed_out = live[HOME].astype(wide) + live[MIXED].astype(wide) + live[SIDE].astype(wide)
-    mixed_out = (middle + mixed_out).astype(narrow)
+    columns = local_heads * HD
     small_step(9)
     gain_step(4)
-    sync()
+    sum_step(IN, 5)
+    even, odd = weight_hops[0]
+    side = jnp.where(odd_core == 0, bit(even), bit(odd))
+    half = live[IN, KEPT].shape[0]
+
+    def put(whole, part, index, at):
+        part = part[:, index * columns : (index + 1) * columns].astype(wide)
+        return lax.dynamic_update_slice_in_dim(whole, part, at * half, 0)
+
+    empty = jnp.zeros((2 * half, columns), wide)
+    live[RAW] = [put(empty, live[IN, KEPT], index, side) for index in range(3)]
+    sync()
+    grads_in = [put(whole, live[IN, GOT], i, 1 - side) for i, whole in enumerate(live[RAW])]
     grad_gain_attn = (live[GAIN][0] + live[GAIN][1])[0]
     small = summed(SMALL, small_hops).reshape(model_width, -1)
-    grad_w_in = summed(IN)
-    columns = local_heads * HD
 
     return (
-        mixed_out,
+        live[MIXED],
         live[TOKENS],
         grad_gain_attn,
-        grad_w_in[:, :columns],
-        grad_w_in[:, columns : 2 * columns],
-        grad_w_in[:, 2 * columns :],
-        grad_w_out,
+        *grads_in,
+        live[OUT],
         small[:, expert_count],
         small[:, :expert_count],
         *live[EXPERTS],

time: 781 us -> 739 us (0.946)
  waiting for transfers between devices: 305 us -> 274 us
  other arithmetic: 97.8 us -> 108 us
  local copies, waits for them, and re-layouts: 54 us -> 45.8 us
    ppermute x102 -> x103, waiting for transfers between devices: 305 us -> 274 us  [swap(): return lax.ppermute(value, BOTH, perm)]
    convert_element_type x24 -> x15, other arithmetic: 47.9 us -> 24.1 us  [add(): return (left.astype(wide) + right.astype(wide)).astype(narrow)]
    convert_element_type x2 -> x9, other arithmetic: 4.65 us -> 19.5 us  [the longest x8 18.3 us: reduce_near(): live[name, plane, SIDE] = near(sums[1].astype(narrow))]
    ppermute x102 -> x103, starting transfers between devices: 113 us -> 108 us  [swap(): return lax.ppermute(value, BOTH, perm)]
  transfers between devices with their start and end apart: 102 -> 103, of which waited for: 34 -> 41; matrix products, arithmetic and copies ran while one was open for 16% -> 15% of each run, Pallas kernels for 22% -> 23%
where the time goes in v1:
time: 739 us; the launch traced here: 729 us
  waiting for transfers between devices  274 us (37%)
  Pallas kernels  166 us (22%)
  other arithmetic  108 us (15%)
  starting transfers between devices  108 us (15%)
  local copies, waits for them, and re-layouts  45.8 us (6%)
  matrix products  25.4 us (3%)
    ppermute x103, waiting for transfers between devices, swap(): return lax.ppermute(value, BOTH, perm)  274 us
    pallas_call x4, Pallas kernels, expert_chunk(): pl.pallas_call(functools.partial(expert_kernel, places, top_count), in_sp...  120 us
    ppermute x103, starting transfers between devices, swap(): return lax.ppermute(value, BOTH, perm)  108 us
    pallas_call x4, Pallas kernels, weight_grads(): pl.pallas_call(functools.partial(weight_kernel, parts, len(partial)), gri...  45.1 us
    convert_element_type x15, other arithmetic, add(): return (left.astype(wide) + right.astype(wide)).astype(narrow)  24.1 us
    convert_element_type x8, other arithmetic, reduce_near(): live[name, plane, SIDE] = near(sums[1].astype(narrow))  18.3 us
    unnamed x194, local copies, waits for them, and re-layouts  15.1 us
  transfers between devices with their start and end apart: 103, of which 41 were waited for; matrix products, arithmetic and copies ran while one was open for 15% of the time, Pallas kernels for 23%

profile of v1, /device:TPU:0, one launch (start us, length us, event | category | flops | bytes accessed | tf_op | source)
XLA Modules:
  0.0 729.0 jit_solution(8358027311183151818)
XLA Ops:
  36.7 10.3 %collective-permute-done.4 = bf16[64,2176]{1,0:T(8,128)(2,1)S(1)} collective-permute-done((bf16[64,2176]{1,0:T(8,128)(2,1)S(1)}, bf16[64,2176]{1,0:T(8,128)(2,1)S(1)}, u32[]{:S(2)}, u32[]{:S(2)}) %collective-permute-start.4) | collective-permute-done | bytes 278560 | tf_op jit(solution)/shard_map/ppermute | solution.py:691
  48.9 7.9 %collective-permute-done.9.refs_8_ = bf16[128,2176]{1,0:T(8,128)(2,1)S(1)} collective-permute-done((bf16[128,2176]{1,0:T(8,128)(2,1)S(1)}, bf16[128,2176]{1,0:T(8,128)(2,1)S(1)}, u32[]{:S(2)}, u32[]{:S(2)}) %collective-permute-start.9) | collective-permute-done | bytes 557088 | tf_op jit(solution)/shard_map/ppermute | solution.py:691
  61.0 11.3 %collective-permute-done.10 = bf16[128,2048]{1,0:T(8,128)(2,1)S(1)} collective-permute-done((bf16[128,2048]{1,0:T(8,128)(2,1)S(1)}, bf16[128,2048]{1,0:T(8,128)(2,1)S(1)}, u32[]{:S(2)}, u32[]{:S(2)}) %collective-permute-start.10) | collective-permute-done | bytes 524320 | tf_op jit(solution)/shard_map/ppermute | solution.py:691
  85.1 10.5 %collective-permute-done.12.refs_1_ = bf16[128,2048]{1,0:T(8,128)(2,1)S(1)} collective-permute-done((bf16[128,2048]{1,0:T(8,128)(2,1)S(1)}, bf16[128,2048]{1,0:T(8,128)(2,1)S(1)}, u32[]{:S(2)}, u32[]{:S(2)}) %collective-permute-start.12) | collective-permute-done | bytes 524320 | tf_op jit(solution)/shard_map/ppermute | solution.py:691
  104.7 7.5 %collective-permute-done.20 = bf16[64,2048]{1,0:T(8,128)(2,1)S(1)} collective-permute-done((bf16[64,2048]{1,0:T(8,128)(2,1)S(1)}, bf16[64,2048]{1,0:T(8,128)(2,1)S(1)}, u32[]{:S(2)}, u32[]{:S(2)}) %collective-permute-start.20) | collective-permute-done | bytes 262176 | tf_op jit(solution)/shard_map/ppermute | solution.py:691
  143.0 30.2 %shard_map.220 = (bf16[512,2048]{1,0:T(8,128)(2,1)}, bf16[512,2048]{1,0:T(8,128)(2,1)}, bf16[512,2048]{1,0:T(8,128)(2,1)}, bf16[512,2048]{1,0:T(8,128)(2,1)}, f3...) custom-call(bf16[128,2048]{1,0:T(8,128)(2,1)} %copy-done.8, ...), custom_call_target="tpu_custom_call" | custom-call | flops 19327352832 | bytes 37748736 | tf_op jit(solution)/shard_map/pallas_call | solution.py:576
  183.3 30.0 %shard_map.221 = (bf16[512,2048]{1,0:T(8,128)(2,1)}, bf16[512,2048]{1,0:T(8,128)(2,1)}, bf16[512,2048]{1,0:T(8,128)(2,1)}, bf16[512,2048]{1,0:T(8,128)(2,1)}, f3...) custom-call(bf16[128,2048]{1,0:T(8,128)(2,1)} %copy-done.69, ...), custom_call_target="tpu_custom_call" | custom-call | flops 19327352832 | bytes 37748736 | tf_op jit(solution)/shard_map/pallas_call | solution.py:576
  230.6 30.2 %shard_map.222 = (bf16[512,2048]{1,0:T(8,128)(2,1)}, bf16[512,2048]{1,0:T(8,128)(2,1)}, bf16[512,2048]{1,0:T(8,128)(2,1)}, bf16[512,2048]{1,0:T(8,128)(2,1)}, f3...) custom-call(bf16[128,4224]{1,0:T(8,128)(2,1)} %pad_maximum_fusion.7., ...), custom_call_target="tpu_custom_call" | custom-call | flops 19327352832 | bytes 37748736 | tf_op jit(solution)/shard_map/pallas_call | solution.py:576
  279.2 30.0 %shard_map.223 = (bf16[512,2048]{1,0:T(8,128)(2,1)}, bf16[512,2048]{1,0:T(8,128)(2,1)}, bf16[512,2048]{1,0:T(8,128)(2,1)}, bf16[512,2048]{1,0:T(8,128)(2,1)}, f3...) custom-call(bf16[128,4224]{1,0:T(8,128)(2,1)} %constant_dynamic-upda, ...), custom_call_target="tpu_custom_call" | custom-call | flops 19327352832 | bytes 37748736 | tf_op jit(solution)/shard_map/pallas_call | solution.py:576
  328.4 16.3 %collective-permute-done.48 = f32[4,2,8,128]{3,2,1,0:T(8,128)S(1)} collective-permute-done((f32[4,2,8,128]{3,2,1,0:T(8,128)S(1)}, f32[4,2,8,128]{3,2,1,0:T(8,128)S(1)}, u32[]{:S(2)}, u32[]{:S(2)}) %collective-permute-start.48) | collective-permute-done | bytes 32800 | tf_op jit(solution)/shard_map/ppermute | solution.py:691
  375.9 19.9 %collective-permute-done.57 = f32[2,2,8,128]{3,2,1,0:T(8,128)S(1)} collective-permute-done((f32[2,2,8,128]{3,2,1,0:T(8,128)S(1)}, f32[2,2,8,128]{3,2,1,0:T(8,128)S(1)}, u32[]{:S(2)}, u32[]{:S(2)}) %collective-permute-start.57) | collective-permute-done | bytes 16416 | tf_op jit(solution)/shard_map/ppermute | solution.py:691
  459.1 11.9 %collective-permute-done.70 = bf16[128,2048]{1,0:T(8,128)(2,1)S(1)} collective-permute-done((bf16[128,2048]{1,0:T(8,128)(2,1)S(1)}, bf16[128,2048]{1,0:T(8,128)(2,1)S(1)}, u32[]{:S(2)}, u32[]{:S(2)}) %collective-permute-start.70) | collective-permute-done | bytes 524320 | tf_op jit(solution)/shard_map/ppermute | solution.py:691
  497.9 10.1 %collective-permute-done.72 = bf16[128,2048]{1,0:T(8,128)(2,1)S(1)} collective-permute-done((bf16[128,2048]{1,0:T(8,128)(2,1)}, bf16[128,2048]{1,0:T(8,128)(2,1)S(1)}, u32[]{:S(2)}, u32[]{:S(2)}) %collective-permute-start.72) | collective-permute-done | bytes 524320 | tf_op jit(solution)/shard_map/ppermute | solution.py:691
  517.1 11.3 %shard_map.224 = (f32[8,2048,256]{2,1,0:T(8,128)}, f32[8,2048,256]{2,1,0:T(8,128)}, f32[8,256,2048]{2,1,0:T(8,128)}) custom-call(bf16[8,192,2048]{2,1,0:T(8,128)(2,1)} %get-tuple-element.1668.refs_0_, bf16[8,192,2048]{2,1,0:T(8,128)(2,1)} %get-tuple-element.1672.refs_1_, bf16[8,192,2048]{2,1,0:T(8,128)(2,1)} %get-tuple-element.1680.refs_2_, ...), custom_call_target="tpu_custom_call" | custom-call | flops 4831838208 | bytes 27525120 | tf_op jit(solution)/shard_map/pallas_call | solution.py:638
  531.8 17.4 %collective-permute-done.78 = bf16[1024,1536]{1,0:T(8,128)(2,1)} collective-permute-done((bf16[1024,1536]{1,0:T(8,128)(2,1)}, bf16[1024,1536]{1,0:T(8,128)(2,1)}, u32[]{:S(2)}, u32[]{:S(2)}) %collective-permute-start.78) | collective-permute-done | bytes 3145760 | tf_op jit(solution)/shard_map/ppermute | solution.py:691
  558.7 11.2 %shard_map.225 = (f32[8,2048,256]{2,1,0:T(8,128)}, f32[8,2048,256]{2,1,0:T(8,128)}, f32[8,256,2048]{2,1,0:T(8,128)}) custom-call(bf16[8,192,2048]{2,1,0:T(8,128)(2,1)} %get-tuple-element.1668.refs_0_, bf16[8,192,2048]{2,1,0:T(8,128)(2,1)} %get-tuple-element.1672.refs_1_, ...), custom_call_target="tpu_custom_call", output_to_operand_aliasing={{0}: (16, {}), {1}: (17, {}), {2}: (18, {})} | custom-call | flops 4831838208 | bytes 27525120 | tf_op jit(solution)/shard_map/pallas_call | solution.py:638
  570.1 7.9 %collective-permute-done.83 = bf16[64,2048]{1,0:T(8,128)(2,1)} collective-permute-done((bf16[64,2048]{1,0:T(8,128)(2,1)S(1)}, bf16[64,2048]{1,0:T(8,128)(2,1)}, u32[]{:S(2)}, u32[]{:S(2)}) %collective-permute-start.83) | collective-permute-done | bytes 262176 | tf_op jit(solution)/shard_map/ppermute | solution.py:691
  594.7 11.2 %shard_map.226 = (f32[8,2048,256]{2,1,0:T(8,128)}, f32[8,2048,256]{2,1,0:T(8,128)}, f32[8,256,2048]{2,1,0:T(8,128)}) custom-call(bf16[8,192,2048]{2,1,0:T(8,128)(2,1)} %get-tuple-element.1668.refs_0_, bf16[8,192,2048]{2,1,0:T(8,128)(2,1)} %get-tuple-element.1672.refs_1_, ...), custom_call_target="tpu_custom_call", output_to_operand_aliasing={{0}: (16, {}), {1}: (17, {}), {2}: (18, {})} | custom-call | flops 4831838208 | bytes 27525120 | tf_op jit(solution)/shard_map/pallas_call | solution.py:638
  607.3 8.1 %collective-permute-done.90 = f32[2,64,65]{2,1,0:T(8,128)S(1)} collective-permute-done((f32[2,64,65]{2,1,0:T(8,128)S(1)}, f32[2,64,65]{2,1,0:T(8,128)S(1)}, u32[]{:S(2)}, u32[]{:S(2)}) %collective-permute-start.90) | collective-permute-done | bytes 33312 | tf_op jit(solution)/shard_map/ppermute | solution.py:691
  615.4 8.5 %collective-permute-done.86 = bf16[256,1536]{1,0:T(8,128)(2,1)} collective-permute-done((bf16[256,1536]{1,0:T(8,128)(2,1)}, bf16[256,1536]{1,0:T(8,128)(2,1)}, u32[]{:S(2)}, u32[]{:S(2)}) %collective-permute-start.86) | collective-permute-done | bytes 786464 | tf_op jit(solution)/shard_map/ppermute | solution.py:691
  633.2 11.4 %shard_map.227 = (f32[8,2048,256]{2,1,0:T(8,128)}, f32[8,2048,256]{2,1,0:T(8,128)}, f32[8,256,2048]{2,1,0:T(8,128)}) custom-call(bf16[8,192,2048]{2,1,0:T(8,128)(2,1)} %get-tuple-element.1668.refs_0_, bf16[8,192,2048]{2,1,0:T(8,128)(2,1)} %get-tuple-element.1672.refs_1_, ...), custom_call_target="tpu_custom_call", output_to_operand_aliasing={{0}: (16, {}), {1}: (17, {}), {2}: (18, {})} | custom-call | flops 4831838208 | bytes 27525120 | tf_op jit(solution)/shard_map/pallas_call | solution.py:638
  648.6 12.6 %collective-permute-done.92 = bf16[256,1536]{1,0:T(8,128)(2,1)S(1)} collective-permute-done((bf16[256,1536]{1,0:T(8,128)(2,1)S(1)}, bf16[256,1536]{1,0:T(8,128)(2,1)S(1)}, u32[]{:S(2)}, u32[]{:S(2)}) %collective-permute-start.92) | collective-permute-done | bytes 786464 | tf_op jit(solution)/shard_map/ppermute | solution.py:691
  671.2 11.0 %collective-permute-done.97 = f32[1,2048]{1,0:T(1,128)S(1)} collective-permute-done((f32[1,2048]{1,0:T(1,128)S(1)}, f32[1,2048]{1,0:T(1,128)S(1)}, u32[]{:S(2)}, u32[]{:S(2)}) %collective-permute-start.97) | collective-permute-done | bytes 8224 | tf_op jit(solution)/shard_map/ppermute | solution.py:691
  693.0 27.3 %collective-permute-done.102 = bf16[1024,1536]{1,0:T(8,128)(2,1)} collective-permute-done((bf16[1024,1536]{1,0:T(8,128)(2,1)S(1)}, bf16[1024,1536]{1,0:T(8,128)(2,1)}, u32[]{:S(2)}, u32[]{:S(2)}) %collective-permute-start.102) | collective-permute-done | bytes 3145760 | tf_op jit(solution)/shard_map/ppermute | solution.py:691
  (586 shorter events, 361.9 us)
Async XLA Ops:
  132.4 40.8 %collective-permute-start.24 = (bf16[512,2048]{1,0:T(8,128)(2,1)}, bf16[512,2048]{1,0:T(8,128)(2,1)}, u32[]{:S(2)}, u32[]{:S(2)}) collective-permute-start(bf16[512,2048]{1,0:T(8,128)(2,1)} %pad_maximum_fusion.6), channel_id=1, source_target_pairs={{0,1},{1,0},{2,3},{3,2},{4,5},{5,4},{6,7},{7,6},{8,9},{9,8},{10,11... | collective-permute-start | bytes 6291464 | tf_op jit(solution)/shard_map/ppermute | solution.py:691
  133.6 39.6 %collective-permute-start.25 = (bf16[128,4224]{1,0:T(8,128)(2,1)}, bf16[128,4224]{1,0:T(8,128)(2,1)}, u32[]{:S(2)}, u32[]{:S(2)}) collective-permute-start(bf16[128,4224]{1,0:T(8,128)(2,1)} %pad_maximum_fusion.7.refs_0_), channel_id=1, source_target_pairs={{0,2},{1,5},{2,0},{3,7},{4,6},{5,1},{6,4},{7,3},{8,10},{9,13},{10,... | collective-permute-start | bytes 3244040 | tf_op jit(solution)/shard_map/ppermute | solution.py:691
  134.8 38.5 %collective-permute-start.26 = (bf16[128,4224]{1,0:T(8,128)(2,1)}, bf16[128,4224]{1,0:T(8,128)(2,1)}, u32[]{:S(2)}, u32[]{:S(2)}) collective-permute-start(bf16[128,4224]{1,0:T(8,128)(2,1)} %pad_maximum_fusion.7.refs_0_), channel_id=1, source_target_pairs={{0,4},{1,3},{2,6},{3,1},{4,0},{5,7},{6,2},{7,5},{8,12},{9,11},{10,... | collective-permute-start | bytes 3244040 | tf_op jit(solution)/shard_map/ppermute | solution.py:691
  135.9 37.3 %collective-permute-start.27 = (bf16[128,2048]{1,0:T(8,128)(2,1)S(1)}, bf16[128,2048]{1,0:T(8,128)(2,1)}, u32[]{:S(2)}, u32[]{:S(2)}) collective-permute-start(bf16[128,2048]{1,0:T(8,128)(2,1)S(1)} %multiply_convert_fusion.1.refs_0_), channel_id=1, source_target_pairs={{0,16},{1,17},{2,18},{3,19},{4,20},{5,21},{6,22},{7,23},{8,24},{9,... | collective-permute-start | bytes 1572872 | tf_op jit(solution)/shard_map/ppermute | solution.py:691
  177.1 41.0 %collective-permute-start.29 = (bf16[384,4224]{1,0:T(8,128)(2,1)}, bf16[384,4224]{1,0:T(8,128)(2,1)}, u32[]{:S(2)}, u32[]{:S(2)}) collective-permute-start(bf16[384,4224]{1,0:T(8,128)(2,1)} %pad_maximum_fusion), channel_id=1, source_target_pairs={{0,1},{1,0},{2,3},{3,2},{4,5},{5,4},{6,7},{7,6},{8,9},{9,8},{10,11... | collective-permute-start | bytes 9732104 | tf_op jit(solution)/shard_map/ppermute | solution.py:691
  177.1 41.0 %collective-permute-start.32 = (bf16[512,2048]{1,0:T(8,128)(2,1)}, bf16[512,2048]{1,0:T(8,128)(2,1)}, u32[]{:S(2)}, u32[]{:S(2)}) collective-permute-start(bf16[512,2048]{1,0:T(8,128)(2,1)} %get-tuple-element.1046), channel_id=1, source_target_pairs={{0,1},{1,0},{2,3},{3,2},{4,5},{5,4},{6,7},{7,6},{8,9},{9,8},{10,11... | collective-permute-start | bytes 6291464 | tf_op jit(solution)/shard_map/ppermute | solution.py:691
  180.4 32.9 %collective-permute-start.30 = (bf16[128,4224]{1,0:T(8,128)(2,1)}, bf16[128,4224]{1,0:T(8,128)(2,1)}, u32[]{:S(2)}, u32[]{:S(2)}) collective-permute-start(bf16[128,4224]{1,0:T(8,128)(2,1)} %constant_dynamic-update-slice_fusion.refs_0_), channel_id=1, source_target_pairs={{0,2},{1,5},{2,0},{3,7},{4,6},{5,1},{6,4},{7,3},{8,10},{9,13},{10,... | collective-permute-start | bytes 3244040 | tf_op jit(solution)/shard_map/ppermute | solution.py:691
  181.2 32.0 %collective-permute-start.31 = (bf16[128,4224]{1,0:T(8,128)(2,1)}, bf16[128,4224]{1,0:T(8,128)(2,1)}, u32[]{:S(2)}, u32[]{:S(2)}) collective-permute-start(bf16[128,4224]{1,0:T(8,128)(2,1)} %constant_dynamic-update-slice_fusion.refs_0_), channel_id=1, source_target_pairs={{0,4},{1,3},{2,6},{3,1},{4,0},{5,7},{6,2},{7,5},{8,12},{9,11},{10,... | collective-permute-start | bytes 3244040 | tf_op jit(solution)/shard_map/ppermute | solution.py:691
  181.8 36.3 %collective-permute-start.28 = (bf16[128,4224]{1,0:T(8,128)(2,1)}, bf16[128,4224]{1,0:T(8,128)(2,1)}, u32[]{:S(2)}, u32[]{:S(2)}) collective-permute-start(bf16[128,4224]{1,0:T(8,128)(2,1)} %collective-permute-done.25.refs_1_), channel_id=1, source_target_pairs={{0,4},{1,3},{2,6},{3,1},{4,0},{5,7},{6,2},{7,5},{8,12},{9,11},{10,... | collective-permute-start | bytes 3244040 | tf_op jit(solution)/shard_map/ppermute | solution.py:691
  225.3 35.5 %collective-permute-start.35 = (bf16[384,4224]{1,0:T(8,128)(2,1)}, bf16[384,4224]{1,0:T(8,128)(2,1)}, u32[]{:S(2)}, u32[]{:S(2)}) collective-permute-start(bf16[384,4224]{1,0:T(8,128)(2,1)} %pad_maximum_fusion.1), channel_id=1, source_target_pairs={{0,1},{1,0},{2,3},{3,2},{4,5},{5,4},{6,7},{7,6},{8,9},{9,8},{10,11... | collective-permute-start | bytes 9732104 | tf_op jit(solution)/shard_map/ppermute | solution.py:691
  225.4 35.4 %collective-permute-start.34 = (bf16[128,4224]{1,0:T(8,128)(2,1)}, bf16[128,4224]{1,0:T(8,128)(2,1)}, u32[]{:S(2)}, u32[]{:S(2)}) collective-permute-start(bf16[128,4224]{1,0:T(8,128)(2,1)} %collective-permute-done.30.refs_1_), channel_id=1, source_target_pairs={{0,4},{1,3},{2,6},{3,1},{4,0},{5,7},{6,2},{7,5},{8,12},{9,11},{10,... | collective-permute-start | bytes 3244040 | tf_op jit(solution)/shard_map/ppermute | solution.py:691
  226.7 34.1 %collective-permute-start.37 = (bf16[512,2048]{1,0:T(8,128)(2,1)}, bf16[512,2048]{1,0:T(8,128)(2,1)}, u32[]{:S(2)}, u32[]{:S(2)}) collective-permute-start(bf16[512,2048]{1,0:T(8,128)(2,1)} %get-tuple-element.1125), channel_id=1, source_target_pairs={{0,1},{1,0},{2,3},{3,2},{4,5},{5,4},{6,7},{7,6},{8,9},{9,8},{10,11... | collective-permute-start | bytes 6291464 | tf_op jit(solution)/shard_map/ppermute | solution.py:691
  226.7 34.2 %collective-permute-start.38 = (bf16[512,2048]{1,0:T(8,128)(2,1)}, bf16[512,2048]{1,0:T(8,128)(2,1)}, u32[]{:S(2)}, u32[]{:S(2)}) collective-permute-start(bf16[512,2048]{1,0:T(8,128)(2,1)} %get-tuple-element.1126), channel_id=1, source_target_pairs={{0,1},{1,0},{2,3},{3,2},{4,5},{5,4},{6,7},{7,6},{8,9},{9,8},{10,11... | collective-permute-start | bytes 6291464 | tf_op jit(solution)/shard_map/ppermute | solution.py:691
  229.8 31.0 %collective-permute-start.36 = (bf16[2,128,2048]{2,1,0:T(8,128)(2,1)}, bf16[2,128,2048]{2,1,0:T(8,128)(2,1)}, u32[]{:S(2)}, u32[]{:S(2)}) collective-permute-start(bf16[2,128,2048]{2,1,0:T(8,128)(2,1)} %bitcast.19), channel_id=1, source_target_pairs={{0,4},{1,3},{2,6},{3,1},{4,0},{5,7},{6,2},{7,5},{8,12},{9,11},{10,... | collective-permute-start | bytes 3145736 | tf_op jit(solution)/shard_map/ppermute | solution.py:691
  270.8 38.4 %collective-permute-start.43 = (bf16[2,128,2048]{2,1,0:T(8,128)(2,1)}, bf16[2,128,2048]{2,1,0:T(8,128)(2,1)}, u32[]{:S(2)}, u32[]{:S(2)}) collective-permute-start(bf16[2,128,2048]{2,1,0:T(8,128)(2,1)} %bitcast.23), channel_id=1, source_target_pairs={{0,4},{1,3},{2,6},{3,1},{4,0},{5,7},{6,2},{7,5},{8,12},{9,11},{10,... | collective-permute-start | bytes 3145736 | tf_op jit(solution)/shard_map/ppermute | solution.py:691
  274.7 34.5 %collective-permute-start.42 = (bf16[2,128,2048]{2,1,0:T(8,128)(2,1)}, bf16[2,128,2048]{2,1,0:T(8,128)(2,1)}, u32[]{:S(2)}, u32[]{:S(2)}) collective-permute-start(bf16[2,128,2048]{2,1,0:T(8,128)(2,1)} %bitcast.22), channel_id=1, source_target_pairs={{0,4},{1,3},{2,6},{3,1},{4,0},{5,7},{6,2},{7,5},{8,12},{9,11},{10,... | collective-permute-start | bytes 3145736 | tf_op jit(solution)/shard_map/ppermute | solution.py:691
  275.4 33.8 %collective-permute-start.44 = (bf16[512,2048]{1,0:T(8,128)(2,1)}, bf16[512,2048]{1,0:T(8,128)(2,1)}, u32[]{:S(2)}, u32[]{:S(2)}) collective-permute-start(bf16[512,2048]{1,0:T(8,128)(2,1)} %get-tuple-element.1216), channel_id=1, source_target_pairs={{0,1},{1,0},{2,3},{3,2},{4,5},{5,4},{6,7},{7,6},{8,9},{9,8},{10,11... | collective-permute-start | bytes 6291464 | tf_op jit(solution)/shard_map/ppermute | solution.py:691
  511.6 37.6 %collective-permute-start.78 = (bf16[1024,1536]{1,0:T(8,128)(2,1)}, bf16[1024,1536]{1,0:T(8,128)(2,1)}, u32[]{:S(2)}, u32[]{:S(2)}) collective-permute-start(bf16[1024,1536]{1,0:T(8,128)(2,1)} %dynamic-slice_convert_fusion), channel_id=1, source_target_pairs={{0,4},{1,9},{2,6},{3,11},{4,0},{5,13},{6,2},{7,15},{8,12},{9,1},{1... | collective-permute-start | bytes 9437192 | tf_op jit(solution)/shard_map/ppermute | solution.py:691
  581.6 33.8 %collective-permute-start.89 = (bf16[128,2048]{1,0:T(8,128)(2,1)}, bf16[128,2048]{1,0:T(8,128)(2,1)S(1)}, u32[]{:S(2)}, u32[]{:S(2)}) collective-permute-start(bf16[128,2048]{1,0:T(8,128)(2,1)} %add_convert_fusion.11), channel_id=1, source_target_pairs={{0,8},{1,9},{2,10},{3,11},{4,12},{5,13},{6,14},{7,15},{8,0},{9,1},... | collective-permute-start | bytes 1572872 | tf_op jit(solution)/shard_map/ppermute | solution.py:691
  586.2 37.7 %collective-permute-start.88 = (bf16[2,128,2048]{2,1,0:T(8,128)(2,1)S(1)}, bf16[2,128,2048]{2,1,0:T(8,128)(2,1)}, u32[]{:S(2)}, u32[]{:S(2)}) collective-permute-start(bf16[2,128,2048]{2,1,0:T(8,128)(2,1)S(1)} %bitcast.223), channel_id=1, source_target_pairs={{0,4},{1,3},{2,6},{3,1},{4,0},{5,7},{6,2},{7,5},{8,12},{9,11},{10,... | collective-permute-start | bytes 3145736 | tf_op jit(solution)/shard_map/ppermute | solution.py:691
  592.0 32.0 %collective-permute-start.86 = (bf16[256,1536]{1,0:T(8,128)(2,1)}, bf16[256,1536]{1,0:T(8,128)(2,1)}, u32[]{:S(2)}, u32[]{:S(2)}) collective-permute-start(bf16[256,1536]{1,0:T(8,128)(2,1)} %dynamic-slice_convert_fusion.3), channel_id=1, source_target_pairs={{0,16},{1,17},{2,18},{3,19},{4,20},{5,21},{6,22},{7,23},{8,24},{9,... | collective-permute-start | bytes 2359304 | tf_op jit(solution)/shard_map/ppermute | solution.py:691
  625.3 35.9 %collective-permute-start.93 = (bf16[256,2048]{1,0:T(8,128)(2,1)S(1)}, bf16[256,2048]{1,0:T(8,128)(2,1)S(1)}, u32[]{:S(2)}, u32[]{:S(2)}) collective-permute-start(bf16[256,2048]{1,0:T(8,128)(2,1)S(1)} %constant_dynamic-update-slice_fusion.28), channel_id=1, source_target_pairs={{0,4},{1,9},{2,6},{3,11},{4,0},{5,13},{6,2},{7,15},{8,12},{9,1},{1... | collective-permute-start | bytes 3145736 | tf_op jit(solution)/shard_map/ppermute | solution.py:691
  627.6 33.7 %collective-permute-start.92 = (bf16[256,1536]{1,0:T(8,128)(2,1)S(1)}, bf16[256,1536]{1,0:T(8,128)(2,1)S(1)}, u32[]{:S(2)}, u32[]{:S(2)}) collective-permute-start(bf16[256,1536]{1,0:T(8,128)(2,1)S(1)} %add_convert_fusion.8), channel_id=1, source_target_pairs={{0,16},{1,17},{2,18},{3,19},{4,20},{5,21},{6,22},{7,23},{8,24},{9,... | collective-permute-start | bytes 2359304 | tf_op jit(solution)/shard_map/ppermute | solution.py:691
  682.8 37.4 %collective-permute-start.102 = (bf16[1024,1536]{1,0:T(8,128)(2,1)S(1)}, bf16[1024,1536]{1,0:T(8,128)(2,1)}, u32[]{:S(2)}, u32[]{:S(2)}) collective-permute-start(bf16[1024,1536]{1,0:T(8,128)(2,1)S(1)} %constant_dynamic-update-slice_fusion.16), channel_id=1, source_target_pairs={{0,4},{1,9},{2,6},{3,11},{4,0},{5,13},{6,2},{7,15},{8,12},{9,1},{1... | collective-permute-start | bytes 9437192 | tf_op jit(solution)/shard_map/ppermute | solution.py:691
  (170 other events, 2357.4 us)

commit v2 on v1

--- a/solution.py
+++ b/solution.py
@@ -719,9 +719,16 @@
     def gather_across(name, plane):
         live[name, plane, 3] = swap(live[name, plane, 0], ACROSS | ASIDE)
 
+    def join_core(name, plane, *slots):
+        blocks = [live[name, plane, slot] for slot in slots]
+        live[name, plane, (OTHER,) + slots] = jnp.concatenate(blocks, axis=0)
+
+    def send_core(name, plane, *slots):
+        live[name, plane, (OTHER,) + slots] = core(live[name, plane, (OTHER,) + slots])
+
     def gather_core(name, plane, *slots):
-        blocks = [live[name, plane, slot] for slot in slots]
-        live[name, plane, (OTHER,) + slots] = core(jnp.concatenate(blocks, axis=0))
+        join_core(name, plane, *slots)
+        send_core(name, plane, *slots)
 
     def blocks_of(name, plane):
         found = {}
@@ -739,20 +746,33 @@
     def reduce_core(name, plane):
         live[name, plane, OTHER] = core(live.pop((name, plane, AWAY)))
 
-    def reduce_far(name, plane):
+    def add_far(name, plane):
         kept = live[name, plane, NEAR].reshape(4, block_len, model_width)
         got = live[name, plane, OTHER].reshape(4, block_len, model_width)
-        live[name, plane, FAR] = far(add(kept[2:], got[2:]))
-
-    def reduce_near(name, plane):
+        live[name, plane, FAR] = add(kept[2:], got[2:])
+
+    def send_far(name, plane):
+        live[name, plane, FAR] = far(live[name, plane, FAR])
+
+    def reduce_far(name, plane):
+        add_far(name, plane)
+        send_far(name, plane)
+
+    def add_near(name, plane):
         kept = live.pop((name, plane, NEAR)).reshape(4, block_len, model_width)
         got = live.pop((name, plane, OTHER)).reshape(4, block_len, model_width)
         back = live.pop((name, plane, FAR))
         sums = [
             kept[i].astype(wide) + got[i].astype(wide) + back[i].astype(wide) for i in range(2)
         ]
-        live[name, plane, OWN] = sums[0].astype(narrow)
-        live[name, plane, SIDE] = near(sums[1].astype(narrow))
+        live[name, plane, OWN], live[name, plane, SIDE] = [part.astype(narrow) for part in sums]
+
+    def send_near(name, plane):
+        live[name, plane, SIDE] = near(live[name, plane, SIDE])
+
+    def reduce_near(name, plane):
+        add_near(name, plane)
+        send_near(name, plane)
 
     def reduced(name, plane):
         return add(live.pop((name, plane, OWN)), live.pop((name, plane, SIDE)))
@@ -859,6 +879,10 @@
     split_quarters(jnp.dot(live[HEADS], w_out, preferred_element_type=wide))
     sync()
 
+    expert_range = jnp.arange(expert_count, dtype=jnp.int32)
+    rolled = (first_expert + expert_range) % expert_count
+    live[ROUTER] = jnp.take(w_router.T, rolled, axis=0)
+    live[NAMED] = jnp.broadcast_to(rolled.astype(wide)[:, None], (expert_count, LANES))
     live[SENT] = core(live[SENT])
     gather_far(G, nxt)
     live[G, far_plane, 0] = jnp.concatenate(live[G, far_plane, 0], axis=0)
@@ -885,26 +909,23 @@
 
     gather_near(H, own)
     live[H, nxt, 0] = swap(hidden_two, nxt)
-    gather_core(G, own, 0, 1, 2, 3)
     logits = jnp.dot(hidden_two, w_router, preferred_element_type=wide)
     expert_range = jnp.arange(expert_count, dtype=jnp.int32)
     matches = expert_ids[:, :, None] == expert_range[None, None, :]
     chosen = jnp.sum(jnp.where(matches, logits[:, None, :], 0.0), axis=2)
     gate_weights = jax.nn.softmax(chosen, axis=-1)
-    rolled = (first_expert + expert_range) % expert_count
-    live[ROUTER] = jnp.take(w_router.T, rolled, axis=0)
-    live[NAMED] = jnp.broadcast_to(rolled.astype(wide)[:, None], (expert_count, LANES))
     sync()
 
     gather_far(H, own)
     gather_near(H, nxt)
     hidden_two = live[H, own, 0]
-    gather_core(G, nxt, 0, 1, 2, 3)
+    gather_core(G, own, 0, 1, 2, 3)
     live[H, last, 0] = [swap(hidden_two[:half_block], last)]
     sync()
 
     gather_far(H, nxt)
     gather_core(H, own, 0, 1, 2, 3)
+    gather_core(G, nxt, 0, 1, 2, 3)
     hidden_two = live[H, own, 0]
     live[H, last, 0] = live[H, last, 0] + [swap(hidden_two[half_block:], last)]
     sync()
@@ -950,33 +971,38 @@
     gather_core(H, nxt, 0, 1, 2, 3)
     join_pair(last)
     gather_near(PAIR, last)
+    gather_core(PAIR, last, 0)
     live[H, far_plane, 0] = swap(live[H, own, 0], far_plane)
     experts(own)
     sync()
 
     gather_far(PAIR, last)
-    gather_core(PAIR, last, 0, 1, 2)
+    gather_core(PAIR, last, 1, 2)
     join_pair(far_plane)
     gather_near(PAIR, far_plane)
     reduce_core(R, own)
     experts(nxt)
     sync()
     gather_core(PAIR, last, 3)
+    join_core(PAIR, far_plane, 0, 1, 2)
+    add_far(R, own)
     sync()
 
     gather_far(PAIR, far_plane)
-    gather_core(PAIR, far_plane, 0, 1, 2)
-    reduce_far(R, own)
+    send_core(PAIR, far_plane, 0, 1, 2)
+    send_far(R, own)
     reduce_core(R, nxt)
     reduce_core(M, own)
     experts(last)
     sync()
     gather_core(PAIR, far_plane, 3)
     reduce_core(R, last)
-    sync()
-
-    reduce_near(R, own)
-    reduce_far(R, nxt)
+    add_near(R, own)
+    add_far(R, nxt)
+    sync()
+
+    send_near(R, own)
+    send_far(R, nxt)
     reduce_far(R, last)
     reduce_core(M, nxt)
     experts(far_plane)
@@ -994,70 +1020,70 @@
     sums = sums.reshape(len(PLANES), BLOCKS, local_experts, block_len)
     live[GATES] = [sums[:, :4], core(sums[:, 4:])]
     reduce_core(M, last)
+    add_near(R, last)
     sync()
 
     reduce_far(R, far_plane)
-    reduce_near(R, last)
-    reduce_near(R, nxt)
+    send_near(R, last)
+    add_near(R, nxt)
+    live[HOME] = reduced(R, own)
     sums = live[GATES][0] + live[GATES][1]
     crossed = jnp.stack([sums[:, 0], sums[:, 2], sums[:, 1], sums[:, 3]], axis=1)
     sums = jnp.where(odd_core == 0, sums, crossed)
-    live[GATES] = [sums[:, ::2], swap(sums[:, 1::2], ACROSS)]
+    sums = sums[:, ::2] + swap(sums[:, 1::2], ACROSS)
+    live[GATES] = [sums[:, 0], swap(sums[:, 1], ASIDE)]
     sync()
 
     live[RELAY] = swap(reduced(R, last), nxt)
     reduce_near(R, far_plane)
-    sums = live[GATES][0] + live[GATES][1]
-    sums = jnp.stack([sums[:, 0], swap(sums[:, 1], ASIDE)], axis=1)
+    sums = jnp.stack(live[GATES], axis=1)
     live[GATES] = [sums[::2], swap(sums[1::2], nxt)]
+    send_near(R, nxt)
+    add_far(M, nxt)
+    add_far(M, last)
+    sync()
+
+    live[RELAY] = swap(add(reduced(R, far_plane), live[RELAY]), far_plane)
+    live[SIDE] = swap(reduced(R, nxt), nxt)
+    send_far(M, nxt)
+    send_far(M, last)
     reduce_core(M, far_plane)
-    live[HOME] = reduced(R, own)
-    live[SIDE] = reduced(R, nxt)
-    sync()
-
-    live[RELAY] = swap(add(reduced(R, far_plane), live[RELAY]), far_plane)
-    live[SIDE] = swap(live[SIDE], nxt)
-    sums = jnp.stack(live[GATES], axis=1)
-    live[GATES] = [sums[0], swap(sums[1], far_plane)]
-    reduce_far(M, last)
-    reduce_far(M, far_plane)
-    sync()
-
-    grad_hidden_disp = live.pop(HOME).astype(wide) + live.pop(RELAY).astype(wide)
-    grad_hidden_disp = grad_hidden_disp + live.pop(SIDE).astype(wide)
-    sums = jnp.concatenate(live.pop(GATES), axis=0).reshape(-1, local_experts, block_len)
+    sums = jnp.stack(live.pop(GATES), axis=1)
+    sums = jnp.concatenate([sums[0], swap(sums[1], far_plane)], axis=0)
+    sums = sums.reshape(-1, local_experts, block_len)
     owner = lax.axis_index("expert").astype(jnp.uint32)
     sums = [lax.dynamic_slice_in_dim(sums, owner ^ r, 1, 0)[0] for r in range(sums.shape[0])]
     own_sums = jnp.concatenate(sums, axis=0).T
-    grad_out = cotangent.astype(wide)
     grad_gates = jnp.sum(jnp.where(matches, own_sums[:, None, :], 0.0), axis=2)
     grad_chosen = gate_weights * (
         grad_gates - jnp.sum(gate_weights * grad_gates, axis=-1, keepdims=True)
     )
     grad_logits = jnp.sum(jnp.where(matches, grad_chosen[:, :, None], 0.0), axis=1).astype(narrow)
     grad_router = jnp.einsum("ld,le->de", hidden_two, grad_logits, preferred_element_type=wide)
-    grad_hidden_two = grad_hidden_disp + jnp.einsum(
-        "le,de->ld", grad_logits, w_router, preferred_element_type=wide
-    )
+    live[GATES] = jnp.einsum("le,de->ld", grad_logits, w_router, preferred_element_type=wide)
+    live[SMALL] = grad_router
+    sync()
+
+    grad_hidden_two = live.pop(HOME).astype(wide) + live.pop(RELAY).astype(wide)
+    grad_hidden_two = grad_hidden_two + live.pop(SIDE).astype(wide) + live.pop(GATES)
+    grad_out = cotangent.astype(wide)
     grad_normed_two, grad_gain_moe = norm_backward(middle, inverse_two, gain_moe, grad_hidden_two)
     grad_middle = grad_out + grad_normed_two
     grad_attn = grad_middle.astype(narrow)
 
-    small = jnp.concatenate([grad_router, grad_gain_moe[:, None]], axis=1)
+    small = jnp.concatenate([live.pop(SMALL), grad_gain_moe[:, None]], axis=1)
     live[SMALL, FULL] = small.reshape(device_count, -1, small.shape[1])
     small_step = functools.partial(sum_step, SMALL, hops=small_hops, sent_as=wide)
 
     live[ATTN] = [grad_attn, core(grad_attn), swap(grad_attn, ACROSS)]
     small_step(0)
+    add_near(M, nxt)
+    add_near(M, last)
     sync()
     live[ATTN] = live[ATTN] + [core(live[ATTN][2])]
-    small_step(1)
     sync()
 
     grad_attn_all = jnp.concatenate(live.pop(ATTN), axis=0)
-    reduce_near(M, last)
-    reduce_near(M, far_plane)
-    small_step(2)
     live[OUT, FULL] = jnp.einsum(
         "lh,ld->hd", live[HEADS], grad_attn_all, preferred_element_type=wide
     )
@@ -1070,8 +1096,9 @@
     sync()
 
     grad_heads = live.pop(RAW)
-    live[MIXED] = swap(reduced(M, last), nxt)
-    reduce_far(M, nxt)
+    sum_step(OUT, 0)
+    small_step(1)
+    send_near(M, nxt)
     probability = jnp.exp(masked_scores() - live[TOTALS])
     grad_values = jnp.einsum(
         "hqk,qhd->khd", probability.astype(narrow), grad_heads, preferred_element_type=wide
@@ -1094,79 +1121,87 @@
         flat(rotate(grad_keys, cosine_table, -sine_table)),
         flat(grad_values),
     ]
-    sync()
+    flying = live.pop((OUT, GOT))
+    sync()
+    live[OUT, GOT] = flying
 
     def back(grad_raw, weights):
         return jnp.einsum("lh,dh->ld", grad_raw, weights, preferred_element_type=wide)
 
     raw = live.pop(RAW)
-    split_quarters(back(raw[0], w_query) + back(raw[1], w_key) + back(raw[2], w_value))
+    partial = back(raw[0], w_query) + back(raw[1], w_key) + back(raw[2], w_value)
+    split_quarters(partial)
+    live[GAIN] = partial
     live[IN, FULL] = jnp.einsum(
         "ld,lh->dh", hidden_one, jnp.concatenate(raw, axis=1), preferred_element_type=wide
     )
-    sum_step(OUT, 0)
     sum_step(OUT, 1)
-    live[MIXED] = swap(add(reduced(M, far_plane), live[MIXED]), far_plane)
-    reduce_near(M, nxt)
-    small_step(3)
+    small_step(2)
+    live[MIXED] = swap(reduced(M, nxt), nxt)
     sync()
 
     live[SENT] = core(live[SENT])
     sum_step(IN, 0)
     sum_step(OUT, 2)
-    small_step(4)
     some_weight_grads(0)
-    sync()
-
-    cross_quarters()
-    sum_step(IN, 1)
-    sum_step(OUT, 3)
-    small_step(5)
-    some_weight_grads(1)
-    sync()
-
-    grad_normed_one, grad_gain_attn = norm_backward(
-        own_inputs, own_inverse, gain_attn, quarter_sum()
-    )
-    live[TOKENS] = grad_middle + grad_normed_one
-    live[GAIN] = [grad_gain_attn[None], jnp.zeros_like(grad_gain_attn)[None]]
+    gain = jnp.sum(live.pop(GAIN) * inputs.astype(wide) * inverse_one, axis=0)
+    live[GAIN] = [gain[None], jnp.zeros_like(gain)[None]]
 
     def gain_step(step):
         live[GAIN] = [live[GAIN][0] + live[GAIN][1]]
         live[GAIN] = live[GAIN] + [swap(live[GAIN][0], *small_hops[step])]
 
+    small_step(3)
+    gain_step(0)
+    add_far(M, far_plane)
+    add_far(M, own)
+    sync()
+
+    sum_step(IN, 1)
+    cross_quarters()
+    sum_step(OUT, 3)
+    small_step(4)
+    gain_step(1)
+    some_weight_grads(1)
+    sync()
+
     sum_step(IN, 2)
+    own_grad = quarter_sum()
+    grad_normed_one = norm_backward(own_inputs, own_inverse, gain_attn, own_grad)[0]
+    live[TOKENS] = grad_middle + grad_normed_one
     sum_step(OUT, 4)
-    reduce_far(M, own)
-    live[SIDE] = swap(reduced(M, nxt), nxt)
-    small_step(6)
-    gain_step(0)
+    small_step(5)
+    send_near(M, last)
+    send_far(M, far_plane)
     some_weight_grads(2)
     sync()
 
     sum_step(IN, 3)
     sum_step(OUT, 5)
-    reduce_near(M, own)
-    small_step(7)
-    gain_step(1)
+    small_step(6)
+    live[RELAY] = swap(reduced(M, last), nxt)
+    reduce_near(M, far_plane)
     some_weight_grads(3)
     sync()
     for plane in PLANES:
         live.pop((KEPT, plane))
 
-    mixed_out = middle + reduced(M, own).astype(wide) + live.pop(MIXED).astype(wide)
-    live[MIXED] = (mixed_out + live.pop(SIDE).astype(wide)).astype(narrow)
+    sum_step(IN, 4)
     live[OUT] = summed(OUT)
-    sum_step(IN, 4)
+    live[RELAY] = swap(add(reduced(M, far_plane), live[RELAY]), far_plane)
+    send_far(M, own)
+    small_step(7)
     small_step(8)
     gain_step(2)
+    sync()
+
+    columns = local_heads * HD
+    sum_step(IN, 5)
+    small_step(9)
     gain_step(3)
-    sync()
-
-    columns = local_heads * HD
-    small_step(9)
     gain_step(4)
-    sum_step(IN, 5)
+    reduce_near(M, own)
+    live[MIXED] = middle + live.pop(MIXED).astype(wide) + live.pop(RELAY).astype(wide)
     even, odd = weight_hops[0]
     side = jnp.where(odd_core == 0, bit(even), bit(odd))
     half = live[IN, KEPT].shape[0]
@@ -1178,14 +1213,14 @@
     empty = jnp.zeros((2 * half, columns), wide)
     live[RAW] = [put(empty, live[IN, KEPT], index, side) for index in range(3)]
     sync()
+    mixed_out = (live.pop(MIXED) + reduced(M, own).astype(wide)).astype(narrow)
     grads_in = [put(whole, live[IN, GOT], i, 1 - side) for i, whole in enumerate(live[RAW])]
-    grad_gain_attn = (live[GAIN][0] + live[GAIN][1])[0]
     small = summed(SMALL, small_hops).reshape(model_width, -1)
 
     return (
-        live[MIXED],
+        mixed_out,
         live[TOKENS],
-        grad_gain_attn,
+        (live[GAIN][0] + live[GAIN][1])[0],
         *grads_in,
         live[OUT],
         small[:, expert_count],

time: 739 us -> 707 us (0.957)
  the two profiles are of different devices: /device:TPU:0 before, /device:TPU:1 now
where the time goes in v2:
time: 707 us; the launch traced here: 696 us
  waiting for transfers between devices  239 us (34%)
  Pallas kernels  165 us (23%)
  other arithmetic  109 us (15%)
  starting transfers between devices  102 us (14%)
  local copies, waits for them, and re-layouts  50.6 us (7%)
  matrix products  28 us (4%)
    ppermute x104, waiting for transfers between devices, swap(): return lax.ppermute(value, BOTH, perm)  239 us
    pallas_call x4, Pallas kernels, expert_chunk(): pl.pallas_call(functools.partial(expert_kernel, places, top_count), in_sp...  120 us
    ppermute x104, starting transfers between devices, swap(): return lax.ppermute(value, BOTH, perm)  102 us
    pallas_call x4, Pallas kernels, weight_grads(): pl.pallas_call(functools.partial(weight_kernel, parts, len(partial)), gri...  45.1 us
    convert_element_type x15, other arithmetic, add(): return (left.astype(wide) + right.astype(wide)).astype(narrow)  24.6 us
    convert_element_type x8, other arithmetic, add_near(): part.astype(narrow)  20.7 us
    unnamed x197, local copies, waits for them, and re-layouts  17.7 us
  transfers between devices with their start and end apart: 104, of which 32 were waited for; matrix products, arithmetic and copies ran while one was open for 18% of the time, Pallas kernels for 24%

profile of v2, /device:TPU:1, one launch (start us, length us, event | category | flops | bytes accessed | tf_op | source)
XLA Modules:
  0.0 696.3 jit_solution(4700050435636786073)
XLA Ops:
  36.4 9.3 %collective-permute-done.4 = bf16[64,2176]{1,0:T(8,128)(2,1)S(1)} collective-permute-done((bf16[64,2176]{1,0:T(8,128)(2,1)S(1)}, bf16[64,2176]{1,0:T(8,128)(2,1)S(1)}, u32[]{:S(2)}, u32[]{:S(2)}) %collective-permute-start.4) | collective-permute-done | bytes 278560 | tf_op jit(solution)/shard_map/ppermute | solution.py:691
  63.2 10.9 %collective-permute-done.10 = bf16[128,2048]{1,0:T(8,128)(2,1)S(1)} collective-permute-done((bf16[128,2048]{1,0:T(8,128)(2,1)S(1)}, bf16[128,2048]{1,0:T(8,128)(2,1)S(1)}, u32[]{:S(2)}, u32[]{:S(2)}) %collective-permute-start.10) | collective-permute-done | bytes 524320 | tf_op jit(solution)/shard_map/ppermute | solution.py:691
  78.9 7.5 %collective-permute-done.12.refs_1_ = bf16[128,2048]{1,0:T(8,128)(2,1)S(1)} collective-permute-done((bf16[128,2048]{1,0:T(8,128)(2,1)S(1)}, bf16[128,2048]{1,0:T(8,128)(2,1)S(1)}, u32[]{:S(2)}, u32[]{:S(2)}) %collective-permute-start.12) | collective-permute-done | bytes 524320 | tf_op jit(solution)/shard_map/ppermute | solution.py:691
  99.9 5.8 collective-permute-done.19
  120.0 6.3 collective-permute-done.20
  134.9 6.6 collective-permute-start.28
  141.5 30.2 %shard_map.220 = (bf16[512,2048]{1,0:T(8,128)(2,1)}, bf16[512,2048]{1,0:T(8,128)(2,1)}, bf16[512,2048]{1,0:T(8,128)(2,1)}, bf16[512,2048]{1,0:T(8,128)(2,1)}, f3...) custom-call(bf16[128,2048]{1,0:T(8,128)(2,1)} %copy-done.8, ...), custom_call_target="tpu_custom_call" | custom-call | flops 19327352832 | bytes 37748736 | tf_op jit(solution)/shard_map/pallas_call | solution.py:576
  179.8 30.0 %shard_map.221 = (bf16[512,2048]{1,0:T(8,128)(2,1)}, bf16[512,2048]{1,0:T(8,128)(2,1)}, bf16[512,2048]{1,0:T(8,128)(2,1)}, bf16[512,2048]{1,0:T(8,128)(2,1)}, f3...) custom-call(bf16[128,2048]{1,0:T(8,128)(2,1)} %copy-done.67, ...), custom_call_target="tpu_custom_call" | custom-call | flops 19327352832 | bytes 37748736 | tf_op jit(solution)/shard_map/pallas_call | solution.py:576
  209.8 6.1 collective-permute-done.29.refs_3_
  225.1 30.2 %shard_map.222 = (bf16[512,2048]{1,0:T(8,128)(2,1)}, bf16[512,2048]{1,0:T(8,128)(2,1)}, bf16[512,2048]{1,0:T(8,128)(2,1)}, bf16[512,2048]{1,0:T(8,128)(2,1)}, f3...) custom-call(bf16[128,4224]{1,0:T(8,128)(2,1)} %pad_maximum_fusion.7., ...), custom_call_target="tpu_custom_call" | custom-call | flops 19327352832 | bytes 37748736 | tf_op jit(solution)/shard_map/pallas_call | solution.py:576
  266.2 30.0 %shard_map.223 = (bf16[512,2048]{1,0:T(8,128)(2,1)}, bf16[512,2048]{1,0:T(8,128)(2,1)}, bf16[512,2048]{1,0:T(8,128)(2,1)}, bf16[512,2048]{1,0:T(8,128)(2,1)}, f3...) custom-call(bf16[128,4224]{1,0:T(8,128)(2,1)} %constant_dynamic-upda, ...), custom_call_target="tpu_custom_call" | custom-call | flops 19327352832 | bytes 37748736 | tf_op jit(solution)/shard_map/pallas_call | solution.py:576
  310.5 16.3 %collective-permute-done.49 = f32[4,2,8,128]{3,2,1,0:T(8,128)S(1)} collective-permute-done((f32[4,2,8,128]{3,2,1,0:T(8,128)S(1)}, f32[4,2,8,128]{3,2,1,0:T(8,128)S(1)}, u32[]{:S(2)}, u32[]{:S(2)}) %collective-permute-start.49) | collective-permute-done | bytes 32800 | tf_op jit(solution)/shard_map/ppermute | solution.py:691
  339.8 5.3 collective-permute-done.53
  356.9 13.6 %collective-permute-done.60 = bf16[128,2048]{1,0:T(8,128)(2,1)} collective-permute-done((bf16[128,2048]{1,0:T(8,128)(2,1)}, bf16[128,2048]{1,0:T(8,128)(2,1)}, u32[]{:S(2)}, u32[]{:S(2)}) %collective-permute-start.60) | collective-permute-done | bytes 524320 | tf_op jit(solution)/shard_map/ppermute | solution.py:691
  438.6 7.4 %collective-permute-done.70 = bf16[128,2048]{1,0:T(8,128)(2,1)S(1)} collective-permute-done((bf16[128,2048]{1,0:T(8,128)(2,1)S(1)}, bf16[128,2048]{1,0:T(8,128)(2,1)S(1)}, u32[]{:S(2)}, u32[]{:S(2)}) %collective-permute-start.70) | collective-permute-done | bytes 524320 | tf_op jit(solution)/shard_map/ppermute | solution.py:691
  460.6 11.4 %shard_map.224 = (f32[8,2048,256]{2,1,0:T(8,128)}, f32[8,2048,256]{2,1,0:T(8,128)}, f32[8,256,2048]{2,1,0:T(8,128)}) custom-call(bf16[8,192,2048]{2,1,0:T(8,128)(2,1)} %get-tuple-element.1720.refs_0_, bf16[8,192,2048]{2,1,0:T(8,128)(2,1)} %get-tuple-element.1724.refs_1_, bf16[8,192,2048]{2,1,0:T(8,128)(2,1)} %get-tuple-element.1733.refs_2_, ...), custom_call_target="tpu_custom_call" | custom-call | flops 4831838208 | bytes 27525120 | tf_op jit(solution)/shard_map/pallas_call | solution.py:638
  475.3 14.8 %collective-permute-done.75 = bf16[64,2048]{1,0:T(8,128)(2,1)} collective-permute-done((bf16[64,2048]{1,0:T(8,128)(2,1)S(1)}, bf16[64,2048]{1,0:T(8,128)(2,1)}, u32[]{:S(2)}, u32[]{:S(2)}) %collective-permute-start.75) | collective-permute-done | bytes 262176 | tf_op jit(solution)/shard_map/ppermute | solution.py:691
  502.4 11.2 %shard_map.225 = (f32[8,2048,256]{2,1,0:T(8,128)}, f32[8,2048,256]{2,1,0:T(8,128)}, f32[8,256,2048]{2,1,0:T(8,128)}) custom-call(bf16[8,192,2048]{2,1,0:T(8,128)(2,1)} %get-tuple-element.1720.refs_0_, bf16[8,192,2048]{2,1,0:T(8,128)(2,1)} %get-tuple-element.1724.refs_1_, ...), custom_call_target="tpu_custom_call", output_to_operand_aliasing={{0}: (16, {}), {1}: (17, {}), {2}: (18, {})} | custom-call | flops 4831838208 | bytes 27525120 | tf_op jit(solution)/shard_map/pallas_call | solution.py:638
  527.4 11.2 %shard_map.226 = (f32[8,2048,256]{2,1,0:T(8,128)}, f32[8,2048,256]{2,1,0:T(8,128)}, f32[8,256,2048]{2,1,0:T(8,128)}) custom-call(bf16[8,192,2048]{2,1,0:T(8,128)(2,1)} %get-tuple-element.1720.refs_0_, bf16[8,192,2048]{2,1,0:T(8,128)(2,1)} %get-tuple-element.1724.refs_1_, ...), custom_call_target="tpu_custom_call", output_to_operand_aliasing={{0}: (16, {}), {1}: (17, {}), {2}: (18, {})} | custom-call | flops 4831838208 | bytes 27525120 | tf_op jit(solution)/shard_map/pallas_call | solution.py:638
  538.8 19.4 %collective-permute-done.85 = bf16[256,1536]{1,0:T(8,128)(2,1)} collective-permute-done((bf16[256,1536]{1,0:T(8,128)(2,1)}, bf16[256,1536]{1,0:T(8,128)(2,1)}, u32[]{:S(2)}, u32[]{:S(2)}) %collective-permute-start.85) | collective-permute-done | bytes 786464 | tf_op jit(solution)/shard_map/ppermute | solution.py:691
  567.8 11.4 %shard_map.227 = (f32[8,2048,256]{2,1,0:T(8,128)}, f32[8,2048,256]{2,1,0:T(8,128)}, f32[8,256,2048]{2,1,0:T(8,128)}) custom-call(bf16[8,192,2048]{2,1,0:T(8,128)(2,1)} %get-tuple-element.1720.refs_0_, bf16[8,192,2048]{2,1,0:T(8,128)(2,1)} %get-tuple-element.1724.refs_1_, ...), custom_call_target="tpu_custom_call", output_to_operand_aliasing={{0}: (16, {}), {1}: (17, {}), {2}: (18, {})} | custom-call | flops 4831838208 | bytes 27525120 | tf_op jit(solution)/shard_map/pallas_call | solution.py:638
  579.2 26.9 %collective-permute-done.90 = f32[2,64,65]{2,1,0:T(8,128)S(1)} collective-permute-done((f32[2,64,65]{2,1,0:T(8,128)S(1)}, f32[2,64,65]{2,1,0:T(8,128)S(1)}, u32[]{:S(2)}, u32[]{:S(2)}) %collective-permute-start.90) | collective-permute-done | bytes 33312 | tf_op jit(solution)/shard_map/ppermute | solution.py:691
  610.9 24.8 %collective-permute-done.97 = f32[4,64,65]{2,1,0:T(8,128)S(1)} collective-permute-done((f32[4,64,65]{2,1,0:T(8,128)S(1)}, f32[4,64,65]{2,1,0:T(8,128)S(1)}, u32[]{:S(2)}, u32[]{:S(2)}) %collective-permute-start.97) | collective-permute-done | bytes 66592 | tf_op jit(solution)/shard_map/ppermute | solution.py:691
  654.3 25.3 %collective-permute-done.99 = f32[1,2048]{1,0:T(1,128)S(1)} collective-permute-done((f32[1,2048]{1,0:T(1,128)S(1)}, f32[1,2048]{1,0:T(1,128)S(1)}, u32[]{:S(2)}, u32[]{:S(2)}) %collective-permute-start.99) | collective-permute-done | bytes 8224 | tf_op jit(solution)/shard_map/ppermute | solution.py:691
  (597 shorter events, 321.4 us)
Async XLA Ops:
  129.8 41.9 %collective-permute-start.24 = (bf16[512,2048]{1,0:T(8,128)(2,1)}, bf16[512,2048]{1,0:T(8,128)(2,1)}, u32[]{:S(2)}, u32[]{:S(2)}) collective-permute-start(bf16[512,2048]{1,0:T(8,128)(2,1)} %pad_maximum_fusion.6), channel_id=1, source_target_pairs={{0,1},{1,0},{2,3},{3,2},{4,5},{5,4},{6,7},{7,6},{8,9},{9,8},{10,11... | collective-permute-start | bytes 6291464 | tf_op jit(solution)/shard_map/ppermute | solution.py:691
  132.7 39.0 %collective-permute-start.25 = (bf16[128,4224]{1,0:T(8,128)(2,1)}, bf16[128,4224]{1,0:T(8,128)(2,1)}, u32[]{:S(2)}, u32[]{:S(2)}) collective-permute-start(bf16[128,4224]{1,0:T(8,128)(2,1)} %pad_maximum_fusion.7.refs_0_), channel_id=1, source_target_pairs={{0,2},{1,5},{2,0},{3,7},{4,6},{5,1},{6,4},{7,3},{8,10},{9,13},{10,... | collective-permute-start | bytes 3244040 | tf_op jit(solution)/shard_map/ppermute | solution.py:691
  133.4 38.3 %collective-permute-start.26 = (bf16[128,4224]{1,0:T(8,128)(2,1)}, bf16[128,4224]{1,0:T(8,128)(2,1)}, u32[]{:S(2)}, u32[]{:S(2)}) collective-permute-start(bf16[128,4224]{1,0:T(8,128)(2,1)} %pad_maximum_fusion.7.refs_0_), channel_id=1, source_target_pairs={{0,4},{1,3},{2,6},{3,1},{4,0},{5,7},{6,2},{7,5},{8,12},{9,11},{10,... | collective-permute-start | bytes 3244040 | tf_op jit(solution)/shard_map/ppermute | solution.py:691
  134.3 37.4 %collective-permute-start.27 = (bf16[128,4224]{1,0:T(8,128)(2,1)}, bf16[128,4224]{1,0:T(8,128)(2,1)}, u32[]{:S(2)}, u32[]{:S(2)}) collective-permute-start(bf16[128,4224]{1,0:T(8,128)(2,1)} %pad_maximum_fusion.7.refs_0_), channel_id=1, source_target_pairs={{0,1},{1,0},{2,3},{3,2},{4,5},{5,4},{6,7},{7,6},{8,9},{9,8},{10,11... | collective-permute-start | bytes 3244040 | tf_op jit(solution)/shard_map/ppermute | solution.py:691
  134.9 36.8 %collective-permute-start.28 = (bf16[128,2048]{1,0:T(8,128)(2,1)S(1)}, bf16[128,2048]{1,0:T(8,128)(2,1)}, u32[]{:S(2)}, u32[]{:S(2)}) collective-permute-start(bf16[128,2048]{1,0:T(8,128)(2,1)S(1)} %multiply_convert_fusion.1.refs_0_), channel_id=1, source_target_pairs={{0,16},{1,17},{2,18},{3,19},{4,20},{5,21},{6,22},{7,23},{8,24},{9,... | collective-permute-start | bytes 1572872 | tf_op jit(solution)/shard_map/ppermute | solution.py:691
  176.7 39.2 %collective-permute-start.30 = (bf16[256,4224]{1,0:T(8,128)(2,1)}, bf16[256,4224]{1,0:T(8,128)(2,1)}, u32[]{:S(2)}, u32[]{:S(2)}) collective-permute-start(bf16[256,4224]{1,0:T(8,128)(2,1)} %pad_maximum_fusion.3), channel_id=1, source_target_pairs={{0,1},{1,0},{2,3},{3,2},{4,5},{5,4},{6,7},{7,6},{8,9},{9,8},{10,11... | collective-permute-start | bytes 6488072 | tf_op jit(solution)/shard_map/ppermute | solution.py:691
  177.0 38.9 %collective-permute-start.33 = (bf16[512,2048]{1,0:T(8,128)(2,1)}, bf16[512,2048]{1,0:T(8,128)(2,1)}, u32[]{:S(2)}, u32[]{:S(2)}) collective-permute-start(bf16[512,2048]{1,0:T(8,128)(2,1)} %get-tuple-element.1081), channel_id=1, source_target_pairs={{0,1},{1,0},{2,3},{3,2},{4,5},{5,4},{6,7},{7,6},{8,9},{9,8},{10,11... | collective-permute-start | bytes 6291464 | tf_op jit(solution)/shard_map/ppermute | solution.py:691
  178.9 37.0 %collective-permute-start.29 = (bf16[128,4224]{1,0:T(8,128)(2,1)}, bf16[128,4224]{1,0:T(8,128)(2,1)}, u32[]{:S(2)}, u32[]{:S(2)}) collective-permute-start(bf16[128,4224]{1,0:T(8,128)(2,1)} %collective-permute-done.25.refs_1_), channel_id=1, source_target_pairs={{0,4},{1,3},{2,6},{3,1},{4,0},{5,7},{6,2},{7,5},{8,12},{9,11},{10,... | collective-permute-start | bytes 3244040 | tf_op jit(solution)/shard_map/ppermute | solution.py:691
  262.5 33.8 %collective-permute-start.45 = (bf16[512,2048]{1,0:T(8,128)(2,1)}, bf16[512,2048]{1,0:T(8,128)(2,1)}, u32[]{:S(2)}, u32[]{:S(2)}) collective-permute-start(bf16[512,2048]{1,0:T(8,128)(2,1)} %get-tuple-element.1255), channel_id=1, source_target_pairs={{0,1},{1,0},{2,3},{3,2},{4,5},{5,4},{6,7},{7,6},{8,9},{9,8},{10,11... | collective-permute-start | bytes 6291464 | tf_op jit(solution)/shard_map/ppermute | solution.py:691
  448.1 42.8 %collective-permute-start.74 = (bf16[1024,1536]{1,0:T(8,128)(2,1)}, bf16[1024,1536]{1,0:T(8,128)(2,1)}, u32[]{:S(2)}, u32[]{:S(2)}) collective-permute-start(bf16[1024,1536]{1,0:T(8,128)(2,1)} %dynamic-slice_convert_fusion), channel_id=1, source_target_pairs={{0,4},{1,9},{2,6},{3,11},{4,0},{5,13},{6,2},{7,15},{8,12},{9,1},{1... | collective-permute-start | bytes 9437192 | tf_op jit(solution)/shard_map/ppermute | solution.py:691
  449.7 40.4 %collective-permute-start.75 = (bf16[64,2048]{1,0:T(8,128)(2,1)S(1)}, bf16[64,2048]{1,0:T(8,128)(2,1)}, u32[]{:S(2)}, u32[]{:S(2)}) collective-permute-start(bf16[64,2048]{1,0:T(8,128)(2,1)S(1)} %dynamic-slice_convert_fusion.5), channel_id=1, source_target_pairs={{0,16},{1,17},{2,18},{3,19},{4,20},{5,21},{6,22},{7,23},{8,24},{9,... | collective-permute-start | bytes 786440 | tf_op jit(solution)/shard_map/ppermute | solution.py:691
  455.5 34.7 %collective-permute-start.73 = (bf16[2,128,2048]{2,1,0:T(8,128)(2,1)S(1)}, bf16[2,128,2048]{2,1,0:T(8,128)(2,1)S(1)}, u32[]{:S(2)}, u32[]{:S(2)}) collective-permute-start(bf16[2,128,2048]{2,1,0:T(8,128)(2,1)S(1)} %pad_maximum_fusion.9), channel_id=1, source_target_pairs={{0,1},{1,0},{2,3},{3,2},{4,5},{5,4},{6,7},{7,6},{8,9},{9,8},{10,11... | collective-permute-start | bytes 3145736 | tf_op jit(solution)/shard_map/ppermute | solution.py:691
  523.2 34.9 %collective-permute-start.85 = (bf16[256,1536]{1,0:T(8,128)(2,1)}, bf16[256,1536]{1,0:T(8,128)(2,1)}, u32[]{:S(2)}, u32[]{:S(2)}) collective-permute-start(bf16[256,1536]{1,0:T(8,128)(2,1)} %dynamic-slice_convert_fusion.3), channel_id=1, source_target_pairs={{0,16},{1,17},{2,18},{3,19},{4,20},{5,21},{6,22},{7,23},{8,24},{9,... | collective-permute-start | bytes 2359304 | tf_op jit(solution)/shard_map/ppermute | solution.py:691
  524.8 33.4 %collective-permute-start.84 = (bf16[2,128,2048]{2,1,0:T(8,128)(2,1)}, bf16[2,128,2048]{2,1,0:T(8,128)(2,1)}, u32[]{:S(2)}, u32[]{:S(2)}) collective-permute-start(bf16[2,128,2048]{2,1,0:T(8,128)(2,1)} %bitcast.72), channel_id=1, source_target_pairs={{0,4},{1,3},{2,6},{3,1},{4,0},{5,7},{6,2},{7,5},{8,12},{9,11},{10,... | collective-permute-start | bytes 3145736 | tf_op jit(solution)/shard_map/ppermute | solution.py:691
  560.3 45.8 %collective-permute-start.92 = (bf16[128,2048]{1,0:T(8,128)(2,1)S(1)}, bf16[128,2048]{1,0:T(8,128)(2,1)S(1)}, u32[]{:S(2)}, u32[]{:S(2)}) collective-permute-start(bf16[128,2048]{1,0:T(8,128)(2,1)S(1)} %get-tuple-element.1823), channel_id=1, source_target_pairs={{0,2},{1,5},{2,0},{3,7},{4,6},{5,1},{6,4},{7,3},{8,10},{9,13},{10,... | collective-permute-start | bytes 1572872 | tf_op jit(solution)/shard_map/ppermute | solution.py:691
  562.0 44.1 %collective-permute-start.89 = (bf16[256,2048]{1,0:T(8,128)(2,1)S(1)}, bf16[256,2048]{1,0:T(8,128)(2,1)S(1)}, u32[]{:S(2)}, u32[]{:S(2)}) collective-permute-start(bf16[256,2048]{1,0:T(8,128)(2,1)S(1)} %constant_dynamic-update-slice_fusion.30), channel_id=1, source_target_pairs={{0,4},{1,9},{2,6},{3,11},{4,0},{5,13},{6,2},{7,15},{8,12},{9,1},{1... | collective-permute-start | bytes 3145736 | tf_op jit(solution)/shard_map/ppermute | solution.py:691
  563.4 42.6 %collective-permute-start.88 = (bf16[256,1536]{1,0:T(8,128)(2,1)S(1)}, bf16[256,1536]{1,0:T(8,128)(2,1)S(1)}, u32[]{:S(2)}, u32[]{:S(2)}) collective-permute-start(bf16[256,1536]{1,0:T(8,128)(2,1)S(1)} %add_convert_fusion.8), channel_id=1, source_target_pairs={{0,16},{1,17},{2,18},{3,19},{4,20},{5,21},{6,22},{7,23},{8,24},{9,... | collective-permute-start | bytes 2359304 | tf_op jit(solution)/shard_map/ppermute | solution.py:691
  566.2 39.9 %collective-permute-start.91 = (bf16[128,2048]{1,0:T(8,128)(2,1)S(1)}, bf16[128,2048]{1,0:T(8,128)(2,1)S(1)}, u32[]{:S(2)}, u32[]{:S(2)}) collective-permute-start(bf16[128,2048]{1,0:T(8,128)(2,1)S(1)} %add_convert_fusion.13), channel_id=1, source_target_pairs={{0,8},{1,9},{2,10},{3,11},{4,12},{5,13},{6,14},{7,15},{8,0},{9,1},... | collective-permute-start | bytes 1572872 | tf_op jit(solution)/shard_map/ppermute | solution.py:691
  566.3 39.8 %collective-permute-start.90 = (f32[2,64,65]{2,1,0:T(8,128)S(1)}, f32[2,64,65]{2,1,0:T(8,128)S(1)}, u32[]{:S(2)}, u32[]{:S(2)}) collective-permute-start(f32[2,64,65]{2,1,0:T(8,128)S(1)} %constant_dynamic-update-slice_fusion.28), channel_id=1, source_target_pairs={{0,8},{1,9},{2,10},{3,11},{4,12},{5,13},{6,14},{7,15},{8,0},{9,1},... | collective-permute-start | bytes 99848 | tf_op jit(solution)/shard_map/ppermute | solution.py:691
  606.3 34.9 %collective-permute-start.96 = (bf16[512,1536]{1,0:T(8,128)(2,1)S(1)}, bf16[512,1536]{1,0:T(8,128)(2,1)S(1)}, u32[]{:S(2)}, u32[]{:S(2)}) collective-permute-start(bf16[512,1536]{1,0:T(8,128)(2,1)S(1)} %constant_dynamic-update-slice_fusion.26), channel_id=1, source_target_pairs={{0,8},{1,5},{2,10},{3,7},{4,12},{5,1},{6,14},{7,3},{8,0},{9,13},{1... | collective-permute-start | bytes 4718600 | tf_op jit(solution)/shard_map/ppermute | solution.py:691
  608.0 33.3 %collective-permute-start.94 = (bf16[2,128,2048]{2,1,0:T(8,128)(2,1)S(1)}, bf16[2,128,2048]{2,1,0:T(8,128)(2,1)S(1)}, u32[]{:S(2)}, u32[]{:S(2)}) collective-permute-start(bf16[2,128,2048]{2,1,0:T(8,128)(2,1)S(1)} %bitcast.226), channel_id=1, source_target_pairs={{0,4},{1,3},{2,6},{3,1},{4,0},{5,7},{6,2},{7,5},{8,12},{9,11},{10,... | collective-permute-start | bytes 3145736 | tf_op jit(solution)/shard_map/ppermute | solution.py:691
  641.9 41.2 %collective-permute-start.101 = (bf16[1024,1536]{1,0:T(8,128)(2,1)S(1)}, bf16[1024,1536]{1,0:T(8,128)(2,1)S(1)}, u32[]{:S(2)}, u32[]{:S(2)}) collective-permute-start(bf16[1024,1536]{1,0:T(8,128)(2,1)S(1)} %constant_dynamic-update-slice_fusion.18), channel_id=1, source_target_pairs={{0,4},{1,9},{2,6},{3,11},{4,0},{5,13},{6,2},{7,15},{8,12},{9,1},{1... | collective-permute-start | bytes 9437192 | tf_op jit(solution)/shard_map/ppermute | solution.py:691
  647.2 35.9 %collective-permute-start.103 = (bf16[128,2048]{1,0:T(8,128)(2,1)S(1)}, bf16[128,2048]{1,0:T(8,128)(2,1)S(1)}, u32[]{:S(2)}, u32[]{:S(2)}) collective-permute-start(bf16[128,2048]{1,0:T(8,128)(2,1)S(1)} %get-tuple-element.1821), channel_id=1, source_target_pairs={{0,2},{1,5},{2,0},{3,7},{4,6},{5,1},{6,4},{7,3},{8,10},{9,13},{10,... | collective-permute-start | bytes 1572872 | tf_op jit(solution)/shard_map/ppermute | solution.py:691
  648.4 34.6 %collective-permute-start.102 = (f32[16,64,65]{2,1,0:T(8,128)S(1)}, f32[16,64,65]{2,1,0:T(8,128)S(1)}, u32[]{:S(2)}, u32[]{:S(2)}) collective-permute-start(f32[16,64,65]{2,1,0:T(8,128)S(1)} %constant_dynamic-update-slice_fusion.16), channel_id=1, source_target_pairs={{0,1},{1,0},{2,3},{3,2},{4,5},{5,4},{6,7},{7,6},{8,9},{9,8},{10,11... | collective-permute-start | bytes 798728 | tf_op jit(solution)/shard_map/ppermute | solution.py:691
  (174 other events, 2544.8 us)

commit v3 on v2

--- a/solution.py
+++ b/solution.py
@@ -1097,7 +1097,6 @@
 
     grad_heads = live.pop(RAW)
     sum_step(OUT, 0)
-    small_step(1)
     send_near(M, nxt)
     probability = jnp.exp(masked_scores() - live[TOTALS])
     grad_values = jnp.einsum(
@@ -1136,6 +1135,7 @@
         "ld,lh->dh", hidden_one, jnp.concatenate(raw, axis=1), preferred_element_type=wide
     )
     sum_step(OUT, 1)
+    small_step(1)
     small_step(2)
     live[MIXED] = swap(reduced(M, nxt), nxt)
     sync()
@@ -1161,6 +1161,7 @@
     cross_quarters()
     sum_step(OUT, 3)
     small_step(4)
+    small_step(5)
     gain_step(1)
     some_weight_grads(1)
     sync()
@@ -1170,7 +1171,7 @@
     grad_normed_one = norm_backward(own_inputs, own_inverse, gain_attn, own_grad)[0]
     live[TOKENS] = grad_middle + grad_normed_one
     sum_step(OUT, 4)
-    small_step(5)
+    small_step(6)
     send_near(M, last)
     send_far(M, far_plane)
     some_weight_grads(2)
@@ -1178,9 +1179,10 @@
 
     sum_step(IN, 3)
     sum_step(OUT, 5)
-    small_step(6)
+    small_step(7)
     live[RELAY] = swap(reduced(M, last), nxt)
     reduce_near(M, far_plane)
+    send_far(M, own)
     some_weight_grads(3)
     sync()
     for plane in PLANES:
@@ -1189,19 +1191,20 @@
     sum_step(IN, 4)
     live[OUT] = summed(OUT)
     live[RELAY] = swap(add(reduced(M, far_plane), live[RELAY]), far_plane)
-    send_far(M, own)
-    small_step(7)
+    reduce_near(M, own)
     small_step(8)
+    small_step(9)
     gain_step(2)
     sync()
 
     columns = local_heads * HD
     sum_step(IN, 5)
-    small_step(9)
     gain_step(3)
     gain_step(4)
-    reduce_near(M, own)
-    live[MIXED] = middle + live.pop(MIXED).astype(wide) + live.pop(RELAY).astype(wide)
+    small = summed(SMALL, small_hops).reshape(model_width, -1)
+    live[SMALL] = [small[:, :expert_count], small[:, expert_count]]
+    mixed_out = middle + reduced(M, own).astype(wide) + live.pop(MIXED).astype(wide)
+    live[MIXED] = (mixed_out + live.pop(RELAY).astype(wide)).astype(narrow)
     even, odd = weight_hops[0]
     side = jnp.where(odd_core == 0, bit(even), bit(odd))
     half = live[IN, KEPT].shape[0]
@@ -1213,18 +1216,16 @@
     empty = jnp.zeros((2 * half, columns), wide)
     live[RAW] = [put(empty, live[IN, KEPT], index, side) for index in range(3)]
     sync()
-    mixed_out = (live.pop(MIXED) + reduced(M, own).astype(wide)).astype(narrow)
     grads_in = [put(whole, live[IN, GOT], i, 1 - side) for i, whole in enumerate(live[RAW])]
-    small = summed(SMALL, small_hops).reshape(model_width, -1)
 
     return (
-        mixed_out,
+        live[MIXED],
         live[TOKENS],
         (live[GAIN][0] + live[GAIN][1])[0],
         *grads_in,
         live[OUT],
-        small[:, expert_count],
-        small[:, :expert_count],
+        live[SMALL][1],
+        live[SMALL][0],
         *live[EXPERTS],
     )
 

time: 707 us -> 703 us (level)
  the two profiles are of different devices: /device:TPU:1 before, /device:TPU:0 now
where the time goes in v3:
time: 703 us; the launch traced here: 690 us
  waiting for transfers between devices  220 us (31%)
  Pallas kernels  165 us (23%)
  other arithmetic  112 us (16%)
  starting transfers between devices  110 us (16%)
  local copies, waits for them, and re-layouts  52.1 us (7%)
  matrix products  28 us (4%)
    ppermute x104, waiting for transfers between devices, swap(): return lax.ppermute(value, BOTH, perm)  220 us
    pallas_call x4, Pallas kernels, expert_chunk(): pl.pallas_call(functools.partial(expert_kernel, places, top_count), in_sp...  120 us
    ppermute x104, starting transfers between devices, swap(): return lax.ppermute(value, BOTH, perm)  110 us
    pallas_call x4, Pallas kernels, weight_grads(): pl.pallas_call(functools.partial(weight_kernel, parts, len(partial)), gri...  45.1 us
    convert_element_type x15, other arithmetic, add(): return (left.astype(wide) + right.astype(wide)).astype(narrow)  25.9 us
    convert_element_type x8, other arithmetic, add_near(): part.astype(narrow)  20.7 us
    unnamed x201, local copies, waits for them, and re-layouts  17.2 us
  transfers between devices with their start and end apart: 104, of which 35 were waited for; matrix products, arithmetic and copies ran while one was open for 19% of the time, Pallas kernels for 24%

profile of v3, /device:TPU:0, one launch (start us, length us, event | category | flops | bytes accessed | tf_op | source)
XLA Modules:
  0.0 690.4 jit_solution(578654949479732072)
XLA Ops:
  38.9 9.4 %collective-permute-done.4 = bf16[64,2176]{1,0:T(8,128)(2,1)S(1)} collective-permute-done((bf16[64,2176]{1,0:T(8,128)(2,1)S(1)}, bf16[64,2176]{1,0:T(8,128)(2,1)S(1)}, u32[]{:S(2)}, u32[]{:S(2)}) %collective-permute-start.4) | collective-permute-done | bytes 278560 | tf_op jit(solution)/shard_map/ppermute | solution.py:691
  55.7 5.4 collective-permute-done.9.refs_8_
  64.7 11.5 %collective-permute-done.10 = bf16[128,2048]{1,0:T(8,128)(2,1)S(1)} collective-permute-done((bf16[128,2048]{1,0:T(8,128)(2,1)S(1)}, bf16[128,2048]{1,0:T(8,128)(2,1)S(1)}, u32[]{:S(2)}, u32[]{:S(2)}) %collective-permute-start.10) | collective-permute-done | bytes 524320 | tf_op jit(solution)/shard_map/ppermute | solution.py:691
  81.9 10.0 %collective-permute-done.12.refs_1_ = bf16[128,2048]{1,0:T(8,128)(2,1)S(1)} collective-permute-done((bf16[128,2048]{1,0:T(8,128)(2,1)S(1)}, bf16[128,2048]{1,0:T(8,128)(2,1)S(1)}, u32[]{:S(2)}, u32[]{:S(2)}) %collective-permute-start.12) | collective-permute-done | bytes 524320 | tf_op jit(solution)/shard_map/ppermute | solution.py:691
  100.2 7.1 %collective-permute-done.19 = bf16[64,2048]{1,0:T(8,128)(2,1)S(1)} collective-permute-done((bf16[64,2048]{1,0:T(8,128)(2,1)S(1)}, bf16[64,2048]{1,0:T(8,128)(2,1)S(1)}, u32[]{:S(2)}, u32[]{:S(2)}) %collective-permute-start.19) | collective-permute-done | bytes 262176 | tf_op jit(solution)/shard_map/ppermute | solution.py:691
  121.6 6.3 collective-permute-done.20
  134.8 6.9 collective-permute-start.28
  141.6 30.2 %shard_map.220 = (bf16[512,2048]{1,0:T(8,128)(2,1)}, bf16[512,2048]{1,0:T(8,128)(2,1)}, bf16[512,2048]{1,0:T(8,128)(2,1)}, bf16[512,2048]{1,0:T(8,128)(2,1)}, f3...) custom-call(bf16[128,2048]{1,0:T(8,128)(2,1)} %copy-done.8, ...), custom_call_target="tpu_custom_call" | custom-call | flops 19327352832 | bytes 37748736 | tf_op jit(solution)/shard_map/pallas_call | solution.py:576
  181.2 30.0 %shard_map.221 = (bf16[512,2048]{1,0:T(8,128)(2,1)}, bf16[512,2048]{1,0:T(8,128)(2,1)}, bf16[512,2048]{1,0:T(8,128)(2,1)}, bf16[512,2048]{1,0:T(8,128)(2,1)}, f3...) custom-call(bf16[128,2048]{1,0:T(8,128)(2,1)} %copy-done.72, ...), custom_call_target="tpu_custom_call" | custom-call | flops 19327352832 | bytes 37748736 | tf_op jit(solution)/shard_map/pallas_call | solution.py:576
  226.0 30.2 %shard_map.222 = (bf16[512,2048]{1,0:T(8,128)(2,1)}, bf16[512,2048]{1,0:T(8,128)(2,1)}, bf16[512,2048]{1,0:T(8,128)(2,1)}, bf16[512,2048]{1,0:T(8,128)(2,1)}, f3...) custom-call(bf16[128,4224]{1,0:T(8,128)(2,1)} %pad_maximum_fusion.7., ...), custom_call_target="tpu_custom_call" | custom-call | flops 19327352832 | bytes 37748736 | tf_op jit(solution)/shard_map/pallas_call | solution.py:576
  267.5 30.0 %shard_map.223 = (bf16[512,2048]{1,0:T(8,128)(2,1)}, bf16[512,2048]{1,0:T(8,128)(2,1)}, bf16[512,2048]{1,0:T(8,128)(2,1)}, bf16[512,2048]{1,0:T(8,128)(2,1)}, f3...) custom-call(bf16[128,4224]{1,0:T(8,128)(2,1)} %constant_dynamic-upda, ...), custom_call_target="tpu_custom_call" | custom-call | flops 19327352832 | bytes 37748736 | tf_op jit(solution)/shard_map/pallas_call | solution.py:576
  311.6 11.3 %collective-permute-done.49 = f32[4,2,8,128]{3,2,1,0:T(8,128)S(1)} collective-permute-done((f32[4,2,8,128]{3,2,1,0:T(8,128)S(1)}, f32[4,2,8,128]{3,2,1,0:T(8,128)S(1)}, u32[]{:S(2)}, u32[]{:S(2)}) %collective-permute-start.49) | collective-permute-done | bytes 32800 | tf_op jit(solution)/shard_map/ppermute | solution.py:691
  338.9 5.3 collective-permute-done.53
  358.1 12.5 %collective-permute-done.60 = bf16[128,2048]{1,0:T(8,128)(2,1)} collective-permute-done((bf16[128,2048]{1,0:T(8,128)(2,1)}, bf16[128,2048]{1,0:T(8,128)(2,1)}, u32[]{:S(2)}, u32[]{:S(2)}) %collective-permute-start.60) | collective-permute-done | bytes 524320 | tf_op jit(solution)/shard_map/ppermute | solution.py:691
  458.0 11.3 %shard_map.224 = (f32[8,2048,256]{2,1,0:T(8,128)}, f32[8,2048,256]{2,1,0:T(8,128)}, f32[8,256,2048]{2,1,0:T(8,128)}) custom-call(bf16[8,192,2048]{2,1,0:T(8,128)(2,1)} %get-tuple-element.1717.refs_0_, bf16[8,192,2048]{2,1,0:T(8,128)(2,1)} %get-tuple-element.1721.refs_1_, bf16[8,192,2048]{2,1,0:T(8,128)(2,1)} %get-tuple-element.1730.refs_2_, ...), custom_call_target="tpu_custom_call" | custom-call | flops 4831838208 | bytes 27525120 | tf_op jit(solution)/shard_map/pallas_call | solution.py:638
  472.6 11.3 %collective-permute-done.74 = bf16[1024,1536]{1,0:T(8,128)(2,1)} collective-permute-done((bf16[1024,1536]{1,0:T(8,128)(2,1)}, bf16[1024,1536]{1,0:T(8,128)(2,1)}, u32[]{:S(2)}, u32[]{:S(2)}) %collective-permute-start.74) | collective-permute-done | bytes 3145760 | tf_op jit(solution)/shard_map/ppermute | solution.py:691
  495.9 11.2 %shard_map.225 = (f32[8,2048,256]{2,1,0:T(8,128)}, f32[8,2048,256]{2,1,0:T(8,128)}, f32[8,256,2048]{2,1,0:T(8,128)}) custom-call(bf16[8,192,2048]{2,1,0:T(8,128)(2,1)} %get-tuple-element.1717.refs_0_, bf16[8,192,2048]{2,1,0:T(8,128)(2,1)} %get-tuple-element.1721.refs_1_, ...), custom_call_target="tpu_custom_call", output_to_operand_aliasing={{0}: (16, {}), {1}: (17, {}), {2}: (18, {})} | custom-call | flops 4831838208 | bytes 27525120 | tf_op jit(solution)/shard_map/pallas_call | solution.py:638
  528.9 11.2 %shard_map.226 = (f32[8,2048,256]{2,1,0:T(8,128)}, f32[8,2048,256]{2,1,0:T(8,128)}, f32[8,256,2048]{2,1,0:T(8,128)}) custom-call(bf16[8,192,2048]{2,1,0:T(8,128)(2,1)} %get-tuple-element.1717.refs_0_, bf16[8,192,2048]{2,1,0:T(8,128)(2,1)} %get-tuple-element.1721.refs_1_, ...), custom_call_target="tpu_custom_call", output_to_operand_aliasing={{0}: (16, {}), {1}: (17, {}), {2}: (18, {})} | custom-call | flops 4831838208 | bytes 27525120 | tf_op jit(solution)/shard_map/pallas_call | solution.py:638
  541.4 22.0 %collective-permute-done.86 = bf16[256,1536]{1,0:T(8,128)(2,1)} collective-permute-done((bf16[256,1536]{1,0:T(8,128)(2,1)}, bf16[256,1536]{1,0:T(8,128)(2,1)}, u32[]{:S(2)}, u32[]{:S(2)}) %collective-permute-start.86) | collective-permute-done | bytes 786464 | tf_op jit(solution)/shard_map/ppermute | solution.py:691
  575.9 11.4 %shard_map.227 = (f32[8,2048,256]{2,1,0:T(8,128)}, f32[8,2048,256]{2,1,0:T(8,128)}, f32[8,256,2048]{2,1,0:T(8,128)}) custom-call(bf16[8,192,2048]{2,1,0:T(8,128)(2,1)} %get-tuple-element.1717.refs_0_, bf16[8,192,2048]{2,1,0:T(8,128)(2,1)} %get-tuple-element.1721.refs_1_, ...), custom_call_target="tpu_custom_call", output_to_operand_aliasing={{0}: (16, {}), {1}: (17, {}), {2}: (18, {})} | custom-call | flops 4831838208 | bytes 27525120 | tf_op jit(solution)/shard_map/pallas_call | solution.py:638
  587.3 15.2 %collective-permute-done.93 = bf16[128,2048]{1,0:T(8,128)(2,1)S(1)} collective-permute-done((bf16[128,2048]{1,0:T(8,128)(2,1)S(1)}, bf16[128,2048]{1,0:T(8,128)(2,1)S(1)}, u32[]{:S(2)}, u32[]{:S(2)}) %collective-permute-start.93) | collective-permute-done | bytes 524320 | tf_op jit(solution)/shard_map/ppermute | solution.py:691
  602.5 6.5 collective-permute-done.90
  623.9 15.9 %collective-permute-done.96 = bf16[128,2048]{1,0:T(8,128)(2,1)S(1)} collective-permute-done((bf16[128,2048]{1,0:T(8,128)(2,1)S(1)}, bf16[128,2048]{1,0:T(8,128)(2,1)S(1)}, u32[]{:S(2)}, u32[]{:S(2)}) %collective-permute-start.96) | collective-permute-done | bytes 524320 | tf_op jit(solution)/shard_map/ppermute | solution.py:691
  665.2 19.1 %collective-permute-done.103 = bf16[1024,1536]{1,0:T(8,128)(2,1)} collective-permute-done((bf16[1024,1536]{1,0:T(8,128)(2,1)}, bf16[1024,1536]{1,0:T(8,128)(2,1)}, u32[]{:S(2)}, u32[]{:S(2)}) %collective-permute-start.103) | collective-permute-done | bytes 3145760 | tf_op jit(solution)/shard_map/ppermute | solution.py:691
  (600 shorter events, 346.0 us)
Async XLA Ops:
  131.5 40.4 %collective-permute-start.24 = (bf16[512,2048]{1,0:T(8,128)(2,1)}, bf16[512,2048]{1,0:T(8,128)(2,1)}, u32[]{:S(2)}, u32[]{:S(2)}) collective-permute-start(bf16[512,2048]{1,0:T(8,128)(2,1)} %pad_maximum_fusion.6), channel_id=1, source_target_pairs={{0,1},{1,0},{2,3},{3,2},{4,5},{5,4},{6,7},{7,6},{8,9},{9,8},{10,11... | collective-permute-start | bytes 6291464 | tf_op jit(solution)/shard_map/ppermute | solution.py:691
  132.6 39.3 %collective-permute-start.25 = (bf16[128,4224]{1,0:T(8,128)(2,1)}, bf16[128,4224]{1,0:T(8,128)(2,1)}, u32[]{:S(2)}, u32[]{:S(2)}) collective-permute-start(bf16[128,4224]{1,0:T(8,128)(2,1)} %pad_maximum_fusion.7.refs_0_), channel_id=1, source_target_pairs={{0,2},{1,5},{2,0},{3,7},{4,6},{5,1},{6,4},{7,3},{8,10},{9,13},{10,... | collective-permute-start | bytes 3244040 | tf_op jit(solution)/shard_map/ppermute | solution.py:691
  133.4 38.4 %collective-permute-start.26 = (bf16[128,4224]{1,0:T(8,128)(2,1)}, bf16[128,4224]{1,0:T(8,128)(2,1)}, u32[]{:S(2)}, u32[]{:S(2)}) collective-permute-start(bf16[128,4224]{1,0:T(8,128)(2,1)} %pad_maximum_fusion.7.refs_0_), channel_id=1, source_target_pairs={{0,4},{1,3},{2,6},{3,1},{4,0},{5,7},{6,2},{7,5},{8,12},{9,11},{10,... | collective-permute-start | bytes 3244040 | tf_op jit(solution)/shard_map/ppermute | solution.py:691
  134.8 37.1 %collective-permute-start.27 = (bf16[128,4224]{1,0:T(8,128)(2,1)}, bf16[128,4224]{1,0:T(8,128)(2,1)}, u32[]{:S(2)}, u32[]{:S(2)}) collective-permute-start(bf16[128,4224]{1,0:T(8,128)(2,1)} %pad_maximum_fusion.7.refs_0_), channel_id=1, source_target_pairs={{0,1},{1,0},{2,3},{3,2},{4,5},{5,4},{6,7},{7,6},{8,9},{9,8},{10,11... | collective-permute-start | bytes 3244040 | tf_op jit(solution)/shard_map/ppermute | solution.py:691
  134.8 37.1 %collective-permute-start.28 = (bf16[128,2048]{1,0:T(8,128)(2,1)S(1)}, bf16[128,2048]{1,0:T(8,128)(2,1)}, u32[]{:S(2)}, u32[]{:S(2)}) collective-permute-start(bf16[128,2048]{1,0:T(8,128)(2,1)S(1)} %multiply_convert_fusion.1.refs_0_), channel_id=1, source_target_pairs={{0,16},{1,17},{2,18},{3,19},{4,20},{5,21},{6,22},{7,23},{8,24},{9,... | collective-permute-start | bytes 1572872 | tf_op jit(solution)/shard_map/ppermute | solution.py:691
  176.9 39.3 %collective-permute-start.30 = (bf16[256,4224]{1,0:T(8,128)(2,1)}, bf16[256,4224]{1,0:T(8,128)(2,1)}, u32[]{:S(2)}, u32[]{:S(2)}) collective-permute-start(bf16[256,4224]{1,0:T(8,128)(2,1)} %pad_maximum_fusion.3), channel_id=1, source_target_pairs={{0,1},{1,0},{2,3},{3,2},{4,5},{5,4},{6,7},{7,6},{8,9},{9,8},{10,11... | collective-permute-start | bytes 6488072 | tf_op jit(solution)/shard_map/ppermute | solution.py:691
  177.1 39.1 %collective-permute-start.33 = (bf16[512,2048]{1,0:T(8,128)(2,1)}, bf16[512,2048]{1,0:T(8,128)(2,1)}, u32[]{:S(2)}, u32[]{:S(2)}) collective-permute-start(bf16[512,2048]{1,0:T(8,128)(2,1)} %get-tuple-element.1078), channel_id=1, source_target_pairs={{0,1},{1,0},{2,3},{3,2},{4,5},{5,4},{6,7},{7,6},{8,9},{9,8},{10,11... | collective-permute-start | bytes 6291464 | tf_op jit(solution)/shard_map/ppermute | solution.py:691
  178.3 32.8 %collective-permute-start.31 = (bf16[128,4224]{1,0:T(8,128)(2,1)}, bf16[128,4224]{1,0:T(8,128)(2,1)}, u32[]{:S(2)}, u32[]{:S(2)}) collective-permute-start(bf16[128,4224]{1,0:T(8,128)(2,1)} %constant_dynamic-update-slice_fusion.refs_0_), channel_id=1, source_target_pairs={{0,2},{1,5},{2,0},{3,7},{4,6},{5,1},{6,4},{7,3},{8,10},{9,13},{10,... | collective-permute-start | bytes 3244040 | tf_op jit(solution)/shard_map/ppermute | solution.py:691
  179.1 32.0 %collective-permute-start.32 = (bf16[128,4224]{1,0:T(8,128)(2,1)}, bf16[128,4224]{1,0:T(8,128)(2,1)}, u32[]{:S(2)}, u32[]{:S(2)}) collective-permute-start(bf16[128,4224]{1,0:T(8,128)(2,1)} %constant_dynamic-update-slice_fusion.refs_0_), channel_id=1, source_target_pairs={{0,4},{1,3},{2,6},{3,1},{4,0},{5,7},{6,2},{7,5},{8,12},{9,11},{10,... | collective-permute-start | bytes 3244040 | tf_op jit(solution)/shard_map/ppermute | solution.py:691
  179.6 36.6 %collective-permute-start.29 = (bf16[128,4224]{1,0:T(8,128)(2,1)}, bf16[128,4224]{1,0:T(8,128)(2,1)}, u32[]{:S(2)}, u32[]{:S(2)}) collective-permute-start(bf16[128,4224]{1,0:T(8,128)(2,1)} %collective-permute-done.25.refs_1_), channel_id=1, source_target_pairs={{0,4},{1,3},{2,6},{3,1},{4,0},{5,7},{6,2},{7,5},{8,12},{9,11},{10,... | collective-permute-start | bytes 3244040 | tf_op jit(solution)/shard_map/ppermute | solution.py:691
  223.0 33.2 %collective-permute-start.35 = (bf16[384,4224]{1,0:T(8,128)(2,1)}, bf16[384,4224]{1,0:T(8,128)(2,1)}, u32[]{:S(2)}, u32[]{:S(2)}) collective-permute-start(bf16[384,4224]{1,0:T(8,128)(2,1)} %pad_maximum_fusion), channel_id=1, source_target_pairs={{0,1},{1,0},{2,3},{3,2},{4,5},{5,4},{6,7},{7,6},{8,9},{9,8},{10,11... | collective-permute-start | bytes 9732104 | tf_op jit(solution)/shard_map/ppermute | solution.py:691
  223.4 32.8 %collective-permute-start.38 = (bf16[512,2048]{1,0:T(8,128)(2,1)}, bf16[512,2048]{1,0:T(8,128)(2,1)}, u32[]{:S(2)}, u32[]{:S(2)}) collective-permute-start(bf16[512,2048]{1,0:T(8,128)(2,1)} %get-tuple-element.1160), channel_id=1, source_target_pairs={{0,1},{1,0},{2,3},{3,2},{4,5},{5,4},{6,7},{7,6},{8,9},{9,8},{10,11... | collective-permute-start | bytes 6291464 | tf_op jit(solution)/shard_map/ppermute | solution.py:691
  223.6 32.7 %collective-permute-start.39 = (bf16[512,2048]{1,0:T(8,128)(2,1)}, bf16[512,2048]{1,0:T(8,128)(2,1)}, u32[]{:S(2)}, u32[]{:S(2)}) collective-permute-start(bf16[512,2048]{1,0:T(8,128)(2,1)} %get-tuple-element.1161), channel_id=1, source_target_pairs={{0,1},{1,0},{2,3},{3,2},{4,5},{5,4},{6,7},{7,6},{8,9},{9,8},{10,11... | collective-permute-start | bytes 6291464 | tf_op jit(solution)/shard_map/ppermute | solution.py:691
  223.9 32.2 %collective-permute-start.37 = (bf16[128,4224]{1,0:T(8,128)(2,1)}, bf16[128,4224]{1,0:T(8,128)(2,1)}, u32[]{:S(2)}, u32[]{:S(2)}) collective-permute-start(bf16[128,4224]{1,0:T(8,128)(2,1)} %collective-permute-done.31.refs_1_), channel_id=1, source_target_pairs={{0,4},{1,3},{2,6},{3,1},{4,0},{5,7},{6,2},{7,5},{8,12},{9,11},{10,... | collective-permute-start | bytes 3244040 | tf_op jit(solution)/shard_map/ppermute | solution.py:691
  262.8 34.7 %collective-permute-start.45 = (bf16[512,2048]{1,0:T(8,128)(2,1)}, bf16[512,2048]{1,0:T(8,128)(2,1)}, u32[]{:S(2)}, u32[]{:S(2)}) collective-permute-start(bf16[512,2048]{1,0:T(8,128)(2,1)} %get-tuple-element.1252), channel_id=1, source_target_pairs={{0,1},{1,0},{2,3},{3,2},{4,5},{5,4},{6,7},{7,6},{8,9},{9,8},{10,11... | collective-permute-start | bytes 6291464 | tf_op jit(solution)/shard_map/ppermute | solution.py:691
  264.6 32.8 %collective-permute-start.44 = (bf16[2,128,2048]{2,1,0:T(8,128)(2,1)}, bf16[2,128,2048]{2,1,0:T(8,128)(2,1)}, u32[]{:S(2)}, u32[]{:S(2)}) collective-permute-start(bf16[2,128,2048]{2,1,0:T(8,128)(2,1)} %bitcast.23), channel_id=1, source_target_pairs={{0,4},{1,3},{2,6},{3,1},{4,0},{5,7},{6,2},{7,5},{8,12},{9,11},{10,... | collective-permute-start | bytes 3145736 | tf_op jit(solution)/shard_map/ppermute | solution.py:691
  265.2 32.3 %collective-permute-start.43 = (bf16[2,128,2048]{2,1,0:T(8,128)(2,1)}, bf16[2,128,2048]{2,1,0:T(8,128)(2,1)}, u32[]{:S(2)}, u32[]{:S(2)}) collective-permute-start(bf16[2,128,2048]{2,1,0:T(8,128)(2,1)} %bitcast.22), channel_id=1, source_target_pairs={{0,4},{1,3},{2,6},{3,1},{4,0},{5,7},{6,2},{7,5},{8,12},{9,11},{10,... | collective-permute-start | bytes 3145736 | tf_op jit(solution)/shard_map/ppermute | solution.py:691
  446.4 37.6 %collective-permute-start.74 = (bf16[1024,1536]{1,0:T(8,128)(2,1)}, bf16[1024,1536]{1,0:T(8,128)(2,1)}, u32[]{:S(2)}, u32[]{:S(2)}) collective-permute-start(bf16[1024,1536]{1,0:T(8,128)(2,1)} %dynamic-slice_convert_fusion), channel_id=1, source_target_pairs={{0,4},{1,9},{2,6},{3,11},{4,0},{5,13},{6,2},{7,15},{8,12},{9,1},{1... | collective-permute-start | bytes 9437192 | tf_op jit(solution)/shard_map/ppermute | solution.py:691
  525.5 37.9 %collective-permute-start.86 = (bf16[256,1536]{1,0:T(8,128)(2,1)}, bf16[256,1536]{1,0:T(8,128)(2,1)}, u32[]{:S(2)}, u32[]{:S(2)}) collective-permute-start(bf16[256,1536]{1,0:T(8,128)(2,1)} %dynamic-slice_convert_fusion.3), channel_id=1, source_target_pairs={{0,16},{1,17},{2,18},{3,19},{4,20},{5,21},{6,22},{7,23},{8,24},{9,... | collective-permute-start | bytes 2359304 | tf_op jit(solution)/shard_map/ppermute | solution.py:691
  525.5 37.9 %collective-permute-start.85 = (bf16[2,128,2048]{2,1,0:T(8,128)(2,1)}, bf16[2,128,2048]{2,1,0:T(8,128)(2,1)}, u32[]{:S(2)}, u32[]{:S(2)}) collective-permute-start(bf16[2,128,2048]{2,1,0:T(8,128)(2,1)} %bitcast.72), channel_id=1, source_target_pairs={{0,4},{1,3},{2,6},{3,1},{4,0},{5,7},{6,2},{7,5},{8,12},{9,11},{10,... | collective-permute-start | bytes 3145736 | tf_op jit(solution)/shard_map/ppermute | solution.py:691
  569.7 39.3 %collective-permute-start.91 = (bf16[256,2048]{1,0:T(8,128)(2,1)S(1)}, bf16[256,2048]{1,0:T(8,128)(2,1)S(1)}, u32[]{:S(2)}, u32[]{:S(2)}) collective-permute-start(bf16[256,2048]{1,0:T(8,128)(2,1)S(1)} %constant_dynamic-update-slice_fusion.28), channel_id=1, source_target_pairs={{0,4},{1,9},{2,6},{3,11},{4,0},{5,13},{6,2},{7,15},{8,12},{9,1},{1... | collective-permute-start | bytes 3145736 | tf_op jit(solution)/shard_map/ppermute | solution.py:691
  570.6 38.4 %collective-permute-start.89 = (bf16[2,128,2048]{2,1,0:T(8,128)(2,1)S(1)}, bf16[2,128,2048]{2,1,0:T(8,128)(2,1)S(1)}, u32[]{:S(2)}, u32[]{:S(2)}) collective-permute-start(bf16[2,128,2048]{2,1,0:T(8,128)(2,1)S(1)} %bitcast.226), channel_id=1, source_target_pairs={{0,4},{1,3},{2,6},{3,1},{4,0},{5,7},{6,2},{7,5},{8,12},{9,11},{10,... | collective-permute-start | bytes 3145736 | tf_op jit(solution)/shard_map/ppermute | solution.py:691
  573.2 35.8 %collective-permute-start.90 = (bf16[256,1536]{1,0:T(8,128)(2,1)S(1)}, bf16[256,1536]{1,0:T(8,128)(2,1)S(1)}, u32[]{:S(2)}, u32[]{:S(2)}) collective-permute-start(bf16[256,1536]{1,0:T(8,128)(2,1)S(1)} %add_convert_fusion.8), channel_id=1, source_target_pairs={{0,16},{1,17},{2,18},{3,19},{4,20},{5,21},{6,22},{7,23},{8,24},{9,... | collective-permute-start | bytes 2359304 | tf_op jit(solution)/shard_map/ppermute | solution.py:691
  646.7 37.6 %collective-permute-start.103 = (bf16[1024,1536]{1,0:T(8,128)(2,1)}, bf16[1024,1536]{1,0:T(8,128)(2,1)}, u32[]{:S(2)}, u32[]{:S(2)}) collective-permute-start(bf16[1024,1536]{1,0:T(8,128)(2,1)} %constant_dynamic-update-slice_fusion.16), channel_id=1, source_target_pairs={{0,4},{1,9},{2,6},{3,11},{4,0},{5,13},{6,2},{7,15},{8,12},{9,1},{1... | collective-permute-start | bytes 9437192 | tf_op jit(solution)/shard_map/ppermute | solution.py:691
  (176 other events, 2438.2 us)

commit v4 on v3

--- a/solution.py
+++ b/solution.py
@@ -785,10 +785,8 @@
     small_hops = tuple((mask, mask) for mask in (CORE, ACROSS, ASIDE, PLANE_NEXT, PLANE_FAR))
 
     def joined(own, got, side):
-        count = own.shape[0]
-        both = jnp.zeros((2 * count,) + own.shape[1:], own.dtype)
-        both = lax.dynamic_update_slice_in_dim(both, own, side * count, 0)
-        return lax.dynamic_update_slice_in_dim(both, got, (1 - side) * count, 0)
+        first, second = jnp.where(side == 0, own, got), jnp.where(side == 0, got, own)
+        return jnp.concatenate([first, second], axis=0)
 
     def sum_step(name, step, hops=weight_hops, sent_as=narrow):
         count = len(hops)
@@ -934,7 +932,9 @@
         rows, grads = [live.pop((name, plane, 0)) for name in (H, G)]
         if isinstance(rows, list):
             rows = jnp.concatenate(rows, axis=0)
-        live[PAIR, plane, 0] = jnp.concatenate([rows, grads], axis=1)
+        after, ahead = grads.shape[1], rows.shape[1]
+        pair = jnp.pad(rows, ((0, 0), (0, after))) + jnp.pad(grads, ((0, 0), (ahead, 0)))
+        live[PAIR, plane, 0] = pair
 
     def experts(plane):
         if (PAIR, plane, 0) in live:
@@ -1083,7 +1083,7 @@
     live[ATTN] = live[ATTN] + [core(live[ATTN][2])]
     sync()
 
-    grad_attn_all = jnp.concatenate(live.pop(ATTN), axis=0)
+    grad_attn_all = jnp.stack(live.pop(ATTN)).reshape(seq_length, model_width)
     live[OUT, FULL] = jnp.einsum(
         "lh,ld->hd", live[HEADS], grad_attn_all, preferred_element_type=wide
     )
@@ -1236,7 +1236,8 @@
     block_len, top_count = expert_ids.shape
     capacity = 3 * block_len * top_count // (2 * w_router.shape[1])
     buffer_rows = capacity * quarters * owners * w_gate.shape[0]
-    gathers = owners * tokens.shape[0] <= buffer_rows and (owners, quarters) == (8, 4)
+    gathers = owners * tokens.shape[0] <= buffer_rows and w_router.shape[1] <= 256
+    gathers = gathers and (owners, quarters) == (8, 4)
     return (gathered_layer if gathers else routed_layer)(*operands)
 
 

time: 703 us -> 697 us (level)
  local copies, waits for them, and re-layouts: 52.1 us -> 37.1 us
  waiting for transfers between devices: 220 us -> 230 us
    ppermute x104, waiting for transfers between devices: 220 us -> 230 us  [swap(): return lax.ppermute(value, BOTH, perm)]
    unnamed x201 -> x180, local copies, waits for them, and re-layouts: 17.2 us -> 13.7 us
  transfers between devices with their start and end apart: 104 -> 104, of which waited for: 35 -> 34; matrix products, arithmetic and copies ran while one was open for 19% -> 19% of each run, Pallas kernels for 24% -> 24%
where the time goes in v4:
time: 697 us; the launch traced here: 687 us
  waiting for transfers between devices  230 us (33%)
  Pallas kernels  166 us (24%)
  other arithmetic  118 us (17%)
  starting transfers between devices  105 us (15%)
  local copies, waits for them, and re-layouts  37.1 us (5%)
  matrix products  28 us (4%)
    ppermute x104, waiting for transfers between devices, swap(): return lax.ppermute(value, BOTH, perm)  230 us
    pallas_call x4, Pallas kernels, expert_chunk(): pl.pallas_call(functools.partial(expert_kernel, places, top_count), in_sp...  120 us
    ppermute x104, starting transfers between devices, swap(): return lax.ppermute(value, BOTH, perm)  105 us
    pallas_call x4, Pallas kernels, weight_grads(): pl.pallas_call(functools.partial(weight_kernel, parts, len(partial)), gri...  45.2 us
    convert_element_type x15, other arithmetic, add(): return (left.astype(wide) + right.astype(wide)).astype(narrow)  26.9 us
    convert_element_type x8, other arithmetic, add_near(): part.astype(narrow)  21 us
  transfers between devices with their start and end apart: 104, of which 34 were waited for; matrix products, arithmetic and copies ran while one was open for 19% of the time, Pallas kernels for 24%

profile of v4, /device:TPU:0, one launch (start us, length us, event | category | flops | bytes accessed | tf_op | source)
XLA Modules:
  0.0 686.9 jit_solution(10110377042630148838)
XLA Ops:
  38.9 9.4 %collective-permute-done.4 = bf16[64,2176]{1,0:T(8,128)(2,1)S(1)} collective-permute-done((bf16[64,2176]{1,0:T(8,128)(2,1)S(1)}, bf16[64,2176]{1,0:T(8,128)(2,1)S(1)}, u32[]{:S(2)}, u32[]{:S(2)}) %collective-permute-start.4) | collective-permute-done | bytes 278560 | tf_op jit(solution)/shard_map/ppermute | solution.py:691
  55.7 5.4 collective-permute-done.9.refs_8_
  64.7 11.5 %collective-permute-done.10 = bf16[128,2048]{1,0:T(8,128)(2,1)S(1)} collective-permute-done((bf16[128,2048]{1,0:T(8,128)(2,1)S(1)}, bf16[128,2048]{1,0:T(8,128)(2,1)S(1)}, u32[]{:S(2)}, u32[]{:S(2)}) %collective-permute-start.10) | collective-permute-done | bytes 524320 | tf_op jit(solution)/shard_map/ppermute | solution.py:691
  82.0 10.0 %collective-permute-done.12.refs_1_ = bf16[128,2048]{1,0:T(8,128)(2,1)S(1)} collective-permute-done((bf16[128,2048]{1,0:T(8,128)(2,1)S(1)}, bf16[128,2048]{1,0:T(8,128)(2,1)S(1)}, u32[]{:S(2)}, u32[]{:S(2)}) %collective-permute-start.12) | collective-permute-done | bytes 524320 | tf_op jit(solution)/shard_map/ppermute | solution.py:691
  100.3 7.1 %collective-permute-done.19 = bf16[64,2048]{1,0:T(8,128)(2,1)S(1)} collective-permute-done((bf16[64,2048]{1,0:T(8,128)(2,1)S(1)}, bf16[64,2048]{1,0:T(8,128)(2,1)S(1)}, u32[]{:S(2)}, u32[]{:S(2)}) %collective-permute-start.19) | collective-permute-done | bytes 262176 | tf_op jit(solution)/shard_map/ppermute | solution.py:691
  121.7 6.3 collective-permute-done.20
  134.9 6.9 %collective-permute-start.28 = (bf16[128,2048]{1,0:T(8,128)(2,1)S(1)}, bf16[128,2048]{1,0:T(8,128)(2,1)}, u32[]{:S(2)}, u32[]{:S(2)}) collective-permute-start(bf16[128,2048]{1,0:T(8,128)(2,1)S(1)} %multiply_convert_fusion.1.refs_0_), channel_id=1, source_target_pairs={{0,16},{1,17},{2,18},{3,19},{4,20},{5,21},{6,22},{7,23},{8,24},{9,... | collective-permute-start | bytes 1572872 | tf_op jit(solution)/shard_map/ppermute | solution.py:691
  141.7 30.2 %shard_map.220 = (bf16[512,2048]{1,0:T(8,128)(2,1)}, bf16[512,2048]{1,0:T(8,128)(2,1)}, bf16[512,2048]{1,0:T(8,128)(2,1)}, bf16[512,2048]{1,0:T(8,128)(2,1)}, f3...) custom-call(bf16[128,2048]{1,0:T(8,128)(2,1)} %copy-done.8, ...), custom_call_target="tpu_custom_call" | custom-call | flops 19327352832 | bytes 37748736 | tf_op jit(solution)/shard_map/pallas_call | solution.py:576
  180.7 30.0 %shard_map.221 = (bf16[512,2048]{1,0:T(8,128)(2,1)}, bf16[512,2048]{1,0:T(8,128)(2,1)}, bf16[512,2048]{1,0:T(8,128)(2,1)}, bf16[512,2048]{1,0:T(8,128)(2,1)}, f3...) custom-call(bf16[128,2048]{1,0:T(8,128)(2,1)} %copy-done.63, ...), custom_call_target="tpu_custom_call" | custom-call | flops 19327352832 | bytes 37748736 | tf_op jit(solution)/shard_map/pallas_call | solution.py:576
  225.5 30.2 %shard_map.222 = (bf16[512,2048]{1,0:T(8,128)(2,1)}, bf16[512,2048]{1,0:T(8,128)(2,1)}, bf16[512,2048]{1,0:T(8,128)(2,1)}, bf16[512,2048]{1,0:T(8,128)(2,1)}, f3...) custom-call(bf16[128,4224]{1,0:T(8,128)(2,1)} %fusion.31.refs_0_, ...), custom_call_target="tpu_custom_call" | custom-call | flops 19327352832 | bytes 37748736 | tf_op jit(solution)/shard_map/pallas_call | solution.py:576
  267.0 30.0 %shard_map.223 = (bf16[512,2048]{1,0:T(8,128)(2,1)}, bf16[512,2048]{1,0:T(8,128)(2,1)}, bf16[512,2048]{1,0:T(8,128)(2,1)}, bf16[512,2048]{1,0:T(8,128)(2,1)}, f3...) custom-call(bf16[128,4224]{1,0:T(8,128)(2,1)} %pad_add_fusion.refs_0, ...), custom_call_target="tpu_custom_call" | custom-call | flops 19327352832 | bytes 37748736 | tf_op jit(solution)/shard_map/pallas_call | solution.py:576
  311.2 11.3 %collective-permute-done.49 = f32[4,2,8,128]{3,2,1,0:T(8,128)S(1)} collective-permute-done((f32[4,2,8,128]{3,2,1,0:T(8,128)S(1)}, f32[4,2,8,128]{3,2,1,0:T(8,128)S(1)}, u32[]{:S(2)}, u32[]{:S(2)}) %collective-permute-start.49) | collective-permute-done | bytes 32800 | tf_op jit(solution)/shard_map/ppermute | solution.py:691
  338.4 5.3 collective-permute-done.53
  357.7 12.5 %collective-permute-done.60 = bf16[128,2048]{1,0:T(8,128)(2,1)} collective-permute-done((bf16[128,2048]{1,0:T(8,128)(2,1)}, bf16[128,2048]{1,0:T(8,128)(2,1)}, u32[]{:S(2)}, u32[]{:S(2)}) %collective-permute-start.60) | collective-permute-done | bytes 524320 | tf_op jit(solution)/shard_map/ppermute | solution.py:691
  452.6 11.4 %shard_map.224 = (f32[8,2048,256]{2,1,0:T(8,128)}, f32[8,2048,256]{2,1,0:T(8,128)}, f32[8,256,2048]{2,1,0:T(8,128)}) custom-call(bf16[8,192,2048]{2,1,0:T(8,128)(2,1)} %get-tuple-element.1717.refs_0_, bf16[8,192,2048]{2,1,0:T(8,128)(2,1)} %get-tuple-element.1721.refs_1_, bf16[8,192,2048]{2,1,0:T(8,128)(2,1)} %get-tuple-element.1730.refs_2_, ...), custom_call_target="tpu_custom_call" | custom-call | flops 4831838208 | bytes 27525120 | tf_op jit(solution)/shard_map/pallas_call | solution.py:638
  467.3 13.3 %collective-permute-done.74 = bf16[1024,1536]{1,0:T(8,128)(2,1)} collective-permute-done((bf16[1024,1536]{1,0:T(8,128)(2,1)}, bf16[1024,1536]{1,0:T(8,128)(2,1)}, u32[]{:S(2)}, u32[]{:S(2)}) %collective-permute-start.74) | collective-permute-done | bytes 3145760 | tf_op jit(solution)/shard_map/ppermute | solution.py:691
  492.0 11.2 %shard_map.225 = (f32[8,2048,256]{2,1,0:T(8,128)}, f32[8,2048,256]{2,1,0:T(8,128)}, f32[8,256,2048]{2,1,0:T(8,128)}) custom-call(bf16[8,192,2048]{2,1,0:T(8,128)(2,1)} %get-tuple-element.1717.refs_0_, bf16[8,192,2048]{2,1,0:T(8,128)(2,1)} %get-tuple-element.1721.refs_1_, ...), custom_call_target="tpu_custom_call", output_to_operand_aliasing={{0}: (16, {}), {1}: (17, {}), {2}: (18, {})} | custom-call | flops 4831838208 | bytes 27525120 | tf_op jit(solution)/shard_map/pallas_call | solution.py:638
  523.1 11.2 %shard_map.226 = (f32[8,2048,256]{2,1,0:T(8,128)}, f32[8,2048,256]{2,1,0:T(8,128)}, f32[8,256,2048]{2,1,0:T(8,128)}) custom-call(bf16[8,192,2048]{2,1,0:T(8,128)(2,1)} %get-tuple-element.1717.refs_0_, bf16[8,192,2048]{2,1,0:T(8,128)(2,1)} %get-tuple-element.1721.refs_1_, ...), custom_call_target="tpu_custom_call", output_to_operand_aliasing={{0}: (16, {}), {1}: (17, {}), {2}: (18, {})} | custom-call | flops 4831838208 | bytes 27525120 | tf_op jit(solution)/shard_map/pallas_call | solution.py:638
  535.7 21.5 %collective-permute-done.86 = bf16[256,1536]{1,0:T(8,128)(2,1)} collective-permute-done((bf16[256,1536]{1,0:T(8,128)(2,1)S(1)}, bf16[256,1536]{1,0:T(8,128)(2,1)}, u32[]{:S(2)}, u32[]{:S(2)}) %collective-permute-start.86) | collective-permute-done | bytes 786464 | tf_op jit(solution)/shard_map/ppermute | solution.py:691
  570.2 11.6 %shard_map.227 = (f32[8,2048,256]{2,1,0:T(8,128)}, f32[8,2048,256]{2,1,0:T(8,128)}, f32[8,256,2048]{2,1,0:T(8,128)}) custom-call(bf16[8,192,2048]{2,1,0:T(8,128)(2,1)} %get-tuple-element.1717.refs_0_, bf16[8,192,2048]{2,1,0:T(8,128)(2,1)} %get-tuple-element.1721.refs_1_, ...), custom_call_target="tpu_custom_call", output_to_operand_aliasing={{0}: (16, {}), {1}: (17, {}), {2}: (18, {})} | custom-call | flops 4831838208 | bytes 27525120 | tf_op jit(solution)/shard_map/pallas_call | solution.py:638
  581.8 13.8 %collective-permute-done.93 = bf16[128,2048]{1,0:T(8,128)(2,1)} collective-permute-done((bf16[128,2048]{1,0:T(8,128)(2,1)}, bf16[128,2048]{1,0:T(8,128)(2,1)}, u32[]{:S(2)}, u32[]{:S(2)}) %collective-permute-start.93) | collective-permute-done | bytes 524320 | tf_op jit(solution)/shard_map/ppermute | solution.py:691
  595.6 6.4 collective-permute-done.90
  616.9 21.3 %collective-permute-done.96 = bf16[128,2048]{1,0:T(8,128)(2,1)S(1)} collective-permute-done((bf16[128,2048]{1,0:T(8,128)(2,1)S(1)}, bf16[128,2048]{1,0:T(8,128)(2,1)S(1)}, u32[]{:S(2)}, u32[]{:S(2)}) %collective-permute-start.96) | collective-permute-done | bytes 524320 | tf_op jit(solution)/shard_map/ppermute | solution.py:691
  656.4 24.5 %collective-permute-done.103 = bf16[1024,1536]{1,0:T(8,128)(2,1)} collective-permute-done((bf16[1024,1536]{1,0:T(8,128)(2,1)}, bf16[1024,1536]{1,0:T(8,128)(2,1)}, u32[]{:S(2)}, u32[]{:S(2)}) %collective-permute-start.103) | collective-permute-done | bytes 3145760 | tf_op jit(solution)/shard_map/ppermute | solution.py:691
  (565 shorter events, 331.6 us)
Async XLA Ops:
  131.6 40.4 %collective-permute-start.24 = (bf16[512,2048]{1,0:T(8,128)(2,1)}, bf16[512,2048]{1,0:T(8,128)(2,1)}, u32[]{:S(2)}, u32[]{:S(2)}) collective-permute-start(bf16[512,2048]{1,0:T(8,128)(2,1)} %pad_maximum_fusion.7), channel_id=1, source_target_pairs={{0,1},{1,0},{2,3},{3,2},{4,5},{5,4},{6,7},{7,6},{8,9},{9,8},{10,11... | collective-permute-start | bytes 6291464 | tf_op jit(solution)/shard_map/ppermute | solution.py:691
  132.7 39.3 %collective-permute-start.25 = (bf16[128,4224]{1,0:T(8,128)(2,1)}, bf16[128,4224]{1,0:T(8,128)(2,1)}, u32[]{:S(2)}, u32[]{:S(2)}) collective-permute-start(bf16[128,4224]{1,0:T(8,128)(2,1)} %fusion.31.refs_0_), channel_id=1, source_target_pairs={{0,2},{1,5},{2,0},{3,7},{4,6},{5,1},{6,4},{7,3},{8,10},{9,13},{10,... | collective-permute-start | bytes 3244040 | tf_op jit(solution)/shard_map/ppermute | solution.py:691
  133.5 38.5 %collective-permute-start.26 = (bf16[128,4224]{1,0:T(8,128)(2,1)}, bf16[128,4224]{1,0:T(8,128)(2,1)}, u32[]{:S(2)}, u32[]{:S(2)}) collective-permute-start(bf16[128,4224]{1,0:T(8,128)(2,1)} %fusion.31.refs_0_), channel_id=1, source_target_pairs={{0,4},{1,3},{2,6},{3,1},{4,0},{5,7},{6,2},{7,5},{8,12},{9,11},{10,... | collective-permute-start | bytes 3244040 | tf_op jit(solution)/shard_map/ppermute | solution.py:691
  134.9 37.1 %collective-permute-start.27 = (bf16[128,4224]{1,0:T(8,128)(2,1)}, bf16[128,4224]{1,0:T(8,128)(2,1)}, u32[]{:S(2)}, u32[]{:S(2)}) collective-permute-start(bf16[128,4224]{1,0:T(8,128)(2,1)} %fusion.31.refs_0_), channel_id=1, source_target_pairs={{0,1},{1,0},{2,3},{3,2},{4,5},{5,4},{6,7},{7,6},{8,9},{9,8},{10,11... | collective-permute-start | bytes 3244040 | tf_op jit(solution)/shard_map/ppermute | solution.py:691
  134.9 37.1 %collective-permute-start.28 = (bf16[128,2048]{1,0:T(8,128)(2,1)S(1)}, bf16[128,2048]{1,0:T(8,128)(2,1)}, u32[]{:S(2)}, u32[]{:S(2)}) collective-permute-start(bf16[128,2048]{1,0:T(8,128)(2,1)S(1)} %multiply_convert_fusion.1.refs_0_), channel_id=1, source_target_pairs={{0,16},{1,17},{2,18},{3,19},{4,20},{5,21},{6,22},{7,23},{8,24},{9,... | collective-permute-start | bytes 1572872 | tf_op jit(solution)/shard_map/ppermute | solution.py:691
  175.1 40.6 %collective-permute-start.30 = (bf16[256,4224]{1,0:T(8,128)(2,1)}, bf16[256,4224]{1,0:T(8,128)(2,1)}, u32[]{:S(2)}, u32[]{:S(2)}) collective-permute-start(bf16[256,4224]{1,0:T(8,128)(2,1)} %pad_maximum_fusion.4), channel_id=1, source_target_pairs={{0,1},{1,0},{2,3},{3,2},{4,5},{5,4},{6,7},{7,6},{8,9},{9,8},{10,11... | collective-permute-start | bytes 6488072 | tf_op jit(solution)/shard_map/ppermute | solution.py:691
  175.4 40.4 %collective-permute-start.33 = (bf16[512,2048]{1,0:T(8,128)(2,1)}, bf16[512,2048]{1,0:T(8,128)(2,1)}, u32[]{:S(2)}, u32[]{:S(2)}) collective-permute-start(bf16[512,2048]{1,0:T(8,128)(2,1)} %get-tuple-element.1078), channel_id=1, source_target_pairs={{0,1},{1,0},{2,3},{3,2},{4,5},{5,4},{6,7},{7,6},{8,9},{9,8},{10,11... | collective-permute-start | bytes 6291464 | tf_op jit(solution)/shard_map/ppermute | solution.py:691
  177.8 32.8 %collective-permute-start.31 = (bf16[128,4224]{1,0:T(8,128)(2,1)}, bf16[128,4224]{1,0:T(8,128)(2,1)}, u32[]{:S(2)}, u32[]{:S(2)}) collective-permute-start(bf16[128,4224]{1,0:T(8,128)(2,1)} %pad_add_fusion.refs_0_), channel_id=1, source_target_pairs={{0,2},{1,5},{2,0},{3,7},{4,6},{5,1},{6,4},{7,3},{8,10},{9,13},{10,... | collective-permute-start | bytes 3244040 | tf_op jit(solution)/shard_map/ppermute | solution.py:691
  179.2 36.6 %collective-permute-start.29 = (bf16[128,4224]{1,0:T(8,128)(2,1)}, bf16[128,4224]{1,0:T(8,128)(2,1)}, u32[]{:S(2)}, u32[]{:S(2)}) collective-permute-start(bf16[128,4224]{1,0:T(8,128)(2,1)} %collective-permute-done.25.refs_1_), channel_id=1, source_target_pairs={{0,4},{1,3},{2,6},{3,1},{4,0},{5,7},{6,2},{7,5},{8,12},{9,11},{10,... | collective-permute-start | bytes 3244040 | tf_op jit(solution)/shard_map/ppermute | solution.py:691
  222.6 33.2 %collective-permute-start.35 = (bf16[384,4224]{1,0:T(8,128)(2,1)}, bf16[384,4224]{1,0:T(8,128)(2,1)}, u32[]{:S(2)}, u32[]{:S(2)}) collective-permute-start(bf16[384,4224]{1,0:T(8,128)(2,1)} %pad_maximum_fusion.1), channel_id=1, source_target_pairs={{0,1},{1,0},{2,3},{3,2},{4,5},{5,4},{6,7},{7,6},{8,9},{9,8},{10,11... | collective-permute-start | bytes 9732104 | tf_op jit(solution)/shard_map/ppermute | solution.py:691
  223.0 32.8 %collective-permute-start.38 = (bf16[512,2048]{1,0:T(8,128)(2,1)}, bf16[512,2048]{1,0:T(8,128)(2,1)}, u32[]{:S(2)}, u32[]{:S(2)}) collective-permute-start(bf16[512,2048]{1,0:T(8,128)(2,1)} %get-tuple-element.1160), channel_id=1, source_target_pairs={{0,1},{1,0},{2,3},{3,2},{4,5},{5,4},{6,7},{7,6},{8,9},{9,8},{10,11... | collective-permute-start | bytes 6291464 | tf_op jit(solution)/shard_map/ppermute | solution.py:691
  223.1 32.7 %collective-permute-start.39 = (bf16[512,2048]{1,0:T(8,128)(2,1)}, bf16[512,2048]{1,0:T(8,128)(2,1)}, u32[]{:S(2)}, u32[]{:S(2)}) collective-permute-start(bf16[512,2048]{1,0:T(8,128)(2,1)} %get-tuple-element.1161), channel_id=1, source_target_pairs={{0,1},{1,0},{2,3},{3,2},{4,5},{5,4},{6,7},{7,6},{8,9},{9,8},{10,11... | collective-permute-start | bytes 6291464 | tf_op jit(solution)/shard_map/ppermute | solution.py:691
  223.5 32.2 %collective-permute-start.37 = (bf16[128,4224]{1,0:T(8,128)(2,1)}, bf16[128,4224]{1,0:T(8,128)(2,1)}, u32[]{:S(2)}, u32[]{:S(2)}) collective-permute-start(bf16[128,4224]{1,0:T(8,128)(2,1)} %collective-permute-done.31.refs_1_), channel_id=1, source_target_pairs={{0,4},{1,3},{2,6},{3,1},{4,0},{5,7},{6,2},{7,5},{8,12},{9,11},{10,... | collective-permute-start | bytes 3244040 | tf_op jit(solution)/shard_map/ppermute | solution.py:691
  262.4 34.7 %collective-permute-start.45 = (bf16[512,2048]{1,0:T(8,128)(2,1)}, bf16[512,2048]{1,0:T(8,128)(2,1)}, u32[]{:S(2)}, u32[]{:S(2)}) collective-permute-start(bf16[512,2048]{1,0:T(8,128)(2,1)} %get-tuple-element.1252), channel_id=1, source_target_pairs={{0,1},{1,0},{2,3},{3,2},{4,5},{5,4},{6,7},{7,6},{8,9},{9,8},{10,11... | collective-permute-start | bytes 6291464 | tf_op jit(solution)/shard_map/ppermute | solution.py:691
  264.2 32.9 %collective-permute-start.44 = (bf16[2,128,2048]{2,1,0:T(8,128)(2,1)}, bf16[2,128,2048]{2,1,0:T(8,128)(2,1)}, u32[]{:S(2)}, u32[]{:S(2)}) collective-permute-start(bf16[2,128,2048]{2,1,0:T(8,128)(2,1)} %bitcast.23), channel_id=1, source_target_pairs={{0,4},{1,3},{2,6},{3,1},{4,0},{5,7},{6,2},{7,5},{8,12},{9,11},{10,... | collective-permute-start | bytes 3145736 | tf_op jit(solution)/shard_map/ppermute | solution.py:691
  264.8 32.3 %collective-permute-start.43 = (bf16[2,128,2048]{2,1,0:T(8,128)(2,1)}, bf16[2,128,2048]{2,1,0:T(8,128)(2,1)}, u32[]{:S(2)}, u32[]{:S(2)}) collective-permute-start(bf16[2,128,2048]{2,1,0:T(8,128)(2,1)} %bitcast.22), channel_id=1, source_target_pairs={{0,4},{1,3},{2,6},{3,1},{4,0},{5,7},{6,2},{7,5},{8,12},{9,11},{10,... | collective-permute-start | bytes 3145736 | tf_op jit(solution)/shard_map/ppermute | solution.py:691
  443.0 37.6 %collective-permute-start.74 = (bf16[1024,1536]{1,0:T(8,128)(2,1)}, bf16[1024,1536]{1,0:T(8,128)(2,1)}, u32[]{:S(2)}, u32[]{:S(2)}) collective-permute-start(bf16[1024,1536]{1,0:T(8,128)(2,1)} %dynamic-slice_convert_fusion), channel_id=1, source_target_pairs={{0,4},{1,9},{2,6},{3,11},{4,0},{5,13},{6,2},{7,15},{8,12},{9,1},{1... | collective-permute-start | bytes 9437192 | tf_op jit(solution)/shard_map/ppermute | solution.py:691
  519.2 38.0 %collective-permute-start.86 = (bf16[256,1536]{1,0:T(8,128)(2,1)S(1)}, bf16[256,1536]{1,0:T(8,128)(2,1)}, u32[]{:S(2)}, u32[]{:S(2)}) collective-permute-start(bf16[256,1536]{1,0:T(8,128)(2,1)S(1)} %dynamic-slice_convert_fusion.3), channel_id=1, source_target_pairs={{0,16},{1,17},{2,18},{3,19},{4,20},{5,21},{6,22},{7,23},{8,24},{9,... | collective-permute-start | bytes 2359304 | tf_op jit(solution)/shard_map/ppermute | solution.py:691
  519.5 37.7 %collective-permute-start.85 = (bf16[2,128,2048]{2,1,0:T(8,128)(2,1)}, bf16[2,128,2048]{2,1,0:T(8,128)(2,1)}, u32[]{:S(2)}, u32[]{:S(2)}) collective-permute-start(bf16[2,128,2048]{2,1,0:T(8,128)(2,1)} %bitcast.77), channel_id=1, source_target_pairs={{0,4},{1,3},{2,6},{3,1},{4,0},{5,7},{6,2},{7,5},{8,12},{9,11},{10,... | collective-permute-start | bytes 3145736 | tf_op jit(solution)/shard_map/ppermute | solution.py:691
  562.7 39.3 %collective-permute-start.91 = (bf16[256,2048]{1,0:T(8,128)(2,1)S(1)}, bf16[256,2048]{1,0:T(8,128)(2,1)}, u32[]{:S(2)}, u32[]{:S(2)}) collective-permute-start(bf16[256,2048]{1,0:T(8,128)(2,1)S(1)} %pad_maximum_fusion.12), channel_id=1, source_target_pairs={{0,4},{1,9},{2,6},{3,11},{4,0},{5,13},{6,2},{7,15},{8,12},{9,1},{1... | collective-permute-start | bytes 3145736 | tf_op jit(solution)/shard_map/ppermute | solution.py:691
  564.1 37.9 %collective-permute-start.89 = (bf16[2,128,2048]{2,1,0:T(8,128)(2,1)}, bf16[2,128,2048]{2,1,0:T(8,128)(2,1)}, u32[]{:S(2)}, u32[]{:S(2)}) collective-permute-start(bf16[2,128,2048]{2,1,0:T(8,128)(2,1)} %bitcast.78), channel_id=1, source_target_pairs={{0,4},{1,3},{2,6},{3,1},{4,0},{5,7},{6,2},{7,5},{8,12},{9,11},{10,... | collective-permute-start | bytes 3145736 | tf_op jit(solution)/shard_map/ppermute | solution.py:691
  566.1 35.9 %collective-permute-start.90 = (bf16[256,1536]{1,0:T(8,128)(2,1)S(1)}, bf16[256,1536]{1,0:T(8,128)(2,1)}, u32[]{:S(2)}, u32[]{:S(2)}) collective-permute-start(bf16[256,1536]{1,0:T(8,128)(2,1)S(1)} %add_convert_fusion.8), channel_id=1, source_target_pairs={{0,16},{1,17},{2,18},{3,19},{4,20},{5,21},{6,22},{7,23},{8,24},{9,... | collective-permute-start | bytes 2359304 | tf_op jit(solution)/shard_map/ppermute | solution.py:691
  607.6 33.6 %collective-permute-start.97 = (bf16[512,1536]{1,0:T(8,128)(2,1)S(1)}, bf16[512,1536]{1,0:T(8,128)(2,1)S(1)}, u32[]{:S(2)}, u32[]{:S(2)}) collective-permute-start(bf16[512,1536]{1,0:T(8,128)(2,1)S(1)} %pad_maximum_fusion.9), channel_id=1, source_target_pairs={{0,8},{1,5},{2,10},{3,7},{4,12},{5,1},{6,14},{7,3},{8,0},{9,13},{1... | collective-permute-start | bytes 4718600 | tf_op jit(solution)/shard_map/ppermute | solution.py:691
  643.3 37.6 %collective-permute-start.103 = (bf16[1024,1536]{1,0:T(8,128)(2,1)}, bf16[1024,1536]{1,0:T(8,128)(2,1)}, u32[]{:S(2)}, u32[]{:S(2)}) collective-permute-start(bf16[1024,1536]{1,0:T(8,128)(2,1)} %pad_maximum_fusion), channel_id=1, source_target_pairs={{0,4},{1,9},{2,6},{3,11},{4,0},{5,13},{6,2},{7,15},{8,12},{9,1},{1... | collective-permute-start | bytes 9437192 | tf_op jit(solution)/shard_map/ppermute | solution.py:691
  (167 other events, 2381.8 us)

commit v5 on v4

--- a/solution.py
+++ b/solution.py
@@ -1043,8 +1043,11 @@
     add_far(M, last)
     sync()
 
-    live[RELAY] = swap(add(reduced(R, far_plane), live[RELAY]), far_plane)
-    live[SIDE] = swap(reduced(R, nxt), nxt)
+    live[RELAY] = add(reduced(R, far_plane), live[RELAY])
+    live[SIDE] = reduced(R, nxt)
+    sync()
+    live[RELAY] = swap(live[RELAY], far_plane)
+    live[SIDE] = swap(live[SIDE], nxt)
     send_far(M, nxt)
     send_far(M, last)
     reduce_core(M, far_plane)
@@ -1071,14 +1074,12 @@
     grad_middle = grad_out + grad_normed_two
     grad_attn = grad_middle.astype(narrow)
 
-    small = jnp.concatenate([live.pop(SMALL), grad_gain_moe[:, None]], axis=1)
-    live[SMALL, FULL] = small.reshape(device_count, -1, small.shape[1])
+    live[SMALL, FULL] = live.pop(SMALL).reshape(device_count, -1, expert_count)
     small_step = functools.partial(sum_step, SMALL, hops=small_hops, sent_as=wide)
 
     live[ATTN] = [grad_attn, core(grad_attn), swap(grad_attn, ACROSS)]
     small_step(0)
     add_near(M, nxt)
-    add_near(M, last)
     sync()
     live[ATTN] = live[ATTN] + [core(live[ATTN][2])]
     sync()
@@ -1145,7 +1146,8 @@
     sum_step(OUT, 2)
     some_weight_grads(0)
     gain = jnp.sum(live.pop(GAIN) * inputs.astype(wide) * inverse_one, axis=0)
-    live[GAIN] = [gain[None], jnp.zeros_like(gain)[None]]
+    gain = jnp.stack([gain, grad_gain_moe])
+    live[GAIN] = [gain, jnp.zeros_like(gain)]
 
     def gain_step(step):
         live[GAIN] = [live[GAIN][0] + live[GAIN][1]]
@@ -1153,6 +1155,7 @@
 
     small_step(3)
     gain_step(0)
+    add_near(M, last)
     add_far(M, far_plane)
     add_far(M, own)
     sync()
@@ -1188,9 +1191,11 @@
     for plane in PLANES:
         live.pop((KEPT, plane))
 
+    live[RELAY] = add(reduced(M, far_plane), live[RELAY])
+    sync()
+    live[RELAY] = swap(live[RELAY], far_plane)
     sum_step(IN, 4)
     live[OUT] = summed(OUT)
-    live[RELAY] = swap(add(reduced(M, far_plane), live[RELAY]), far_plane)
     reduce_near(M, own)
     small_step(8)
     small_step(9)
@@ -1201,8 +1206,7 @@
     sum_step(IN, 5)
     gain_step(3)
     gain_step(4)
-    small = summed(SMALL, small_hops).reshape(model_width, -1)
-    live[SMALL] = [small[:, :expert_count], small[:, expert_count]]
+    live[SMALL] = summed(SMALL, small_hops).reshape(model_width, -1)
     mixed_out = middle + reduced(M, own).astype(wide) + live.pop(MIXED).astype(wide)
     live[MIXED] = (mixed_out + live.pop(RELAY).astype(wide)).astype(narrow)
     even, odd = weight_hops[0]
@@ -1218,14 +1222,15 @@
     sync()
     grads_in = [put(whole, live[IN, GOT], i, 1 - side) for i, whole in enumerate(live[RAW])]
 
+    gains = live[GAIN][0] + live[GAIN][1]
     return (
         live[MIXED],
         live[TOKENS],
-        (live[GAIN][0] + live[GAIN][1])[0],
+        gains[0],
         *grads_in,
         live[OUT],
-        live[SMALL][1],
-        live[SMALL][0],
+        gains[1],
+        live[SMALL],
         *live[EXPERTS],
     )
 

time: 697 us -> 696 us (level)
    unnamed x180 -> x183, local copies, waits for them, and re-layouts: 13.7 us -> 16.4 us
  transfers between devices with their start and end apart: 104 -> 104, of which waited for: 34 -> 36; matrix products, arithmetic and copies ran while one was open for 19% -> 18% of each run, Pallas kernels for 24% -> 24%
where the time goes in v5:
time: 696 us; the launch traced here: 685 us
  waiting for transfers between devices  224 us (32%)
  Pallas kernels  165 us (24%)
  other arithmetic  116 us (17%)
  starting transfers between devices  110 us (16%)
  local copies, waits for them, and re-layouts  40 us (6%)
  matrix products  27.1 us (4%)
    ppermute x104, waiting for transfers between devices, swap(): return lax.ppermute(value, BOTH, perm)  224 us
    pallas_call x4, Pallas kernels, expert_chunk(): pl.pallas_call(functools.partial(expert_kernel, places, top_count), in_sp...  120 us
    ppermute x104, starting transfers between devices, swap(): return lax.ppermute(value, BOTH, perm)  110 us
    pallas_call x4, Pallas kernels, weight_grads(): pl.pallas_call(functools.partial(weight_kernel, parts, len(partial)), gri...  45 us
    convert_element_type x15, other arithmetic, add(): return (left.astype(wide) + right.astype(wide)).astype(narrow)  26.9 us
    convert_element_type x8, other arithmetic, add_near(): part.astype(narrow)  20.4 us
    unnamed x183, local copies, waits for them, and re-layouts  16.4 us
  transfers between devices with their start and end apart: 104, of which 36 were waited for; matrix products, arithmetic and copies ran while one was open for 18% of the time, Pallas kernels for 24%

profile of v5, /device:TPU:0, one launch (start us, length us, event | category | flops | bytes accessed | tf_op | source)
XLA Modules:
  0.0 685.4 jit_solution(11645435495371500658)
XLA Ops:
  38.9 9.4 %collective-permute-done.4 = bf16[64,2176]{1,0:T(8,128)(2,1)S(1)} collective-permute-done((bf16[64,2176]{1,0:T(8,128)(2,1)S(1)}, bf16[64,2176]{1,0:T(8,128)(2,1)S(1)}, u32[]{:S(2)}, u32[]{:S(2)}) %collective-permute-start.4) | collective-permute-done | bytes 278560 | tf_op jit(solution)/shard_map/ppermute | solution.py:691
  56.0 5.4 collective-permute-done.9.refs_8_
  65.0 11.5 %collective-permute-done.10 = bf16[128,2048]{1,0:T(8,128)(2,1)S(1)} collective-permute-done((bf16[128,2048]{1,0:T(8,128)(2,1)S(1)}, bf16[128,2048]{1,0:T(8,128)(2,1)S(1)}, u32[]{:S(2)}, u32[]{:S(2)}) %collective-permute-start.10) | collective-permute-done | bytes 524320 | tf_op jit(solution)/shard_map/ppermute | solution.py:691
  82.2 10.0 %collective-permute-done.12.refs_1_ = bf16[128,2048]{1,0:T(8,128)(2,1)S(1)} collective-permute-done((bf16[128,2048]{1,0:T(8,128)(2,1)S(1)}, bf16[128,2048]{1,0:T(8,128)(2,1)S(1)}, u32[]{:S(2)}, u32[]{:S(2)}) %collective-permute-start.12) | collective-permute-done | bytes 524320 | tf_op jit(solution)/shard_map/ppermute | solution.py:691
  100.5 7.1 %collective-permute-done.19 = bf16[64,2048]{1,0:T(8,128)(2,1)S(1)} collective-permute-done((bf16[64,2048]{1,0:T(8,128)(2,1)S(1)}, bf16[64,2048]{1,0:T(8,128)(2,1)S(1)}, u32[]{:S(2)}, u32[]{:S(2)}) %collective-permute-start.19) | collective-permute-done | bytes 262176 | tf_op jit(solution)/shard_map/ppermute | solution.py:691
  121.9 6.3 collective-permute-done.20
  135.1 6.9 %collective-permute-start.28 = (bf16[128,2048]{1,0:T(8,128)(2,1)S(1)}, bf16[128,2048]{1,0:T(8,128)(2,1)}, u32[]{:S(2)}, u32[]{:S(2)}) collective-permute-start(bf16[128,2048]{1,0:T(8,128)(2,1)S(1)} %multiply_convert_fusion.1.refs_0_), channel_id=1, source_target_pairs={{0,16},{1,17},{2,18},{3,19},{4,20},{5,21},{6,22},{7,23},{8,24},{9,... | collective-permute-start | bytes 1572872 | tf_op jit(solution)/shard_map/ppermute | solution.py:691
  142.0 30.0 %shard_map.220 = (bf16[512,2048]{1,0:T(8,128)(2,1)}, bf16[512,2048]{1,0:T(8,128)(2,1)}, bf16[512,2048]{1,0:T(8,128)(2,1)}, bf16[512,2048]{1,0:T(8,128)(2,1)}, f3...) custom-call(bf16[128,2048]{1,0:T(8,128)(2,1)} %copy-done.8, ...), custom_call_target="tpu_custom_call" | custom-call | flops 19327352832 | bytes 37748736 | tf_op jit(solution)/shard_map/pallas_call | solution.py:576
  180.6 30.0 %shard_map.221 = (bf16[512,2048]{1,0:T(8,128)(2,1)}, bf16[512,2048]{1,0:T(8,128)(2,1)}, bf16[512,2048]{1,0:T(8,128)(2,1)}, bf16[512,2048]{1,0:T(8,128)(2,1)}, f3...) custom-call(bf16[128,2048]{1,0:T(8,128)(2,1)} %copy-done.64, ...), custom_call_target="tpu_custom_call" | custom-call | flops 19327352832 | bytes 37748736 | tf_op jit(solution)/shard_map/pallas_call | solution.py:576
  225.5 30.3 %shard_map.222 = (bf16[512,2048]{1,0:T(8,128)(2,1)}, bf16[512,2048]{1,0:T(8,128)(2,1)}, bf16[512,2048]{1,0:T(8,128)(2,1)}, bf16[512,2048]{1,0:T(8,128)(2,1)}, f3...) custom-call(bf16[128,4224]{1,0:T(8,128)(2,1)} %fusion.31.refs_0_, ...), custom_call_target="tpu_custom_call" | custom-call | flops 19327352832 | bytes 37748736 | tf_op jit(solution)/shard_map/pallas_call | solution.py:576
  267.0 30.0 %shard_map.223 = (bf16[512,2048]{1,0:T(8,128)(2,1)}, bf16[512,2048]{1,0:T(8,128)(2,1)}, bf16[512,2048]{1,0:T(8,128)(2,1)}, bf16[512,2048]{1,0:T(8,128)(2,1)}, f3...) custom-call(bf16[128,4224]{1,0:T(8,128)(2,1)} %pad_add_fusion.refs_0, ...), custom_call_target="tpu_custom_call" | custom-call | flops 19327352832 | bytes 37748736 | tf_op jit(solution)/shard_map/pallas_call | solution.py:576
  311.2 11.3 %collective-permute-done.49 = f32[4,2,8,128]{3,2,1,0:T(8,128)S(1)} collective-permute-done((f32[4,2,8,128]{3,2,1,0:T(8,128)S(1)}, f32[4,2,8,128]{3,2,1,0:T(8,128)S(1)}, u32[]{:S(2)}, u32[]{:S(2)}) %collective-permute-start.49) | collective-permute-done | bytes 32800 | tf_op jit(solution)/shard_map/ppermute | solution.py:691
  358.1 17.3 %collective-permute-done.57 = bf16[128,2048]{1,0:T(8,128)(2,1)} collective-permute-done((bf16[128,2048]{1,0:T(8,128)(2,1)}, bf16[128,2048]{1,0:T(8,128)(2,1)}, u32[]{:S(2)}, u32[]{:S(2)}) %collective-permute-start.57) | collective-permute-done | bytes 524320 | tf_op jit(solution)/shard_map/ppermute | solution.py:691
  387.0 7.4 %collective-permute-done.64 = bf16[128,2048]{1,0:T(8,128)(2,1)} collective-permute-done((bf16[128,2048]{1,0:T(8,128)(2,1)}, bf16[128,2048]{1,0:T(8,128)(2,1)}, u32[]{:S(2)}, u32[]{:S(2)}) %collective-permute-start.64) | collective-permute-done | bytes 524320 | tf_op jit(solution)/shard_map/ppermute | solution.py:691
  456.9 11.3 %shard_map.224 = (f32[8,2048,256]{2,1,0:T(8,128)}, f32[8,2048,256]{2,1,0:T(8,128)}, f32[8,256,2048]{2,1,0:T(8,128)}) custom-call(bf16[8,192,2048]{2,1,0:T(8,128)(2,1)} %get-tuple-element.1823.refs_0_, bf16[8,192,2048]{2,1,0:T(8,128)(2,1)} %get-tuple-element.1827.refs_1_, bf16[8,192,2048]{2,1,0:T(8,128)(2,1)} %get-tuple-element.1836.refs_2_, ...), custom_call_target="tpu_custom_call" | custom-call | flops 4831838208 | bytes 27525120 | tf_op jit(solution)/shard_map/pallas_call | solution.py:638
  471.6 12.6 %collective-permute-done.74 = bf16[1024,1536]{1,0:T(8,128)(2,1)} collective-permute-done((bf16[1024,1536]{1,0:T(8,128)(2,1)}, bf16[1024,1536]{1,0:T(8,128)(2,1)}, u32[]{:S(2)}, u32[]{:S(2)}) %collective-permute-start.74) | collective-permute-done | bytes 3145760 | tf_op jit(solution)/shard_map/ppermute | solution.py:691
  496.7 11.2 %shard_map.225 = (f32[8,2048,256]{2,1,0:T(8,128)}, f32[8,2048,256]{2,1,0:T(8,128)}, f32[8,256,2048]{2,1,0:T(8,128)}) custom-call(bf16[8,192,2048]{2,1,0:T(8,128)(2,1)} %get-tuple-element.1823.refs_0_, bf16[8,192,2048]{2,1,0:T(8,128)(2,1)} %get-tuple-element.1827.refs_1_, ...), custom_call_target="tpu_custom_call", output_to_operand_aliasing={{0}: (16, {}), {1}: (17, {}), {2}: (18, {})} | custom-call | flops 4831838208 | bytes 27525120 | tf_op jit(solution)/shard_map/pallas_call | solution.py:638
  512.9 7.1 %collective-permute-done.79 = bf16[512,1536]{1,0:T(8,128)(2,1)} collective-permute-done((bf16[512,1536]{1,0:T(8,128)(2,1)}, bf16[512,1536]{1,0:T(8,128)(2,1)}, u32[]{:S(2)}, u32[]{:S(2)}) %collective-permute-start.79) | collective-permute-done | bytes 1572896 | tf_op jit(solution)/shard_map/ppermute | solution.py:691
  529.2 11.2 %shard_map.226 = (f32[8,2048,256]{2,1,0:T(8,128)}, f32[8,2048,256]{2,1,0:T(8,128)}, f32[8,256,2048]{2,1,0:T(8,128)}) custom-call(bf16[8,192,2048]{2,1,0:T(8,128)(2,1)} %get-tuple-element.1823.refs_0_, bf16[8,192,2048]{2,1,0:T(8,128)(2,1)} %get-tuple-element.1827.refs_1_, ...), custom_call_target="tpu_custom_call", output_to_operand_aliasing={{0}: (16, {}), {1}: (17, {}), {2}: (18, {})} | custom-call | flops 4831838208 | bytes 27525120 | tf_op jit(solution)/shard_map/pallas_call | solution.py:638
  542.4 16.5 %collective-permute-done.86 = bf16[256,1536]{1,0:T(8,128)(2,1)} collective-permute-done((bf16[256,1536]{1,0:T(8,128)(2,1)}, bf16[256,1536]{1,0:T(8,128)(2,1)}, u32[]{:S(2)}, u32[]{:S(2)}) %collective-permute-start.86) | collective-permute-done | bytes 786464 | tf_op jit(solution)/shard_map/ppermute | solution.py:691
  573.9 11.4 %shard_map.227 = (f32[8,2048,256]{2,1,0:T(8,128)}, f32[8,2048,256]{2,1,0:T(8,128)}, f32[8,256,2048]{2,1,0:T(8,128)}) custom-call(bf16[8,192,2048]{2,1,0:T(8,128)(2,1)} %get-tuple-element.1823.refs_0_, bf16[8,192,2048]{2,1,0:T(8,128)(2,1)} %get-tuple-element.1827.refs_1_, ...), custom_call_target="tpu_custom_call", output_to_operand_aliasing={{0}: (16, {}), {1}: (17, {}), {2}: (18, {})} | custom-call | flops 4831838208 | bytes 27525120 | tf_op jit(solution)/shard_map/pallas_call | solution.py:638
  585.3 12.6 %collective-permute-done.93 = bf16[128,2048]{1,0:T(8,128)(2,1)S(1)} collective-permute-done((bf16[128,2048]{1,0:T(8,128)(2,1)}, bf16[128,2048]{1,0:T(8,128)(2,1)S(1)}, u32[]{:S(2)}, u32[]{:S(2)}) %collective-permute-start.93) | collective-permute-done | bytes 524320 | tf_op jit(solution)/shard_map/ppermute | solution.py:691
  620.0 16.9 %collective-permute-done.96 = bf16[128,2048]{1,0:T(8,128)(2,1)S(1)} collective-permute-done((bf16[128,2048]{1,0:T(8,128)(2,1)S(1)}, bf16[128,2048]{1,0:T(8,128)(2,1)S(1)}, u32[]{:S(2)}, u32[]{:S(2)}) %collective-permute-start.96) | collective-permute-done | bytes 524320 | tf_op jit(solution)/shard_map/ppermute | solution.py:691
  657.9 21.7 %collective-permute-done.103 = bf16[1024,1536]{1,0:T(8,128)(2,1)} collective-permute-done((bf16[1024,1536]{1,0:T(8,128)(2,1)}, bf16[1024,1536]{1,0:T(8,128)(2,1)}, u32[]{:S(2)}, u32[]{:S(2)}) %collective-permute-start.103) | collective-permute-done | bytes 3145760 | tf_op jit(solution)/shard_map/ppermute | solution.py:691
  (568 shorter events, 337.4 us)
Async XLA Ops:
  131.8 40.2 %collective-permute-start.24 = (bf16[512,2048]{1,0:T(8,128)(2,1)}, bf16[512,2048]{1,0:T(8,128)(2,1)}, u32[]{:S(2)}, u32[]{:S(2)}) collective-permute-start(bf16[512,2048]{1,0:T(8,128)(2,1)} %pad_maximum_fusion.7), channel_id=1, source_target_pairs={{0,1},{1,0},{2,3},{3,2},{4,5},{5,4},{6,7},{7,6},{8,9},{9,8},{10,11... | collective-permute-start | bytes 6291464 | tf_op jit(solution)/shard_map/ppermute | solution.py:691
  132.9 39.0 %collective-permute-start.25 = (bf16[128,4224]{1,0:T(8,128)(2,1)}, bf16[128,4224]{1,0:T(8,128)(2,1)}, u32[]{:S(2)}, u32[]{:S(2)}) collective-permute-start(bf16[128,4224]{1,0:T(8,128)(2,1)} %fusion.31.refs_0_), channel_id=1, source_target_pairs={{0,2},{1,5},{2,0},{3,7},{4,6},{5,1},{6,4},{7,3},{8,10},{9,13},{10,... | collective-permute-start | bytes 3244040 | tf_op jit(solution)/shard_map/ppermute | solution.py:691
  133.7 38.2 %collective-permute-start.26 = (bf16[128,4224]{1,0:T(8,128)(2,1)}, bf16[128,4224]{1,0:T(8,128)(2,1)}, u32[]{:S(2)}, u32[]{:S(2)}) collective-permute-start(bf16[128,4224]{1,0:T(8,128)(2,1)} %fusion.31.refs_0_), channel_id=1, source_target_pairs={{0,4},{1,3},{2,6},{3,1},{4,0},{5,7},{6,2},{7,5},{8,12},{9,11},{10,... | collective-permute-start | bytes 3244040 | tf_op jit(solution)/shard_map/ppermute | solution.py:691
  135.1 36.9 %collective-permute-start.27 = (bf16[128,4224]{1,0:T(8,128)(2,1)}, bf16[128,4224]{1,0:T(8,128)(2,1)}, u32[]{:S(2)}, u32[]{:S(2)}) collective-permute-start(bf16[128,4224]{1,0:T(8,128)(2,1)} %fusion.31.refs_0_), channel_id=1, source_target_pairs={{0,1},{1,0},{2,3},{3,2},{4,5},{5,4},{6,7},{7,6},{8,9},{9,8},{10,11... | collective-permute-start | bytes 3244040 | tf_op jit(solution)/shard_map/ppermute | solution.py:691
  135.1 36.9 %collective-permute-start.28 = (bf16[128,2048]{1,0:T(8,128)(2,1)S(1)}, bf16[128,2048]{1,0:T(8,128)(2,1)}, u32[]{:S(2)}, u32[]{:S(2)}) collective-permute-start(bf16[128,2048]{1,0:T(8,128)(2,1)S(1)} %multiply_convert_fusion.1.refs_0_), channel_id=1, source_target_pairs={{0,16},{1,17},{2,18},{3,19},{4,20},{5,21},{6,22},{7,23},{8,24},{9,... | collective-permute-start | bytes 1572872 | tf_op jit(solution)/shard_map/ppermute | solution.py:691
  175.1 40.6 %collective-permute-start.30 = (bf16[256,4224]{1,0:T(8,128)(2,1)}, bf16[256,4224]{1,0:T(8,128)(2,1)}, u32[]{:S(2)}, u32[]{:S(2)}) collective-permute-start(bf16[256,4224]{1,0:T(8,128)(2,1)} %pad_maximum_fusion.4), channel_id=1, source_target_pairs={{0,1},{1,0},{2,3},{3,2},{4,5},{5,4},{6,7},{7,6},{8,9},{9,8},{10,11... | collective-permute-start | bytes 6488072 | tf_op jit(solution)/shard_map/ppermute | solution.py:691
  175.3 40.4 %collective-permute-start.33 = (bf16[512,2048]{1,0:T(8,128)(2,1)}, bf16[512,2048]{1,0:T(8,128)(2,1)}, u32[]{:S(2)}, u32[]{:S(2)}) collective-permute-start(bf16[512,2048]{1,0:T(8,128)(2,1)} %get-tuple-element.1139), channel_id=1, source_target_pairs={{0,1},{1,0},{2,3},{3,2},{4,5},{5,4},{6,7},{7,6},{8,9},{9,8},{10,11... | collective-permute-start | bytes 6291464 | tf_op jit(solution)/shard_map/ppermute | solution.py:691
  177.8 32.9 %collective-permute-start.31 = (bf16[128,4224]{1,0:T(8,128)(2,1)}, bf16[128,4224]{1,0:T(8,128)(2,1)}, u32[]{:S(2)}, u32[]{:S(2)}) collective-permute-start(bf16[128,4224]{1,0:T(8,128)(2,1)} %pad_add_fusion.refs_0_), channel_id=1, source_target_pairs={{0,2},{1,5},{2,0},{3,7},{4,6},{5,1},{6,4},{7,3},{8,10},{9,13},{10,... | collective-permute-start | bytes 3244040 | tf_op jit(solution)/shard_map/ppermute | solution.py:691
  179.1 36.6 %collective-permute-start.29 = (bf16[128,4224]{1,0:T(8,128)(2,1)}, bf16[128,4224]{1,0:T(8,128)(2,1)}, u32[]{:S(2)}, u32[]{:S(2)}) collective-permute-start(bf16[128,4224]{1,0:T(8,128)(2,1)} %collective-permute-done.25.refs_1_), channel_id=1, source_target_pairs={{0,4},{1,3},{2,6},{3,1},{4,0},{5,7},{6,2},{7,5},{8,12},{9,11},{10,... | collective-permute-start | bytes 3244040 | tf_op jit(solution)/shard_map/ppermute | solution.py:691
  222.5 33.2 %collective-permute-start.35 = (bf16[384,4224]{1,0:T(8,128)(2,1)}, bf16[384,4224]{1,0:T(8,128)(2,1)}, u32[]{:S(2)}, u32[]{:S(2)}) collective-permute-start(bf16[384,4224]{1,0:T(8,128)(2,1)} %pad_maximum_fusion.1), channel_id=1, source_target_pairs={{0,1},{1,0},{2,3},{3,2},{4,5},{5,4},{6,7},{7,6},{8,9},{9,8},{10,11... | collective-permute-start | bytes 9732104 | tf_op jit(solution)/shard_map/ppermute | solution.py:691
  222.9 32.8 %collective-permute-start.38 = (bf16[512,2048]{1,0:T(8,128)(2,1)}, bf16[512,2048]{1,0:T(8,128)(2,1)}, u32[]{:S(2)}, u32[]{:S(2)}) collective-permute-start(bf16[512,2048]{1,0:T(8,128)(2,1)} %get-tuple-element.1221), channel_id=1, source_target_pairs={{0,1},{1,0},{2,3},{3,2},{4,5},{5,4},{6,7},{7,6},{8,9},{9,8},{10,11... | collective-permute-start | bytes 6291464 | tf_op jit(solution)/shard_map/ppermute | solution.py:691
  223.0 32.7 %collective-permute-start.39 = (bf16[512,2048]{1,0:T(8,128)(2,1)}, bf16[512,2048]{1,0:T(8,128)(2,1)}, u32[]{:S(2)}, u32[]{:S(2)}) collective-permute-start(bf16[512,2048]{1,0:T(8,128)(2,1)} %get-tuple-element.1222), channel_id=1, source_target_pairs={{0,1},{1,0},{2,3},{3,2},{4,5},{5,4},{6,7},{7,6},{8,9},{9,8},{10,11... | collective-permute-start | bytes 6291464 | tf_op jit(solution)/shard_map/ppermute | solution.py:691
  223.4 32.3 %collective-permute-start.37 = (bf16[128,4224]{1,0:T(8,128)(2,1)}, bf16[128,4224]{1,0:T(8,128)(2,1)}, u32[]{:S(2)}, u32[]{:S(2)}) collective-permute-start(bf16[128,4224]{1,0:T(8,128)(2,1)} %collective-permute-done.31.refs_1_), channel_id=1, source_target_pairs={{0,4},{1,3},{2,6},{3,1},{4,0},{5,7},{6,2},{7,5},{8,12},{9,11},{10,... | collective-permute-start | bytes 3244040 | tf_op jit(solution)/shard_map/ppermute | solution.py:691
  262.4 34.7 %collective-permute-start.45 = (bf16[512,2048]{1,0:T(8,128)(2,1)}, bf16[512,2048]{1,0:T(8,128)(2,1)}, u32[]{:S(2)}, u32[]{:S(2)}) collective-permute-start(bf16[512,2048]{1,0:T(8,128)(2,1)} %get-tuple-element.1313), channel_id=1, source_target_pairs={{0,1},{1,0},{2,3},{3,2},{4,5},{5,4},{6,7},{7,6},{8,9},{9,8},{10,11... | collective-permute-start | bytes 6291464 | tf_op jit(solution)/shard_map/ppermute | solution.py:691
  264.2 32.8 %collective-permute-start.44 = (bf16[2,128,2048]{2,1,0:T(8,128)(2,1)}, bf16[2,128,2048]{2,1,0:T(8,128)(2,1)}, u32[]{:S(2)}, u32[]{:S(2)}) collective-permute-start(bf16[2,128,2048]{2,1,0:T(8,128)(2,1)} %bitcast.23), channel_id=1, source_target_pairs={{0,4},{1,3},{2,6},{3,1},{4,0},{5,7},{6,2},{7,5},{8,12},{9,11},{10,... | collective-permute-start | bytes 3145736 | tf_op jit(solution)/shard_map/ppermute | solution.py:691
  264.8 32.3 %collective-permute-start.43 = (bf16[2,128,2048]{2,1,0:T(8,128)(2,1)}, bf16[2,128,2048]{2,1,0:T(8,128)(2,1)}, u32[]{:S(2)}, u32[]{:S(2)}) collective-permute-start(bf16[2,128,2048]{2,1,0:T(8,128)(2,1)} %bitcast.22), channel_id=1, source_target_pairs={{0,4},{1,3},{2,6},{3,1},{4,0},{5,7},{6,2},{7,5},{8,12},{9,11},{10,... | collective-permute-start | bytes 3145736 | tf_op jit(solution)/shard_map/ppermute | solution.py:691
  446.6 37.6 %collective-permute-start.74 = (bf16[1024,1536]{1,0:T(8,128)(2,1)}, bf16[1024,1536]{1,0:T(8,128)(2,1)}, u32[]{:S(2)}, u32[]{:S(2)}) collective-permute-start(bf16[1024,1536]{1,0:T(8,128)(2,1)} %dynamic-slice_convert_fusion), channel_id=1, source_target_pairs={{0,4},{1,9},{2,6},{3,11},{4,0},{5,13},{6,2},{7,15},{8,12},{9,1},{1... | collective-permute-start | bytes 9437192 | tf_op jit(solution)/shard_map/ppermute | solution.py:691
  525.6 33.2 %collective-permute-start.86 = (bf16[256,1536]{1,0:T(8,128)(2,1)}, bf16[256,1536]{1,0:T(8,128)(2,1)}, u32[]{:S(2)}, u32[]{:S(2)}) collective-permute-start(bf16[256,1536]{1,0:T(8,128)(2,1)} %dynamic-slice_convert_fusion.3), channel_id=1, source_target_pairs={{0,16},{1,17},{2,18},{3,19},{4,20},{5,21},{6,22},{7,23},{8,24},{9,... | collective-permute-start | bytes 2359304 | tf_op jit(solution)/shard_map/ppermute | solution.py:691
  525.6 33.2 %collective-permute-start.85 = (bf16[2,128,2048]{2,1,0:T(8,128)(2,1)}, bf16[2,128,2048]{2,1,0:T(8,128)(2,1)}, u32[]{:S(2)}, u32[]{:S(2)}) collective-permute-start(bf16[2,128,2048]{2,1,0:T(8,128)(2,1)} %bitcast.77), channel_id=1, source_target_pairs={{0,4},{1,3},{2,6},{3,1},{4,0},{5,7},{6,2},{7,5},{8,12},{9,11},{10,... | collective-permute-start | bytes 3145736 | tf_op jit(solution)/shard_map/ppermute | solution.py:691
  565.0 38.1 %collective-permute-start.91 = (bf16[256,2048]{1,0:T(8,128)(2,1)S(1)}, bf16[256,2048]{1,0:T(8,128)(2,1)}, u32[]{:S(2)}, u32[]{:S(2)}) collective-permute-start(bf16[256,2048]{1,0:T(8,128)(2,1)S(1)} %pad_maximum_fusion.12), channel_id=1, source_target_pairs={{0,4},{1,9},{2,6},{3,11},{4,0},{5,13},{6,2},{7,15},{8,12},{9,1},{1... | collective-permute-start | bytes 3145736 | tf_op jit(solution)/shard_map/ppermute | solution.py:691
  566.2 36.9 %collective-permute-start.89 = (bf16[2,128,2048]{2,1,0:T(8,128)(2,1)}, bf16[2,128,2048]{2,1,0:T(8,128)(2,1)}, u32[]{:S(2)}, u32[]{:S(2)}) collective-permute-start(bf16[2,128,2048]{2,1,0:T(8,128)(2,1)} %bitcast.78), channel_id=1, source_target_pairs={{0,4},{1,3},{2,6},{3,1},{4,0},{5,7},{6,2},{7,5},{8,12},{9,11},{10,... | collective-permute-start | bytes 3145736 | tf_op jit(solution)/shard_map/ppermute | solution.py:691
  568.5 34.6 %collective-permute-start.90 = (bf16[256,1536]{1,0:T(8,128)(2,1)S(1)}, bf16[256,1536]{1,0:T(8,128)(2,1)}, u32[]{:S(2)}, u32[]{:S(2)}) collective-permute-start(bf16[256,1536]{1,0:T(8,128)(2,1)S(1)} %add_convert_fusion.8), channel_id=1, source_target_pairs={{0,16},{1,17},{2,18},{3,19},{4,20},{5,21},{6,22},{7,23},{8,24},{9,... | collective-permute-start | bytes 2359304 | tf_op jit(solution)/shard_map/ppermute | solution.py:691
  607.2 32.6 %collective-permute-start.97 = (bf16[512,1536]{1,0:T(8,128)(2,1)S(1)}, bf16[512,1536]{1,0:T(8,128)(2,1)S(1)}, u32[]{:S(2)}, u32[]{:S(2)}) collective-permute-start(bf16[512,1536]{1,0:T(8,128)(2,1)S(1)} %pad_maximum_fusion.9), channel_id=1, source_target_pairs={{0,8},{1,5},{2,10},{3,7},{4,12},{5,1},{6,14},{7,3},{8,0},{9,13},{1... | collective-permute-start | bytes 4718600 | tf_op jit(solution)/shard_map/ppermute | solution.py:691
  641.9 37.6 %collective-permute-start.103 = (bf16[1024,1536]{1,0:T(8,128)(2,1)}, bf16[1024,1536]{1,0:T(8,128)(2,1)}, u32[]{:S(2)}, u32[]{:S(2)}) collective-permute-start(bf16[1024,1536]{1,0:T(8,128)(2,1)} %pad_maximum_fusion), channel_id=1, source_target_pairs={{0,4},{1,9},{2,6},{3,11},{4,0},{5,13},{6,2},{7,15},{8,12},{9,1},{1... | collective-permute-start | bytes 9437192 | tf_op jit(solution)/shard_map/ppermute | solution.py:691
  (169 other events, 2385.5 us)
